TPU v7x, 512 devices: a whole 4x4x16 slice. The times are simulated.
512 devices in a mesh: dom: 128 (over y, z, core), slab: 4 (over x).
Axes of the slice: x: 4, y: 4, z: 16, core: 2. Of those that a mesh axis runs over, the one named last changes fastest.
Arguments:
- node_feats: bfloat16 [131072, 512], P(('dom', 'slab')), may hold values from -6 to 6
- weight: bfloat16 [512, 512], replicated, may hold values from -0.25 to 0.25
- cotangent: bfloat16 [131072, 512], P(('dom', 'slab')), may hold values from -96 to 96
- degrees: int32 [131072], P(('dom', 'slab')), may hold values from 8 to 48
- local_weights: int32 [131072, 2, 128], P(('dom', 'slab')), may hold values from 0 to 3, as said below
- local_tiles: int32 [1024, 2], P(('dom', 'slab')), may hold values from 0 to 1
- send_rows: int32 [65536, 8], P(('dom', 'slab')), may hold values from 0 to 255
- send_count: int32 [65536], P(('dom', 'slab')), may hold values from 1 to 8, as said below
- recv_target: int32 [524288, 2], P(('dom', 'slab')), may hold values from 0 to 255
- recv_weight: int32 [524288, 2], P(('dom', 'slab')), may hold values from 1 to 3
Outputs:
- output: bfloat16 [131072, 512], P(('dom', 'slab'))
- grad_feats: bfloat16 [131072, 512], P(('dom', 'slab'))
- grad_weight: float32 [512, 512], replicated
Inputs may be any that keep to these rules, and one draw needn't show every extreme that they name: Entry 0 of send_count is 8 and every entry is between 1 and 8; the live slots of a peer are the leading ones. `local_weights`: most entries are zero.
All inputs are finite; a program needn't handle non-finite values.
Results may differ from a plain program's by a relative error of at most 0.0062.
Values may be sent and summed in bfloat16 or wider, within the bound.
No kernel may reach another device: no remote copies, remote signals or barrier semaphores. Data moves between devices by JAX's collectives and lax.ppermute only.
A program may use at most 64 MiB of HBM per device.

v0:
```python
import math

import jax
import jax.numpy as jnp
from jax import lax
from jax.sharding import PartitionSpec as P


def shards(
    node_feats,
    weight,
    cotangent,
    degrees,
    local_weights,
    local_tiles,
    send_rows,
    send_count,
    recv_target,
    recv_weight,
):
    row_count, feat_width = node_feats.shape
    tile_size = local_weights.shape[2]
    tile_count = row_count // tile_size
    listed = local_tiles.shape[1]
    peer_count = lax.axis_size("dom")
    slot_cap = send_rows.shape[1]
    slot_count = peer_count * slot_cap
    nodes_all = row_count * peer_count * lax.axis_size("slab")
    column_ids = jnp.arange(tile_count, dtype=jnp.int32)
    selector = (local_tiles[:, :, None] == column_ids[None, None, :]).astype(jnp.bfloat16)
    blocks = local_weights.reshape(tile_count, tile_size, listed, tile_size).astype(jnp.bfloat16)
    adjacency = jnp.einsum("ikj,iakb->iajb", selector, blocks, preferred_element_type=jnp.float32)
    adjacency = adjacency.reshape(row_count, row_count).astype(jnp.bfloat16)
    live_slot = jnp.arange(slot_cap, dtype=jnp.int32)[None, :] < send_count[:, None]
    flat_rows = send_rows.reshape(-1)
    outgoing = jnp.take(node_feats, flat_rows, axis=0).reshape(peer_count, slot_cap, feat_width)
    outgoing = jnp.where(live_slot[:, :, None], outgoing, jnp.zeros((), jnp.bfloat16))
    incoming = lax.all_to_all(outgoing, "dom", split_axis=0, concat_axis=0, tiled=True).reshape(
        slot_count, feat_width
    )
    local_sum = jnp.dot(
        adjacency, node_feats, preferred_element_type=jnp.float32
    ) + node_feats.astype(jnp.float32)
    row_ids = jnp.arange(row_count, dtype=jnp.int32)
    mixing = jnp.sum(
        jnp.where(row_ids[:, None, None] == recv_target[None, :, :], recv_weight[None, :, :], 0),
        axis=2,
    )
    mixing = mixing.astype(jnp.bfloat16)
    remote = jnp.dot(mixing, incoming, preferred_element_type=jnp.float32)
    inv_degree = 1.0 / degrees.astype(jnp.float32)
    aggregated = ((local_sum + remote) * inv_degree[:, None]).astype(jnp.bfloat16)
    pre_act = jnp.dot(aggregated, weight, preferred_element_type=jnp.float32)
    gating_value = jax.nn.sigmoid(pre_act)
    output = (pre_act * gating_value).astype(jnp.bfloat16)
    grad_pre = (
        cotangent.astype(jnp.float32) * gating_value * (1.0 + pre_act * (1.0 - gating_value))
    ).astype(jnp.bfloat16)
    weight_part = lax.dot_general(
        aggregated, grad_pre, (((0,), (0,)), ((), ())), preferred_element_type=jnp.float32
    )
    grad_weight = lax.psum(weight_part, ("dom", "slab"))
    grad_weight = grad_weight * (1.0 / math.sqrt(nodes_all))
    grad_sum = lax.dot_general(
        grad_pre, weight, (((1,), (1,)), ((), ())), preferred_element_type=jnp.float32
    )
    grad_sum = (grad_sum * inv_degree[:, None]).astype(jnp.bfloat16)
    slot_grad = lax.dot_general(
        mixing, grad_sum, (((0,), (0,)), ((), ())), preferred_element_type=jnp.float32
    )
    slot_grad = slot_grad.astype(jnp.bfloat16).reshape(peer_count, slot_cap, feat_width)
    returned = lax.all_to_all(slot_grad, "dom", split_axis=0, concat_axis=0, tiled=True)
    returned = jnp.where(live_slot[:, :, None], returned, jnp.zeros((), jnp.bfloat16)).reshape(
        slot_count, feat_width
    )
    local_back = lax.dot_general(
        adjacency, grad_sum, (((0,), (0,)), ((), ())), preferred_element_type=jnp.float32
    )
    local_back = local_back + grad_sum.astype(jnp.float32)
    owner_map = (row_ids[:, None] == flat_rows[None, :]).astype(jnp.bfloat16)
    remote_back = jnp.dot(owner_map, returned, preferred_element_type=jnp.float32)
    grad_feats = (local_back + remote_back).astype(jnp.bfloat16)
    return (output, grad_feats, grad_weight)


def solution(mesh):
    in_specs = (
        P(("dom", "slab"), None),
        P(),
        P(("dom", "slab"), None),
        P(("dom", "slab")),
        P(("dom", "slab"), None, None),
        P(("dom", "slab"), None),
        P(("dom", "slab"), None),
        P(("dom", "slab")),
        P(("dom", "slab"), None),
        P(("dom", "slab"), None),
    )
    out_specs = (P(("dom", "slab"), None), P(("dom", "slab"), None), P())
    return jax.shard_map(shards, mesh=mesh, in_specs=in_specs, out_specs=out_specs, check_vma=False)
```

profile of v0, /device:TPU:1, one launch (start us, length us, event | category | flops | bytes accessed | tf_op | source)
XLA Modules:
  0.0 594.7 jit_solution(5296511989657909261)
XLA Ops:
  7.2 0.8 compare_and_fusion
  7.9 0.8 copy.22
  8.7 0.1 copy.21
  8.8 0.7 iota_compare_fusion.3
  9.6 0.1 reshape.90
  9.7 5.0 gather_fusion
  14.7 1.2 fusion.7
  15.9 20.7 %all-to-all-start = ((bf16[128,8,512]{2,1,0:T(8,128)(2,1)}), bf16[128,8,512]{2,1,0:T(8,128)(2,1)S(1)}, u32[]{:S(2)}, u32[]{:S(2)}) async-start(bf16[128,8,512]{2,1,0:T(8,128)(2,1)} %fusion.7), calls=%async_computation | async-start | bytes 2097152 | tf_op jit(solution)/shard_map/all_to_all | solution.py:38
  36.8 0.4 select_reduce_fusion
  37.4 0.3 convolution_convert_fusion.1
  37.7 0.2 convolution_add_fusion.3
  37.9 0.4 copy-done.2
  38.3 52.7 %all-to-all-done = bf16[128,8,512]{2,1,0:T(8,128)(2,1)S(1)} async-done(((bf16[128,8,512]{2,1,0:T(8,128)(2,1)}), bf16[128,8,512]{2,1,0:T(8,128)(2,1)S(1)}, u32[]{:S(2)}, u32[]{:S(2)}) %all-to-all-start) | async-done | bytes 1048608 | tf_op jit(solution)/shard_map/all_to_all | solution.py:38
  91.0 0.4 fusion.4
  91.5 0.5 copy-done.8
  91.9 1.2 multiply_convert_fusion
  93.1 0.3 fusion.3
  93.5 1.5 fusion
  94.9 8.5 %all-to-all-start.1 = ((bf16[128,8,512]{2,1,0:T(8,128)(2,1)}), bf16[128,8,512]{2,1,0:T(8,128)(2,1)S(1)}, u32[]{:S(2)}, u32[]{:S(2)}) async-start(bf16[128,8,512]{2,1,0:T(8,128)(2,1)} %fusion), calls=%async_computation.1 | async-start | bytes 2097152 | tf_op jit(solution)/shard_map/all_to_all | solution.py:72
  103.5 1.3 fusion.21
  104.9 0.2 convolution_add_fusion.2
  105.2 479.1 %all-reduce.2.cloned.1.call-done = f32[512,512]{1,0:T(8,128)} async-done(((f32[512,512]{1,0:T(8,128)}), f32[512,512]{1,0:T(8,128)}) %all-reduce.2.cloned.1.call-update) | async-done | bytes 1048592 | tf_op jit(solution)/shard_map/psum | solution.py:62
  584.3 2.3 broadcast_multiply_fusion
  586.6 1.2 fusion.2
  (26 shorter events, 0.4 us)
Async XLA Ops:
  7.2 84.3 %copy-start = (bf16[512,512]{1,0:T(8,128)(2,1)S(1)}, bf16[512,512]{1,0:T(8,128)(2,1)}, u32[]{:S(2)}) copy-start(bf16[512,512]{1,0:T(8,128)(2,1)} %param.11) | copy-start | bytes 1572868
  15.9 20.7 %copy-start.4 = (s32[256,2,128]{2,1,0:T(2,128)S(1)}, s32[256,2,128]{2,1,0:T(2,128)}, u32[]{:S(2)}) copy-start(s32[256,2,128]{2,1,0:T(2,128)} %param.14) | copy-start | bytes 786436
  15.9 20.9 %copy-start.5 = (s32[1024,2]{0,1:T(2,128)S(1)}, s32[1024,2]{0,1:T(2,128)}, u32[]{:S(2)}) copy-start(s32[1024,2]{0,1:T(2,128)} %param.19) | copy-start | bytes 24580
  15.9 20.9 %copy-start.6 = (s32[1024,2]{0,1:T(2,128)S(1)}, s32[1024,2]{0,1:T(2,128)}, u32[]{:S(2)}) copy-start(s32[1024,2]{0,1:T(2,128)} %param.18) | copy-start | bytes 24580
  15.9 75.1 %all-to-all-start = ((bf16[128,8,512]{2,1,0:T(8,128)(2,1)}), bf16[128,8,512]{2,1,0:T(8,128)(2,1)S(1)}, u32[]{:S(2)}, u32[]{:S(2)}) async-start(bf16[128,8,512]{2,1,0:T(8,128)(2,1)} %fusion.7), calls=%async_computation | async-start | bytes 2097152 | tf_op jit(solution)/shard_map/all_to_all | solution.py:38
  36.7 0.7 copy-start.7
  36.7 0.7 copy-start.9
  36.7 1.0 copy-start.1
  37.6 0.7 copy-start.2
  91.0 1.0 copy-start.8
  94.9 491.7 %all-to-all-start.1 = ((bf16[128,8,512]{2,1,0:T(8,128)(2,1)}), bf16[128,8,512]{2,1,0:T(8,128)(2,1)S(1)}, u32[]{:S(2)}, u32[]{:S(2)}) async-start(bf16[128,8,512]{2,1,0:T(8,128)(2,1)} %fusion), calls=%async_computation.1 | async-start | bytes 2097152 | tf_op jit(solution)/shard_map/all_to_all | solution.py:72
  103.4 1.5 copy-start.3
  103.4 480.9 %all-reduce.2.cloned.1.call-start = ((), (), s32[]{:S(2)}) async-start(), calls=%async_computation.2 | async-start | bytes 2097152 | tf_op jit(solution)/shard_map/psum | solution.py:62
Sparse Core Ops, SparseCore 0:
  110.3 473.9 all-reduce.1
where the time goes:
time: 595 us
  waiting for transfers between devices  532 us (89%)
  starting transfers between devices  29.2 us (5%)
  between operations  14.2 us (2%)
  local copies, waits for them, and re-layouts  7.12 us (1%)
  matrix products  6.7 us (1%)
    psum x1, waiting for transfers between devices, shards(): grad_weight = lax.psum(weight_part, ('dom', 'slab'))  479 us
    all_to_all x1, waiting for transfers between devices, shards(): lax.all_to_all(outgoing, 'dom', split_axis=0, concat_axis=0, tiled=True)  52.7 us
    all_to_all x1, starting transfers between devices, shards(): lax.all_to_all(outgoing, 'dom', split_axis=0, concat_axis=0, tiled=True)  20.7 us
  transfers between devices with their start and end apart: 3, of which 2 were waited for; matrix products, arithmetic and copies ran while one was open for 1% of the time, Pallas kernels for 0%

commit v1 on v0

--- a/solution.py
+++ b/solution.py
@@ -3,7 +3,29 @@
 import jax
 import jax.numpy as jnp
 from jax import lax
+from jax.sharding import Mesh
 from jax.sharding import PartitionSpec as P
+
+
+DOM = ("y", "z", "core")
+PLANE = ("y", "core", "slab")
+
+
+def reduce_everywhere(part, scale):
+    rows, width = part.shape
+    plane, depth = lax.axis_size(PLANE), lax.axis_size("z")
+    pieces = part.astype(jnp.bfloat16).reshape(plane, rows // plane, width)
+    pieces = lax.all_to_all(pieces, PLANE, split_axis=0, concat_axis=0, tiled=True)
+    mine = jnp.sum(pieces.astype(jnp.float32), axis=0)
+    mine = mine.reshape(depth, rows // plane // depth, width)
+    mine = lax.all_to_all(mine, "z", split_axis=0, concat_axis=0, tiled=True)
+    mine = jnp.sum(mine, axis=0, keepdims=True) * scale
+    mine = jnp.broadcast_to(mine, (depth,) + mine.shape[1:])
+    mine = lax.all_to_all(mine, "z", split_axis=0, concat_axis=0, tiled=True)
+    mine = mine.reshape(1, rows // plane, width).astype(jnp.bfloat16)
+    mine = jnp.broadcast_to(mine, (plane,) + mine.shape[1:])
+    whole = lax.all_to_all(mine, PLANE, split_axis=0, concat_axis=0, tiled=True)
+    return whole.reshape(rows, width).astype(jnp.float32)
 
 
 def shards(
@@ -22,10 +44,10 @@
     tile_size = local_weights.shape[2]
     tile_count = row_count // tile_size
     listed = local_tiles.shape[1]
-    peer_count = lax.axis_size("dom")
+    peer_count = lax.axis_size(DOM)
     slot_cap = send_rows.shape[1]
     slot_count = peer_count * slot_cap
-    nodes_all = row_count * peer_count * lax.axis_size("slab")
+    nodes_all = row_count * lax.axis_size(DOM + ("slab",))
     column_ids = jnp.arange(tile_count, dtype=jnp.int32)
     selector = (local_tiles[:, :, None] == column_ids[None, None, :]).astype(jnp.bfloat16)
     blocks = local_weights.reshape(tile_count, tile_size, listed, tile_size).astype(jnp.bfloat16)
@@ -35,7 +57,7 @@
     flat_rows = send_rows.reshape(-1)
     outgoing = jnp.take(node_feats, flat_rows, axis=0).reshape(peer_count, slot_cap, feat_width)
     outgoing = jnp.where(live_slot[:, :, None], outgoing, jnp.zeros((), jnp.bfloat16))
-    incoming = lax.all_to_all(outgoing, "dom", split_axis=0, concat_axis=0, tiled=True).reshape(
+    incoming = lax.all_to_all(outgoing, DOM, split_axis=0, concat_axis=0, tiled=True).reshape(
         slot_count, feat_width
     )
     local_sum = jnp.dot(
@@ -59,8 +81,7 @@
     weight_part = lax.dot_general(
         aggregated, grad_pre, (((0,), (0,)), ((), ())), preferred_element_type=jnp.float32
     )
-    grad_weight = lax.psum(weight_part, ("dom", "slab"))
-    grad_weight = grad_weight * (1.0 / math.sqrt(nodes_all))
+    grad_weight = reduce_everywhere(weight_part, 1.0 / math.sqrt(nodes_all))
     grad_sum = lax.dot_general(
         grad_pre, weight, (((1,), (1,)), ((), ())), preferred_element_type=jnp.float32
     )
@@ -69,7 +90,7 @@
         mixing, grad_sum, (((0,), (0,)), ((), ())), preferred_element_type=jnp.float32
     )
     slot_grad = slot_grad.astype(jnp.bfloat16).reshape(peer_count, slot_cap, feat_width)
-    returned = lax.all_to_all(slot_grad, "dom", split_axis=0, concat_axis=0, tiled=True)
+    returned = lax.all_to_all(slot_grad, DOM, split_axis=0, concat_axis=0, tiled=True)
     returned = jnp.where(live_slot[:, :, None], returned, jnp.zeros((), jnp.bfloat16)).reshape(
         slot_count, feat_width
     )
@@ -84,17 +105,12 @@
 
 
 def solution(mesh):
-    in_specs = (
-        P(("dom", "slab"), None),
-        P(),
-        P(("dom", "slab"), None),
-        P(("dom", "slab")),
-        P(("dom", "slab"), None, None),
-        P(("dom", "slab"), None),
-        P(("dom", "slab"), None),
-        P(("dom", "slab")),
-        P(("dom", "slab"), None),
-        P(("dom", "slab"), None),
+    slab_count = mesh.shape["slab"]
+    depth = mesh.shape["dom"] // (2 * slab_count)
+    split = Mesh(
+        mesh.devices.reshape(slab_count, depth, 2, slab_count), ("y", "z", "core", "slab")
     )
-    out_specs = (P(("dom", "slab"), None), P(("dom", "slab"), None), P())
-    return jax.shard_map(shards, mesh=mesh, in_specs=in_specs, out_specs=out_specs, check_vma=False)
+    nodes = P(DOM + ("slab",))
+    in_specs = (nodes, P(), nodes, nodes, nodes, nodes, nodes, nodes, nodes, nodes)
+    out_specs = (nodes, nodes, P())
+    return jax.shard_map(shards, mesh=split, in_specs=in_specs, out_specs=out_specs, check_vma=False)

time: 595 us -> 218 us (0.37)
  waiting for transfers between devices: 532 us -> 116 us
  blocking collectives: 0 us -> 48.3 us
  between operations: 14.2 us -> 0.85 us
    psum x1 -> x0, waiting for transfers between devices: 479 us -> none  [shards(): grad_weight = lax.psum(weight_part, ('dom', 'slab'))]
    all_to_all x2 -> x3, waiting for transfers between devices: 52.7 us -> 116 us  [the longest x1 53.1 us: shards(): lax.all_to_all(outgoing, DOM, split_axis=0, concat_axis=0, tiled=True)]
    all_to_all x0 -> x3, blocking collectives: none -> 48.3 us  [the longest x2 27.9 us: reduce_everywhere(): mine = lax.all_to_all(mine, 'z', split_axis=0, concat_axis=0, tiled=True)]
    all_to_all x2 -> x3, starting transfers between devices: 29.2 us -> 33 us  [the longest x1 20.7 us: shards(): lax.all_to_all(outgoing, DOM, split_axis=0, concat_axis=0, tiled=True)]
  transfers between devices with their start and end apart: 3 -> 3, of which waited for: 2 -> 3; matrix products, arithmetic and copies ran while one was open for 1% -> 2% of each run, Pallas kernels for 0% -> 0%
where the time goes in v1:
time: 218 us; the launch traced here: 217 us
  waiting for transfers between devices  116 us (53%)
  blocking collectives  48.3 us (22%)
  starting transfers between devices  33 us (15%)
  local copies, waits for them, and re-layouts  8.16 us (4%)
  matrix products  5.71 us (3%)
  other arithmetic  5.27 us (2%)
    all_to_all x1, waiting for transfers between devices, shards(): lax.all_to_all(outgoing, DOM, split_axis=0, concat_axis=0, tiled=True)  53.1 us
    all_to_all x1, waiting for transfers between devices, shards(): lax.all_to_all(slot_grad, DOM, split_axis=0, concat_axis=0, tiled=True)  53 us
    all_to_all x2, blocking collectives, reduce_everywhere(): mine = lax.all_to_all(mine, 'z', split_axis=0, concat_axis=0, tiled=True)  27.9 us
    all_to_all x1, starting transfers between devices, shards(): lax.all_to_all(outgoing, DOM, split_axis=0, concat_axis=0, tiled=True)  20.7 us
    all_to_all x1, blocking collectives, reduce_everywhere(): lax.all_to_all(pieces, PLANE, split_axis=0, concat_axis=0, tiled=True)  20.4 us
    all_to_all x1, waiting for transfers between devices, reduce_everywhere(): whole = lax.all_to_all(mine, PLANE, split_axis=0, concat_axis=0, tiled=True)  9.6 us
    all_to_all x1, starting transfers between devices, reduce_everywhere(): whole = lax.all_to_all(mine, PLANE, split_axis=0, concat_axis=0, tiled=True)  6.55 us
    all_to_all x1, starting transfers between devices, shards(): lax.all_to_all(slot_grad, DOM, split_axis=0, concat_axis=0, tiled=True)  5.75 us
  transfers between devices with their start and end apart: 3, of which 3 were waited for; matrix products, arithmetic and copies ran while one was open for 2% of the time, Pallas kernels for 0%

profile of v1, /device:TPU:1, one launch (start us, length us, event | category | flops | bytes accessed | tf_op | source)
XLA Modules:
  0.0 217.0 jit_solution(9845034824244176021)
XLA Ops:
  0.6 0.8 compare_and_fusion
  1.4 0.8 copy.33
  2.3 0.7 iota_compare_fusion.3
  3.2 5.0 %gather_fusion = bf16[1024,512]{1,0:T(8,128)(2,1)S(1)} fusion(bf16[256,512]{1,0:T(8,128)(2,1)} %param.10, s32[1024]{0:T(1024)S(1)} %broadcast_clamp_fusion), kind=kCustom, calls=%fused_computation | custom fusion | bytes 2101248 | tf_op jit(solution)/shard_map/jit(_take)/gather | solution.py:58
  8.2 1.2 fusion.7
  9.4 20.7 %all-to-all-start = ((bf16[128,8,512]{2,1,0:T(8,128)(2,1)}), bf16[128,8,512]{2,1,0:T(8,128)(2,1)S(1)}, u32[]{:S(2)}, u32[]{:S(2)}) async-start(bf16[128,8,512]{2,1,0:T(8,128)(2,1)} %fusion.7), calls=%async_computation | async-start | bytes 2097152 | tf_op jit(solution)/shard_map/all_to_all | solution.py:60
  30.3 0.4 select_reduce_fusion
  31.4 53.1 %all-to-all-done = bf16[128,8,512]{2,1,0:T(8,128)(2,1)S(1)} async-done(((bf16[128,8,512]{2,1,0:T(8,128)(2,1)}), bf16[128,8,512]{2,1,0:T(8,128)(2,1)S(1)}, u32[]{:S(2)}, u32[]{:S(2)}) %all-to-all-start) | async-done | bytes 1048608 | tf_op jit(solution)/shard_map/all_to_all | solution.py:60
  84.5 0.4 fusion.4
  84.9 0.5 copy-done.6
  85.4 1.2 multiply_convert_fusion
  86.9 20.4 %all_to_all.30 = bf16[32,16,512]{2,1,0:T(8,128)(2,1)S(1)} all-to-all(bf16[32,16,512]{2,1,0:T(8,128)(2,1)S(1)} %bitcast.44), channel_id=1, replica_groups=mesh['y'=4,'z'=16,'core'=2,'slab'=4] {'y','core','slab'}, dimensions={0} | all-to-all | bytes 1048576 | tf_op jit(solution)/shard_map/all_to_all | solution.py:18
  107.4 14.1 %all_to_all.31 = f32[16,1,512]{2,1,0:T(1,128)S(1)} all-to-all(f32[16,1,512]{2,1,0:T(1,128)S(1)} %reshape.123), channel_id=1, replica_groups=mesh['y'=4,'z'=16,'core'=2,'slab'=4] {'z'}, dimensions={0} | all-to-all | bytes 65536 | tf_op jit(solution)/shard_map/all_to_all | solution.py:21
  121.6 0.5 broadcast.65
  122.1 0.7 reduce.1
  122.9 13.8 %all_to_all.32 = bf16[16,2,256]{2,1,0:T(2,128)(2,1)S(1)} all-to-all(bf16[16,2,256]{2,1,0:T(2,128)(2,1)S(1)} %reshape.134), channel_id=1, replica_groups=mesh['y'=4,'z'=16,'core'=2,'slab'=4] {'z'}, dimensions={0} | all-to-all | bytes 32768 | tf_op jit(solution)/shard_map/all_to_all | solution.py:24
  136.7 0.9 broadcast_in_dim.68
  137.6 6.5 %all-to-all-start.5 = ((bf16[32,16,512]{2,1,0:T(8,128)(2,1)}), bf16[32,16,512]{2,1,0:T(8,128)(2,1)S(1)}, u32[]{:S(2)}, u32[]{:S(2)}) async-start(bf16[32,16,512]{2,1,0:T(8,128)(2,1)} %broadcast_in_dim.68), calls=%async_computation.5 | async-start | bytes 1048576 | tf_op jit(solution)/shard_map/all_to_all | solution.py:27
  144.5 1.4 fusion
  145.9 9.6 %all-to-all-done.5 = bf16[32,16,512]{2,1,0:T(8,128)(2,1)S(1)} async-done(((bf16[32,16,512]{2,1,0:T(8,128)(2,1)}), bf16[32,16,512]{2,1,0:T(8,128)(2,1)S(1)}, u32[]{:S(2)}, u32[]{:S(2)}) %all-to-all-start.5) | async-done | bytes 524320 | tf_op jit(solution)/shard_map/all_to_all | solution.py:27
  155.5 5.7 %all-to-all-start.1 = ((bf16[128,8,512]{2,1,0:T(8,128)(2,1)}), bf16[128,8,512]{2,1,0:T(8,128)(2,1)S(1)}, u32[]{:S(2)}, u32[]{:S(2)}) async-start(bf16[128,8,512]{2,1,0:T(8,128)(2,1)} %fusion), calls=%async_computation.1 | async-start | bytes 2097152 | tf_op jit(solution)/shard_map/all_to_all | solution.py:93
  161.6 1.1 bitcast_convert_fusion
  162.7 53.0 %all-to-all-done.1 = bf16[128,8,512]{2,1,0:T(8,128)(2,1)S(1)} async-done(((bf16[128,8,512]{2,1,0:T(8,128)(2,1)}), bf16[128,8,512]{2,1,0:T(8,128)(2,1)S(1)}, u32[]{:S(2)}, u32[]{:S(2)}) %all-to-all-start.1) | async-done | bytes 1048608 | tf_op jit(solution)/shard_map/all_to_all | solution.py:93
  215.7 1.2 fusion.2
  (35 shorter events, 2.2 us)
Async XLA Ops:
  0.6 84.3 %copy-start = (bf16[512,512]{1,0:T(8,128)(2,1)S(1)}, bf16[512,512]{1,0:T(8,128)(2,1)}, u32[]{:S(2)}) copy-start(bf16[512,512]{1,0:T(8,128)(2,1)} %param.11) | copy-start | bytes 1572868
  9.4 20.7 %copy-start.2 = (s32[256,2,128]{2,1,0:T(2,128)S(1)}, s32[256,2,128]{2,1,0:T(2,128)}, u32[]{:S(2)}) copy-start(s32[256,2,128]{2,1,0:T(2,128)} %param.14) | copy-start | bytes 786436
  9.4 20.9 %copy-start.3 = (s32[1024,2]{0,1:T(2,128)S(1)}, s32[1024,2]{0,1:T(2,128)}, u32[]{:S(2)}) copy-start(s32[1024,2]{0,1:T(2,128)} %param.19) | copy-start | bytes 24580
  9.4 20.9 %copy-start.4 = (s32[1024,2]{0,1:T(2,128)S(1)}, s32[1024,2]{0,1:T(2,128)}, u32[]{:S(2)}) copy-start(s32[1024,2]{0,1:T(2,128)} %param.18) | copy-start | bytes 24580
  9.4 75.1 %all-to-all-start = ((bf16[128,8,512]{2,1,0:T(8,128)(2,1)}), bf16[128,8,512]{2,1,0:T(8,128)(2,1)S(1)}, u32[]{:S(2)}, u32[]{:S(2)}) async-start(bf16[128,8,512]{2,1,0:T(8,128)(2,1)} %fusion.7), calls=%async_computation | async-start | bytes 2097152 | tf_op jit(solution)/shard_map/all_to_all | solution.py:60
  30.1 0.7 copy-start.5
  30.1 0.7 copy-start.7
  30.1 1.0 copy-start.1
  84.5 1.0 copy-start.6
  137.6 17.9 %all-to-all-start.5 = ((bf16[32,16,512]{2,1,0:T(8,128)(2,1)}), bf16[32,16,512]{2,1,0:T(8,128)(2,1)S(1)}, u32[]{:S(2)}, u32[]{:S(2)}) async-start(bf16[32,16,512]{2,1,0:T(8,128)(2,1)} %broadcast_in_dim.68), calls=%async_computation.5 | async-start | bytes 1048576 | tf_op jit(solution)/shard_map/all_to_all | solution.py:27
  155.5 60.2 %all-to-all-start.1 = ((bf16[128,8,512]{2,1,0:T(8,128)(2,1)}), bf16[128,8,512]{2,1,0:T(8,128)(2,1)S(1)}, u32[]{:S(2)}, u32[]{:S(2)}) async-start(bf16[128,8,512]{2,1,0:T(8,128)(2,1)} %fusion), calls=%async_computation.1 | async-start | bytes 2097152 | tf_op jit(solution)/shard_map/all_to_all | solution.py:93

commit v2 on v1

v2 whole, which is shorter than its diff:
```python
import math

import jax
import jax.numpy as jnp
from jax import lax
from jax.sharding import Mesh
from jax.sharding import PartitionSpec as P


DOM = ("y", "z", "core")


def from_peer(value, axis, mask):
    count = lax.axis_size(axis)
    return lax.ppermute(value, axis, [(place, place ^ mask) for place in range(count)])


def scatter_sum(part, axis):
    count, here = lax.axis_size(axis), lax.axis_index(axis)
    rows = part.shape[0] // count
    total = lax.dynamic_slice_in_dim(part, here * rows, rows)
    for mask in range(1, count):
        block = lax.dynamic_slice_in_dim(part, (here ^ mask) * rows, rows)
        total = total + from_peer(block.astype(jnp.bfloat16), axis, mask).astype(jnp.float32)
    return total


def quad_sum(value, axis, stride):
    near = value + from_peer(value, axis, stride)
    far = from_peer(value, axis, 2 * stride) + from_peer(value, axis, 3 * stride)
    return near + far


def gather(block, axis):
    count, here = lax.axis_size(axis), lax.axis_index(axis)
    rows, width = block.shape
    whole = jnp.zeros((count * rows, width), block.dtype)
    whole = lax.dynamic_update_slice_in_dim(whole, block, here * rows, 0)
    for mask in range(1, count):
        other = from_peer(block, axis, mask)
        whole = lax.dynamic_update_slice_in_dim(whole, other, (here ^ mask) * rows, 0)
    return whole


PLANE = ("core", "slab", "y")


def sum_blocks(part, scale):
    mine = scatter_sum(scatter_sum(scatter_sum(part, "core"), "slab"), "y")
    return (quad_sum(quad_sum(mine, "z", 4), "z", 1) * scale).astype(jnp.bfloat16)


def gather_plane(mine):
    plane = lax.axis_size(PLANE)
    mine = jnp.broadcast_to(mine[None], (plane,) + mine.shape)
    whole = lax.all_to_all(mine, PLANE, split_axis=0, concat_axis=0, tiled=True)
    return whole.reshape(-1, mine.shape[-1]).astype(jnp.float32)


def shards(
    node_feats,
    weight,
    cotangent,
    degrees,
    local_weights,
    local_tiles,
    send_rows,
    send_count,
    recv_target,
    recv_weight,
):
    row_count, feat_width = node_feats.shape
    tile_size = local_weights.shape[2]
    tile_count = row_count // tile_size
    listed = local_tiles.shape[1]
    peer_count = lax.axis_size(DOM)
    slot_cap = send_rows.shape[1]
    slot_count = peer_count * slot_cap
    nodes_all = row_count * lax.axis_size(DOM + ("slab",))
    column_ids = jnp.arange(tile_count, dtype=jnp.int32)
    selector = (local_tiles[:, :, None] == column_ids[None, None, :]).astype(jnp.bfloat16)
    blocks = local_weights.reshape(tile_count, tile_size, listed, tile_size).astype(jnp.bfloat16)
    adjacency = jnp.einsum("ikj,iakb->iajb", selector, blocks, preferred_element_type=jnp.float32)
    adjacency = adjacency.reshape(row_count, row_count).astype(jnp.bfloat16)
    live_slot = jnp.arange(slot_cap, dtype=jnp.int32)[None, :] < send_count[:, None]
    row_ids = jnp.arange(row_count, dtype=jnp.int32)
    slot_ids = jnp.arange(slot_count, dtype=jnp.int32)
    live_rows = jnp.where(live_slot, send_rows, row_count).astype(jnp.bfloat16)
    to_slot = jnp.arange(peer_count, dtype=jnp.int32)[:, None] == slot_ids[None, :] // slot_cap
    spread = lax.dot_general(
        live_rows,
        to_slot.astype(jnp.bfloat16),
        (((0,), (0,)), ((), ())),
        preferred_element_type=jnp.float32,
    )
    own_column = jnp.arange(slot_cap, dtype=jnp.int32)[:, None] == slot_ids[None, :] % slot_cap
    flat_rows = jnp.sum(jnp.where(own_column, spread, 0.0), axis=0)
    owner = (row_ids[:, None] == flat_rows.astype(jnp.int32)[None, :]).astype(jnp.bfloat16)
    outgoing = lax.dot_general(
        owner, node_feats, (((0,), (0,)), ((), ())), preferred_element_type=jnp.float32
    )
    outgoing = outgoing.astype(jnp.bfloat16).reshape(peer_count, slot_cap, feat_width)
    incoming = lax.all_to_all(outgoing, DOM, split_axis=0, concat_axis=0, tiled=True).reshape(
        slot_count, feat_width
    )
    local_sum = jnp.dot(
        adjacency, node_feats, preferred_element_type=jnp.float32
    ) + node_feats.astype(jnp.float32)
    mixing = jnp.sum(
        jnp.where(row_ids[:, None, None] == recv_target[None, :, :], recv_weight[None, :, :], 0),
        axis=2,
    )
    mixing = mixing.astype(jnp.bfloat16)
    remote = jnp.dot(mixing, incoming, preferred_element_type=jnp.float32)
    inv_degree = 1.0 / degrees.astype(jnp.float32)
    aggregated = ((local_sum + remote) * inv_degree[:, None]).astype(jnp.bfloat16)
    pre_act = jnp.dot(aggregated, weight, preferred_element_type=jnp.float32)
    gating_value = jax.nn.sigmoid(pre_act)
    output = (pre_act * gating_value).astype(jnp.bfloat16)
    grad_pre = (
        cotangent.astype(jnp.float32) * gating_value * (1.0 + pre_act * (1.0 - gating_value))
    ).astype(jnp.bfloat16)
    grad_sum = lax.dot_general(
        grad_pre, weight, (((1,), (1,)), ((), ())), preferred_element_type=jnp.float32
    )
    grad_sum = (grad_sum * inv_degree[:, None]).astype(jnp.bfloat16)
    slot_grad = lax.dot_general(
        mixing, grad_sum, (((0,), (0,)), ((), ())), preferred_element_type=jnp.float32
    )
    slot_grad = slot_grad.astype(jnp.bfloat16).reshape(peer_count, slot_cap, feat_width)
    slot_grad, aggregated = lax.optimization_barrier((slot_grad, aggregated))
    returned = lax.all_to_all(slot_grad, DOM, split_axis=0, concat_axis=0, tiled=True)
    returned = returned.reshape(slot_count, feat_width)
    weight_part = lax.dot_general(
        aggregated, grad_pre, (((0,), (0,)), ((), ())), preferred_element_type=jnp.float32
    )
    mine = sum_blocks(weight_part, 1.0 / math.sqrt(nodes_all))
    returned, mine = lax.optimization_barrier((returned, mine))
    grad_weight = gather_plane(mine)
    local_back = lax.dot_general(
        adjacency, grad_sum, (((0,), (0,)), ((), ())), preferred_element_type=jnp.float32
    )
    local_back = local_back + grad_sum.astype(jnp.float32)
    remote_back = jnp.dot(owner, returned, preferred_element_type=jnp.float32)
    grad_feats = (local_back + remote_back).astype(jnp.bfloat16)
    return (output, grad_feats, grad_weight)


def solution(mesh):
    slab_count = mesh.shape["slab"]
    depth = mesh.shape["dom"] // (2 * slab_count)
    split = Mesh(
        mesh.devices.reshape(slab_count, depth, 2, slab_count), ("y", "z", "core", "slab")
    )
    nodes = P(DOM + ("slab",))
    in_specs = (nodes, P(), nodes, nodes, nodes, nodes, nodes, nodes, nodes, nodes)
    out_specs = (nodes, nodes, P())
    return jax.shard_map(shards, mesh=split, in_specs=in_specs, out_specs=out_specs, check_vma=False)
```

time: 218 us -> 187 us (0.86)
  starting transfers between devices: 33 us -> 87.5 us
  blocking collectives: 48.3 us -> 0 us
  waiting for transfers between devices: 116 us -> 83.9 us
  local copies, waits for them, and re-layouts: 8.16 us -> 1.59 us
  matrix products: 5.71 us -> 9.01 us
  other arithmetic: 5.27 us -> 2.76 us
    all_to_all x1, waiting for transfers between devices: 53 us -> 0.01 us  [shards(): lax.all_to_all(slot_grad, DOM, split_axis=0, concat_axis=0, tiled=True)]
    all_to_all x3 -> x0, blocking collectives: 48.3 us -> none  [the longest x2 27.9 us: reduce_everywhere(): mine = lax.all_to_all(mine, 'z', split_axis=0, concat_axis=0, tiled=True)]
    ppermute x0 -> x13, starting transfers between devices: none -> 47.4 us  [from_peer(): lax.ppermute(value, axis, [(place, place ^ mask) for place in range(count)])]
    ppermute x0 -> x13, waiting for transfers between devices: none -> 21 us  [from_peer(): lax.ppermute(value, axis, [(place, place ^ mask) for place in range(count)])]
    gather x1 -> x0, local copies, waits for them, and re-layouts: 4.98 us -> none  [shards(): jnp.take(node_feats, flat_rows, axis=0)]
    all_to_all x1, starting transfers between devices: 6.55 us -> 10.8 us  [gather_plane(): whole = lax.all_to_all(mine, PLANE, split_axis=0, concat_axis=0, tiled=True)]
    dot_general x1 -> x3, matrix products: 1.23 us -> 4.52 us  [the longest x1 2.41 us: shards(): lax.dot_general(owner, node_feats, (((0,), (0,)), ((), ())), preferred_el...]
    all_to_all x1, starting transfers between devices: 5.75 us -> 8.61 us  [shards(): lax.all_to_all(slot_grad, DOM, split_axis=0, concat_axis=0, tiled=True)]
  transfers between devices with their start and end apart: 3 -> 16, of which waited for: 3 -> 10; matrix products, arithmetic and copies ran while one was open for 2% -> 2% of each run, Pallas kernels for 0% -> 0%
where the time goes in v2:
time: 187 us; the launch traced here: 186 us
  starting transfers between devices  87.5 us (47%)
  waiting for transfers between devices  83.9 us (45%)
  matrix products  9.01 us (5%)
  other arithmetic  2.76 us (1%)
    all_to_all x1, waiting for transfers between devices, shards(): lax.all_to_all(outgoing, DOM, split_axis=0, concat_axis=0, tiled=True)  53.1 us
    ppermute x13, starting transfers between devices, from_peer(): lax.ppermute(value, axis, [(place, place ^ mask) for place in range(count)])  47.4 us
    ppermute x13, waiting for transfers between devices, from_peer(): lax.ppermute(value, axis, [(place, place ^ mask) for place in range(count)])  21 us
    all_to_all x1, starting transfers between devices, shards(): lax.all_to_all(outgoing, DOM, split_axis=0, concat_axis=0, tiled=True)  20.7 us
    all_to_all x1, starting transfers between devices, gather_plane(): whole = lax.all_to_all(mine, PLANE, split_axis=0, concat_axis=0, tiled=True)  10.8 us
    all_to_all x1, waiting for transfers between devices, gather_plane(): whole = lax.all_to_all(mine, PLANE, split_axis=0, concat_axis=0, tiled=True)  9.77 us
    all_to_all x1, starting transfers between devices, shards(): lax.all_to_all(slot_grad, DOM, split_axis=0, concat_axis=0, tiled=True)  8.61 us
  transfers between devices with their start and end apart: 16, of which 10 were waited for; matrix products, arithmetic and copies ran while one was open for 2% of the time, Pallas kernels for 0%

profile of v2, /device:TPU:1, one launch (start us, length us, event | category | flops | bytes accessed | tf_op | source)
XLA Modules:
  0.0 185.8 jit_solution(11501461839619710624)
XLA Ops:
  1.6 2.4 %fusion = bf16[128,8,512]{2,1,0:T(8,128)(2,1)} fusion(bf16[256,512]{1,0:T(8,128)(2,1)} %param.10, s32[1024]{0:T(1024)S(1)} %convert_element_type.123), kind=kOutput, calls=%fused_computation.4 | convolution fusion | flops 269221888 | bytes 1314816 | tf_op jit(solution)/shard_map/dot_general | solution.py:99
  4.0 20.7 %all-to-all-start = ((bf16[128,8,512]{2,1,0:T(8,128)(2,1)}), bf16[128,8,512]{2,1,0:T(8,128)(2,1)S(1)}, u32[]{:S(2)}, u32[]{:S(2)}) async-start(bf16[128,8,512]{2,1,0:T(8,128)(2,1)} %fusion), calls=%async_computation | async-start | bytes 2097152 | tf_op jit(solution)/shard_map/all_to_all | solution.py:103
  26.0 53.1 %all-to-all-done = bf16[128,8,512]{2,1,0:T(8,128)(2,1)S(1)} async-done(((bf16[128,8,512]{2,1,0:T(8,128)(2,1)}), bf16[128,8,512]{2,1,0:T(8,128)(2,1)S(1)}, u32[]{:S(2)}, u32[]{:S(2)}) %all-to-all-start) | async-done | bytes 1048608 | tf_op jit(solution)/shard_map/all_to_all | solution.py:103
  81.6 1.4 fusion.1
  83.0 8.6 %all-to-all-start.1 = ((bf16[128,8,512]{2,1,0:T(8,128)(2,1)}), bf16[128,8,512]{2,1,0:T(8,128)(2,1)S(1)}, u32[]{:S(2)}, u32[]{:S(2)}) async-start(bf16[128,8,512]{2,1,0:T(8,128)(2,1)} %fusion.1), calls=%async_computation.1 | async-start | bytes 2097152 | tf_op jit(solution)/shard_map/all_to_all | solution.py:132
  92.0 2.8 %collective-permute-start = (bf16[256,512]{1,0:T(8,128)(2,1)S(1)}, bf16[256,512]{1,0:T(8,128)(2,1)}, u32[]{:S(2)}, u32[]{:S(2)}) collective-permute-start(bf16[256,512]{1,0:T(8,128)(2,1)S(1)} %dynamic-slice_convert_fusion), channel_id=1, source_target_pairs={{0,4},{4,0},{1,5},{5,1},{2,6},{6,2},{3,7},{7,3},{8,12},{12,8},{9,1... | collective-permute-start | bytes 786440 | tf_op jit(solution)/shard_map/ppermute | solution.py:15
  97.2 3.1 %collective-permute-start.1 = (bf16[64,512]{1,0:T(8,128)(2,1)S(1)}, bf16[64,512]{1,0:T(8,128)(2,1)S(1)}, u32[]{:S(2)}, u32[]{:S(2)}) collective-permute-start(bf16[64,512]{1,0:T(8,128)(2,1)S(1)} %get-tuple-element.11), channel_id=1, source_target_pairs={{0,1},{1,0},{2,3},{3,2},{4,5},{5,4},{6,7},{7,6},{8,9},{9,8},{10,11... | collective-permute-start | bytes 196616 | tf_op jit(solution)/shard_map/ppermute | solution.py:15
  100.3 4.4 %collective-permute-start.2 = (bf16[64,512]{1,0:T(8,128)(2,1)S(1)}, bf16[64,512]{1,0:T(8,128)(2,1)S(1)}, u32[]{:S(2)}, u32[]{:S(2)}) collective-permute-start(bf16[64,512]{1,0:T(8,128)(2,1)S(1)} %get-tuple-element.13), channel_id=1, source_target_pairs={{0,2},{1,3},{2,0},{3,1},{4,6},{5,7},{6,4},{7,5},{8,10},{9,11},{10,... | collective-permute-start | bytes 196616 | tf_op jit(solution)/shard_map/ppermute | solution.py:15
  104.7 2.1 %collective-permute-start.3 = (bf16[64,512]{1,0:T(8,128)(2,1)S(1)}, bf16[64,512]{1,0:T(8,128)(2,1)S(1)}, u32[]{:S(2)}, u32[]{:S(2)}) collective-permute-start(bf16[64,512]{1,0:T(8,128)(2,1)S(1)} %get-tuple-element.12), channel_id=1, source_target_pairs={{0,3},{1,2},{2,1},{3,0},{4,7},{5,6},{6,5},{7,4},{8,11},{9,10},{10,... | collective-permute-start | bytes 196616 | tf_op jit(solution)/shard_map/ppermute | solution.py:15
  107.1 4.1 %collective-permute-done.3 = bf16[64,512]{1,0:T(8,128)(2,1)S(1)} collective-permute-done((bf16[64,512]{1,0:T(8,128)(2,1)S(1)}, bf16[64,512]{1,0:T(8,128)(2,1)S(1)}, u32[]{:S(2)}, u32[]{:S(2)}) %collective-permute-start.3) | collective-permute-done | bytes 65568 | tf_op jit(solution)/shard_map/ppermute | solution.py:15
  111.3 2.9 %collective-permute-start.4 = (bf16[16,512]{1,0:T(8,128)(2,1)S(1)}, bf16[16,512]{1,0:T(8,128)(2,1)S(1)}, u32[]{:S(2)}, u32[]{:S(2)}) collective-permute-start(bf16[16,512]{1,0:T(8,128)(2,1)S(1)} %get-tuple-element.16), channel_id=1, source_target_pairs={{0,128},{128,0},{256,384},{384,256},{1,129},{129,1},{257,385},{385... | collective-permute-start | bytes 49160 | tf_op jit(solution)/shard_map/ppermute | solution.py:15
  114.2 4.7 %collective-permute-start.5 = (bf16[16,512]{1,0:T(8,128)(2,1)S(1)}, bf16[16,512]{1,0:T(8,128)(2,1)S(1)}, u32[]{:S(2)}, u32[]{:S(2)}) collective-permute-start(bf16[16,512]{1,0:T(8,128)(2,1)S(1)} %get-tuple-element.18), channel_id=1, source_target_pairs={{0,256},{128,384},{256,0},{384,128},{1,257},{129,385},{257,1},{385... | collective-permute-start | bytes 49160 | tf_op jit(solution)/shard_map/ppermute | solution.py:15
  118.9 2.0 %collective-permute-start.6 = (bf16[16,512]{1,0:T(8,128)(2,1)S(1)}, bf16[16,512]{1,0:T(8,128)(2,1)S(1)}, u32[]{:S(2)}, u32[]{:S(2)}) collective-permute-start(bf16[16,512]{1,0:T(8,128)(2,1)S(1)} %get-tuple-element.17), channel_id=1, source_target_pairs={{0,384},{128,256},{256,128},{384,0},{1,385},{129,257},{257,129},{3... | collective-permute-start | bytes 49160 | tf_op jit(solution)/shard_map/ppermute | solution.py:15
  120.9 4.0 %collective-permute-done.6 = bf16[16,512]{1,0:T(8,128)(2,1)S(1)} collective-permute-done((bf16[16,512]{1,0:T(8,128)(2,1)S(1)}, bf16[16,512]{1,0:T(8,128)(2,1)S(1)}, u32[]{:S(2)}, u32[]{:S(2)}) %collective-permute-start.6) | collective-permute-done | bytes 16416 | tf_op jit(solution)/shard_map/ppermute | solution.py:15
  125.0 7.0 %collective-permute-start.7 = (f32[16,512]{1,0:T(8,128)S(1)}, f32[16,512]{1,0:T(8,128)S(1)}, u32[]{:S(2)}, u32[]{:S(2)}) collective-permute-start(f32[16,512]{1,0:T(8,128)S(1)} %convert_add_fusion.2), channel_id=1, source_target_pairs={{0,32},{8,40},{16,48},{24,56},{32,0},{40,8},{48,16},{56,24},{64,96... | collective-permute-start | bytes 98312 | tf_op jit(solution)/shard_map/ppermute | solution.py:15
  132.0 7.2 %collective-permute-start.8 = (f32[16,512]{1,0:T(8,128)S(1)}, f32[16,512]{1,0:T(8,128)S(1)}, u32[]{:S(2)}, u32[]{:S(2)}) collective-permute-start(f32[16,512]{1,0:T(8,128)S(1)} %convert_add_fusion.2), channel_id=1, source_target_pairs={{0,64},{8,72},{16,80},{24,88},{32,96},{40,104},{48,112},{56,120},{... | collective-permute-start | bytes 98312 | tf_op jit(solution)/shard_map/ppermute | solution.py:15
  139.2 2.0 %collective-permute-start.9 = (f32[16,512]{1,0:T(8,128)S(1)}, f32[16,512]{1,0:T(8,128)S(1)}, u32[]{:S(2)}, u32[]{:S(2)}) collective-permute-start(f32[16,512]{1,0:T(8,128)S(1)} %convert_add_fusion.2), channel_id=1, source_target_pairs={{0,96},{8,104},{16,112},{24,120},{32,64},{40,72},{48,80},{56,88},{... | collective-permute-start | bytes 98312 | tf_op jit(solution)/shard_map/ppermute | solution.py:15
  141.4 6.6 %collective-permute-done.8 = f32[16,512]{1,0:T(8,128)S(1)} collective-permute-done((f32[16,512]{1,0:T(8,128)S(1)}, f32[16,512]{1,0:T(8,128)S(1)}, u32[]{:S(2)}, u32[]{:S(2)}) %collective-permute-start.8) | collective-permute-done | bytes 32800 | tf_op jit(solution)/shard_map/ppermute | solution.py:15
  148.9 1.9 %collective-permute-start.10 = (f32[16,512]{1,0:T(8,128)S(1)}, f32[16,512]{1,0:T(8,128)S(1)}, u32[]{:S(2)}, u32[]{:S(2)}) collective-permute-start(f32[16,512]{1,0:T(8,128)S(1)} %add_add_fusion), channel_id=1, source_target_pairs={{0,8},{8,0},{16,24},{24,16},{32,40},{40,32},{48,56},{56,48},{64,72... | collective-permute-start | bytes 98312 | tf_op jit(solution)/shard_map/ppermute | solution.py:15
  150.8 4.4 %collective-permute-start.11 = (f32[16,512]{1,0:T(8,128)S(1)}, f32[16,512]{1,0:T(8,128)S(1)}, u32[]{:S(2)}, u32[]{:S(2)}) collective-permute-start(f32[16,512]{1,0:T(8,128)S(1)} %add_add_fusion), channel_id=1, source_target_pairs={{0,16},{8,24},{16,0},{24,8},{32,48},{40,56},{48,32},{56,40},{64,80... | collective-permute-start | bytes 98312 | tf_op jit(solution)/shard_map/ppermute | solution.py:15
  155.3 2.9 %collective-permute-start.12 = (f32[16,512]{1,0:T(8,128)S(1)}, f32[16,512]{1,0:T(8,128)S(1)}, u32[]{:S(2)}, u32[]{:S(2)}) collective-permute-start(f32[16,512]{1,0:T(8,128)S(1)} %add_add_fusion), channel_id=1, source_target_pairs={{0,24},{8,16},{16,8},{24,0},{32,56},{40,48},{48,40},{56,32},{64,88... | collective-permute-start | bytes 98312 | tf_op jit(solution)/shard_map/ppermute | solution.py:15
  158.2 3.6 %collective-permute-done.12 = f32[16,512]{1,0:T(8,128)S(1)} collective-permute-done((f32[16,512]{1,0:T(8,128)S(1)}, f32[16,512]{1,0:T(8,128)S(1)}, u32[]{:S(2)}, u32[]{:S(2)}) %collective-permute-start.12) | collective-permute-done | bytes 32800 | tf_op jit(solution)/shard_map/ppermute | solution.py:15
  162.7 10.8 %all-to-all-start.2 = ((bf16[32,16,512]{2,1,0:T(8,128)(2,1)}), bf16[32,16,512]{2,1,0:T(8,128)(2,1)S(1)}, u32[]{:S(2)}, u32[]{:S(2)}) async-start(bf16[32,16,512]{2,1,0:T(8,128)(2,1)} %broadcast_in_dim.26), calls=%async_computation.2 | async-start | bytes 1048576 | tf_op jit(solution)/shard_map/all_to_all | solution.py:56
  174.9 9.8 %all-to-all-done.2 = bf16[32,16,512]{2,1,0:T(8,128)(2,1)S(1)} async-done(((bf16[32,16,512]{2,1,0:T(8,128)(2,1)}), bf16[32,16,512]{2,1,0:T(8,128)(2,1)S(1)}, u32[]{:S(2)}, u32[]{:S(2)}) %all-to-all-start.2) | async-done | bytes 524320 | tf_op jit(solution)/shard_map/all_to_all | solution.py:56
  (54 shorter events, 12.2 us)
Async XLA Ops:
  0.6 78.9 %copy-start = (bf16[512,512]{1,0:T(8,128)(2,1)S(1)}, bf16[512,512]{1,0:T(8,128)(2,1)}, u32[]{:S(2)}) copy-start(bf16[512,512]{1,0:T(8,128)(2,1)} %param.11) | copy-start | bytes 1572868
  4.0 20.7 %copy-start.4 = (s32[256,2,128]{2,1,0:T(2,128)S(1)}, s32[256,2,128]{2,1,0:T(2,128)}, u32[]{:S(2)}) copy-start(s32[256,2,128]{2,1,0:T(2,128)} %param.14) | copy-start | bytes 786436
  4.0 20.9 %copy-start.5 = (s32[1024,2]{0,1:T(2,128)S(1)}, s32[1024,2]{0,1:T(2,128)}, u32[]{:S(2)}) copy-start(s32[1024,2]{0,1:T(2,128)} %param.19) | copy-start | bytes 24580
  4.0 20.9 %copy-start.6 = (s32[1024,2]{0,1:T(2,128)S(1)}, s32[1024,2]{0,1:T(2,128)}, u32[]{:S(2)}) copy-start(s32[1024,2]{0,1:T(2,128)} %param.18) | copy-start | bytes 24580
  4.0 75.1 %all-to-all-start = ((bf16[128,8,512]{2,1,0:T(8,128)(2,1)}), bf16[128,8,512]{2,1,0:T(8,128)(2,1)S(1)}, u32[]{:S(2)}, u32[]{:S(2)}) async-start(bf16[128,8,512]{2,1,0:T(8,128)(2,1)} %fusion), calls=%async_computation | async-start | bytes 2097152 | tf_op jit(solution)/shard_map/all_to_all | solution.py:103
  24.8 1.0 copy-start.1
  79.1 1.0 copy-start.8
  80.0 1.2 copy-start.2
  83.0 8.6 %copy-start.3 = (bf16[256,512]{1,0:T(8,128)(2,1)S(1)}, bf16[256,512]{1,0:T(8,128)(2,1)}, u32[]{:S(2)}) copy-start(bf16[256,512]{1,0:T(8,128)(2,1)} %copy-done.2) | copy-start | bytes 786436
  83.0 78.8 %all-to-all-start.1 = ((bf16[128,8,512]{2,1,0:T(8,128)(2,1)}), bf16[128,8,512]{2,1,0:T(8,128)(2,1)S(1)}, u32[]{:S(2)}, u32[]{:S(2)}) async-start(bf16[128,8,512]{2,1,0:T(8,128)(2,1)} %fusion.1), calls=%async_computation.1 | async-start | bytes 2097152 | tf_op jit(solution)/shard_map/all_to_all | solution.py:132
  92.0 4.1 %collective-permute-start = (bf16[256,512]{1,0:T(8,128)(2,1)S(1)}, bf16[256,512]{1,0:T(8,128)(2,1)}, u32[]{:S(2)}, u32[]{:S(2)}) collective-permute-start(bf16[256,512]{1,0:T(8,128)(2,1)S(1)} %dynamic-slice_convert_fusion), channel_id=1, source_target_pairs={{0,4},{4,0},{1,5},{5,1},{2,6},{6,2},{3,7},{7,3},{8,12},{12,8},{9,1... | collective-permute-start | bytes 786440 | tf_op jit(solution)/shard_map/ppermute | solution.py:15
  97.2 9.6 %collective-permute-start.1 = (bf16[64,512]{1,0:T(8,128)(2,1)S(1)}, bf16[64,512]{1,0:T(8,128)(2,1)S(1)}, u32[]{:S(2)}, u32[]{:S(2)}) collective-permute-start(bf16[64,512]{1,0:T(8,128)(2,1)S(1)} %get-tuple-element.11), channel_id=1, source_target_pairs={{0,1},{1,0},{2,3},{3,2},{4,5},{5,4},{6,7},{7,6},{8,9},{9,8},{10,11... | collective-permute-start | bytes 196616 | tf_op jit(solution)/shard_map/ppermute | solution.py:15
  100.3 6.8 %collective-permute-start.2 = (bf16[64,512]{1,0:T(8,128)(2,1)S(1)}, bf16[64,512]{1,0:T(8,128)(2,1)S(1)}, u32[]{:S(2)}, u32[]{:S(2)}) collective-permute-start(bf16[64,512]{1,0:T(8,128)(2,1)S(1)} %get-tuple-element.13), channel_id=1, source_target_pairs={{0,2},{1,3},{2,0},{3,1},{4,6},{5,7},{6,4},{7,5},{8,10},{9,11},{10,... | collective-permute-start | bytes 196616 | tf_op jit(solution)/shard_map/ppermute | solution.py:15
  104.7 6.5 %collective-permute-start.3 = (bf16[64,512]{1,0:T(8,128)(2,1)S(1)}, bf16[64,512]{1,0:T(8,128)(2,1)S(1)}, u32[]{:S(2)}, u32[]{:S(2)}) collective-permute-start(bf16[64,512]{1,0:T(8,128)(2,1)S(1)} %get-tuple-element.12), channel_id=1, source_target_pairs={{0,3},{1,2},{2,1},{3,0},{4,7},{5,6},{6,5},{7,4},{8,11},{9,10},{10,... | collective-permute-start | bytes 196616 | tf_op jit(solution)/shard_map/ppermute | solution.py:15
  111.3 9.6 %collective-permute-start.4 = (bf16[16,512]{1,0:T(8,128)(2,1)S(1)}, bf16[16,512]{1,0:T(8,128)(2,1)S(1)}, u32[]{:S(2)}, u32[]{:S(2)}) collective-permute-start(bf16[16,512]{1,0:T(8,128)(2,1)S(1)} %get-tuple-element.16), channel_id=1, source_target_pairs={{0,128},{128,0},{256,384},{384,256},{1,129},{129,1},{257,385},{385... | collective-permute-start | bytes 49160 | tf_op jit(solution)/shard_map/ppermute | solution.py:15
  114.2 6.7 %collective-permute-start.5 = (bf16[16,512]{1,0:T(8,128)(2,1)S(1)}, bf16[16,512]{1,0:T(8,128)(2,1)S(1)}, u32[]{:S(2)}, u32[]{:S(2)}) collective-permute-start(bf16[16,512]{1,0:T(8,128)(2,1)S(1)} %get-tuple-element.18), channel_id=1, source_target_pairs={{0,256},{128,384},{256,0},{384,128},{1,257},{129,385},{257,1},{385... | collective-permute-start | bytes 49160 | tf_op jit(solution)/shard_map/ppermute | solution.py:15
  118.9 6.1 %collective-permute-start.6 = (bf16[16,512]{1,0:T(8,128)(2,1)S(1)}, bf16[16,512]{1,0:T(8,128)(2,1)S(1)}, u32[]{:S(2)}, u32[]{:S(2)}) collective-permute-start(bf16[16,512]{1,0:T(8,128)(2,1)S(1)} %get-tuple-element.17), channel_id=1, source_target_pairs={{0,384},{128,256},{256,128},{384,0},{1,385},{129,257},{257,129},{3... | collective-permute-start | bytes 49160 | tf_op jit(solution)/shard_map/ppermute | solution.py:15
  125.0 16.5 %collective-permute-start.7 = (f32[16,512]{1,0:T(8,128)S(1)}, f32[16,512]{1,0:T(8,128)S(1)}, u32[]{:S(2)}, u32[]{:S(2)}) collective-permute-start(f32[16,512]{1,0:T(8,128)S(1)} %convert_add_fusion.2), channel_id=1, source_target_pairs={{0,32},{8,40},{16,48},{24,56},{32,0},{40,8},{48,16},{56,24},{64,96... | collective-permute-start | bytes 98312 | tf_op jit(solution)/shard_map/ppermute | solution.py:15
  132.0 16.0 %collective-permute-start.8 = (f32[16,512]{1,0:T(8,128)S(1)}, f32[16,512]{1,0:T(8,128)S(1)}, u32[]{:S(2)}, u32[]{:S(2)}) collective-permute-start(f32[16,512]{1,0:T(8,128)S(1)} %convert_add_fusion.2), channel_id=1, source_target_pairs={{0,64},{8,72},{16,80},{24,88},{32,96},{40,104},{48,112},{56,120},{... | collective-permute-start | bytes 98312 | tf_op jit(solution)/shard_map/ppermute | solution.py:15
  139.2 9.7 %collective-permute-start.9 = (f32[16,512]{1,0:T(8,128)S(1)}, f32[16,512]{1,0:T(8,128)S(1)}, u32[]{:S(2)}, u32[]{:S(2)}) collective-permute-start(f32[16,512]{1,0:T(8,128)S(1)} %convert_add_fusion.2), channel_id=1, source_target_pairs={{0,96},{8,104},{16,112},{24,120},{32,64},{40,72},{48,80},{56,88},{... | collective-permute-start | bytes 98312 | tf_op jit(solution)/shard_map/ppermute | solution.py:15
  148.9 9.3 %collective-permute-start.10 = (f32[16,512]{1,0:T(8,128)S(1)}, f32[16,512]{1,0:T(8,128)S(1)}, u32[]{:S(2)}, u32[]{:S(2)}) collective-permute-start(f32[16,512]{1,0:T(8,128)S(1)} %add_add_fusion), channel_id=1, source_target_pairs={{0,8},{8,0},{16,24},{24,16},{32,40},{40,32},{48,56},{56,48},{64,72... | collective-permute-start | bytes 98312 | tf_op jit(solution)/shard_map/ppermute | solution.py:15
  150.8 7.4 %collective-permute-start.11 = (f32[16,512]{1,0:T(8,128)S(1)}, f32[16,512]{1,0:T(8,128)S(1)}, u32[]{:S(2)}, u32[]{:S(2)}) collective-permute-start(f32[16,512]{1,0:T(8,128)S(1)} %add_add_fusion), channel_id=1, source_target_pairs={{0,16},{8,24},{16,0},{24,8},{32,48},{40,56},{48,32},{56,40},{64,80... | collective-permute-start | bytes 98312 | tf_op jit(solution)/shard_map/ppermute | solution.py:15
  155.3 6.5 %collective-permute-start.12 = (f32[16,512]{1,0:T(8,128)S(1)}, f32[16,512]{1,0:T(8,128)S(1)}, u32[]{:S(2)}, u32[]{:S(2)}) collective-permute-start(f32[16,512]{1,0:T(8,128)S(1)} %add_add_fusion), channel_id=1, source_target_pairs={{0,24},{8,16},{16,8},{24,0},{32,56},{40,48},{48,40},{56,32},{64,88... | collective-permute-start | bytes 98312 | tf_op jit(solution)/shard_map/ppermute | solution.py:15
  162.7 22.0 %all-to-all-start.2 = ((bf16[32,16,512]{2,1,0:T(8,128)(2,1)}), bf16[32,16,512]{2,1,0:T(8,128)(2,1)S(1)}, u32[]{:S(2)}, u32[]{:S(2)}) async-start(bf16[32,16,512]{2,1,0:T(8,128)(2,1)} %broadcast_in_dim.26), calls=%async_computation.2 | async-start | bytes 1048576 | tf_op jit(solution)/shard_map/all_to_all | solution.py:56
  (2 other events, 1.4 us)

commit v3 on v2

--- a/solution.py
+++ b/solution.py
@@ -7,7 +7,7 @@
 from jax.sharding import PartitionSpec as P
 
 
-DOM = ("y", "z", "core")
+DOM = ("y", "z_hi", "z_lo", "core")
 
 
 def from_peer(value, axis, mask):
@@ -25,36 +25,28 @@
     return total
 
 
-def quad_sum(value, axis, stride):
-    near = value + from_peer(value, axis, stride)
-    far = from_peer(value, axis, 2 * stride) + from_peer(value, axis, 3 * stride)
-    return near + far
+def quad_sum(value, axis):
+    near = value + from_peer(value, axis, 1)
+    return near + (from_peer(value, axis, 2) + from_peer(value, axis, 3))
 
 
-def gather(block, axis):
-    count, here = lax.axis_size(axis), lax.axis_index(axis)
-    rows, width = block.shape
-    whole = jnp.zeros((count * rows, width), block.dtype)
-    whole = lax.dynamic_update_slice_in_dim(whole, block, here * rows, 0)
-    for mask in range(1, count):
-        other = from_peer(block, axis, mask)
-        whole = lax.dynamic_update_slice_in_dim(whole, other, (here ^ mask) * rows, 0)
-    return whole
+def to_all(value, axes):
+    count = lax.axis_size(axes)
+    value = jnp.broadcast_to(value[None], (count,) + value.shape)
+    return lax.all_to_all(value, axes, split_axis=0, concat_axis=0, tiled=True)
 
 
 PLANE = ("core", "slab", "y")
 
 
-def sum_blocks(part, scale):
+def sum_blocks(part):
     mine = scatter_sum(scatter_sum(scatter_sum(part, "core"), "slab"), "y")
-    return (quad_sum(quad_sum(mine, "z", 4), "z", 1) * scale).astype(jnp.bfloat16)
+    return quad_sum(mine, "z_hi")
 
 
-def gather_plane(mine):
-    plane = lax.axis_size(PLANE)
-    mine = jnp.broadcast_to(mine[None], (plane,) + mine.shape)
-    whole = lax.all_to_all(mine, PLANE, split_axis=0, concat_axis=0, tiled=True)
-    return whole.reshape(-1, mine.shape[-1]).astype(jnp.float32)
+def finish_sum(mine, scale):
+    mine = (jnp.sum(to_all(mine, "z_lo"), axis=0) * scale).astype(jnp.bfloat16)
+    return to_all(mine, PLANE).reshape(-1, mine.shape[-1]).astype(jnp.float32)
 
 
 def shards(
@@ -134,9 +126,9 @@
     weight_part = lax.dot_general(
         aggregated, grad_pre, (((0,), (0,)), ((), ())), preferred_element_type=jnp.float32
     )
-    mine = sum_blocks(weight_part, 1.0 / math.sqrt(nodes_all))
+    mine = sum_blocks(weight_part)
     returned, mine = lax.optimization_barrier((returned, mine))
-    grad_weight = gather_plane(mine)
+    grad_weight = finish_sum(mine, 1.0 / math.sqrt(nodes_all))
     local_back = lax.dot_general(
         adjacency, grad_sum, (((0,), (0,)), ((), ())), preferred_element_type=jnp.float32
     )
@@ -148,9 +140,8 @@
 
 def solution(mesh):
     slab_count = mesh.shape["slab"]
-    depth = mesh.shape["dom"] // (2 * slab_count)
     split = Mesh(
-        mesh.devices.reshape(slab_count, depth, 2, slab_count), ("y", "z", "core", "slab")
+        mesh.devices.reshape(4, 4, -1, 2, slab_count), ("y", "z_hi", "z_lo", "core", "slab")
     )
     nodes = P(DOM + ("slab",))
     in_specs = (nodes, P(), nodes, nodes, nodes, nodes, nodes, nodes, nodes, nodes)

time: 187 us -> 183 us (0.979)
  starting transfers between devices: 87.5 us -> 79.3 us
  blocking collectives: 0 us -> 8.09 us
  waiting for transfers between devices: 83.9 us -> 80.3 us
    ppermute x13 -> x10, starting transfers between devices: 47.4 us -> 38.2 us  [from_peer(): lax.ppermute(value, axis, [(place, place ^ mask) for place in range(count)])]
    all_to_all x0 -> x1, blocking collectives: none -> 8.09 us  [to_all(): return lax.all_to_all(value, axes, split_axis=0, concat_axis=0, tiled=True)]
    ppermute x13 -> x10, waiting for transfers between devices: 21 us -> 17.4 us  [from_peer(): lax.ppermute(value, axis, [(place, place ^ mask) for place in range(count)])]
  transfers between devices with their start and end apart: 16 -> 13, of which waited for: 10 -> 9; matrix products, arithmetic and copies ran while one was open for 2% -> 2% of each run, Pallas kernels for 0% -> 0%
where the time goes in v3:
time: 183 us; the launch traced here: 182 us
  waiting for transfers between devices  80.3 us (44%)
  starting transfers between devices  79.3 us (43%)
  matrix products  9.01 us (5%)
  blocking collectives  8.09 us (4%)
  other arithmetic  2.77 us (2%)
    all_to_all x1, waiting for transfers between devices, shards(): lax.all_to_all(outgoing, DOM, split_axis=0, concat_axis=0, tiled=True)  53.1 us
    ppermute x10, starting transfers between devices, from_peer(): lax.ppermute(value, axis, [(place, place ^ mask) for place in range(count)])  38.2 us
    all_to_all x1, starting transfers between devices, shards(): lax.all_to_all(outgoing, DOM, split_axis=0, concat_axis=0, tiled=True)  20.7 us
    ppermute x10, waiting for transfers between devices, from_peer(): lax.ppermute(value, axis, [(place, place ^ mask) for place in range(count)])  17.4 us
    all_to_all x1, starting transfers between devices, to_all(): return lax.all_to_all(value, axes, split_axis=0, concat_axis=0, tiled=True)  11.9 us
    all_to_all x1, waiting for transfers between devices, to_all(): return lax.all_to_all(value, axes, split_axis=0, concat_axis=0, tiled=True)  9.78 us
    all_to_all x1, starting transfers between devices, shards(): lax.all_to_all(slot_grad, DOM, split_axis=0, concat_axis=0, tiled=True)  8.61 us
    all_to_all x1, blocking collectives, to_all(): return lax.all_to_all(value, axes, split_axis=0, concat_axis=0, tiled=True)  8.09 us
  transfers between devices with their start and end apart: 13, of which 9 were waited for; matrix products, arithmetic and copies ran while one was open for 2% of the time, Pallas kernels for 0%

profile of v3, /device:TPU:1, one launch (start us, length us, event | category | flops | bytes accessed | tf_op | source)
XLA Modules:
  0.0 182.1 jit_solution(1012320664095690160)
XLA Ops:
  1.6 2.4 %fusion = bf16[128,8,512]{2,1,0:T(8,128)(2,1)} fusion(bf16[256,512]{1,0:T(8,128)(2,1)} %param.10, s32[1024]{0:T(1024)S(1)} %convert_element_type.127), kind=kOutput, calls=%fused_computation.4 | convolution fusion | flops 269221888 | bytes 1314816 | tf_op jit(solution)/shard_map/dot_general | solution.py:91
  4.0 20.7 %all-to-all-start = ((bf16[128,8,512]{2,1,0:T(8,128)(2,1)}), bf16[128,8,512]{2,1,0:T(8,128)(2,1)S(1)}, u32[]{:S(2)}, u32[]{:S(2)}) async-start(bf16[128,8,512]{2,1,0:T(8,128)(2,1)} %fusion), calls=%async_computation | async-start | bytes 2097152 | tf_op jit(solution)/shard_map/all_to_all | solution.py:95
  26.0 53.1 %all-to-all-done = bf16[128,8,512]{2,1,0:T(8,128)(2,1)S(1)} async-done(((bf16[128,8,512]{2,1,0:T(8,128)(2,1)}), bf16[128,8,512]{2,1,0:T(8,128)(2,1)S(1)}, u32[]{:S(2)}, u32[]{:S(2)}) %all-to-all-start) | async-done | bytes 1048608 | tf_op jit(solution)/shard_map/all_to_all | solution.py:95
  80.1 1.2 multiply_convert_fusion
  81.6 1.4 fusion.1
  83.0 8.6 %all-to-all-start.1 = ((bf16[128,8,512]{2,1,0:T(8,128)(2,1)}), bf16[128,8,512]{2,1,0:T(8,128)(2,1)S(1)}, u32[]{:S(2)}, u32[]{:S(2)}) async-start(bf16[128,8,512]{2,1,0:T(8,128)(2,1)} %fusion.1), calls=%async_computation.1 | async-start | bytes 2097152 | tf_op jit(solution)/shard_map/all_to_all | solution.py:124
  92.0 2.8 %collective-permute-start = (bf16[256,512]{1,0:T(8,128)(2,1)S(1)}, bf16[256,512]{1,0:T(8,128)(2,1)}, u32[]{:S(2)}, u32[]{:S(2)}) collective-permute-start(bf16[256,512]{1,0:T(8,128)(2,1)S(1)} %dynamic-slice_convert_fusion), channel_id=1, source_target_pairs={{0,4},{4,0},{1,5},{5,1},{2,6},{6,2},{3,7},{7,3},{8,12},{12,8},{9,1... | collective-permute-start | bytes 786440 | tf_op jit(solution)/shard_map/ppermute | solution.py:15
  94.9 1.2 collective-permute-done
  97.2 3.1 %collective-permute-start.1 = (bf16[64,512]{1,0:T(8,128)(2,1)S(1)}, bf16[64,512]{1,0:T(8,128)(2,1)S(1)}, u32[]{:S(2)}, u32[]{:S(2)}) collective-permute-start(bf16[64,512]{1,0:T(8,128)(2,1)S(1)} %get-tuple-element.11), channel_id=1, source_target_pairs={{0,1},{1,0},{2,3},{3,2},{4,5},{5,4},{6,7},{7,6},{8,9},{9,8},{10,11... | collective-permute-start | bytes 196616 | tf_op jit(solution)/shard_map/ppermute | solution.py:15
  100.3 4.4 %collective-permute-start.2 = (bf16[64,512]{1,0:T(8,128)(2,1)S(1)}, bf16[64,512]{1,0:T(8,128)(2,1)S(1)}, u32[]{:S(2)}, u32[]{:S(2)}) collective-permute-start(bf16[64,512]{1,0:T(8,128)(2,1)S(1)} %get-tuple-element.13), channel_id=1, source_target_pairs={{0,2},{1,3},{2,0},{3,1},{4,6},{5,7},{6,4},{7,5},{8,10},{9,11},{10,... | collective-permute-start | bytes 196616 | tf_op jit(solution)/shard_map/ppermute | solution.py:15
  104.7 2.1 %collective-permute-start.3 = (bf16[64,512]{1,0:T(8,128)(2,1)S(1)}, bf16[64,512]{1,0:T(8,128)(2,1)S(1)}, u32[]{:S(2)}, u32[]{:S(2)}) collective-permute-start(bf16[64,512]{1,0:T(8,128)(2,1)S(1)} %get-tuple-element.12), channel_id=1, source_target_pairs={{0,3},{1,2},{2,1},{3,0},{4,7},{5,6},{6,5},{7,4},{8,11},{9,10},{10,... | collective-permute-start | bytes 196616 | tf_op jit(solution)/shard_map/ppermute | solution.py:15
  107.1 4.1 %collective-permute-done.3 = bf16[64,512]{1,0:T(8,128)(2,1)S(1)} collective-permute-done((bf16[64,512]{1,0:T(8,128)(2,1)S(1)}, bf16[64,512]{1,0:T(8,128)(2,1)S(1)}, u32[]{:S(2)}, u32[]{:S(2)}) %collective-permute-start.3) | collective-permute-done | bytes 65568 | tf_op jit(solution)/shard_map/ppermute | solution.py:15
  111.3 2.9 %collective-permute-start.4 = (bf16[16,512]{1,0:T(8,128)(2,1)S(1)}, bf16[16,512]{1,0:T(8,128)(2,1)S(1)}, u32[]{:S(2)}, u32[]{:S(2)}) collective-permute-start(bf16[16,512]{1,0:T(8,128)(2,1)S(1)} %get-tuple-element.16), channel_id=1, source_target_pairs={{0,128},{128,0},{256,384},{384,256},{1,129},{129,1},{257,385},{385... | collective-permute-start | bytes 49160 | tf_op jit(solution)/shard_map/ppermute | solution.py:15
  114.2 4.7 %collective-permute-start.5 = (bf16[16,512]{1,0:T(8,128)(2,1)S(1)}, bf16[16,512]{1,0:T(8,128)(2,1)S(1)}, u32[]{:S(2)}, u32[]{:S(2)}) collective-permute-start(bf16[16,512]{1,0:T(8,128)(2,1)S(1)} %get-tuple-element.18), channel_id=1, source_target_pairs={{0,256},{128,384},{256,0},{384,128},{1,257},{129,385},{257,1},{385... | collective-permute-start | bytes 49160 | tf_op jit(solution)/shard_map/ppermute | solution.py:15
  118.9 2.0 %collective-permute-start.6 = (bf16[16,512]{1,0:T(8,128)(2,1)S(1)}, bf16[16,512]{1,0:T(8,128)(2,1)S(1)}, u32[]{:S(2)}, u32[]{:S(2)}) collective-permute-start(bf16[16,512]{1,0:T(8,128)(2,1)S(1)} %get-tuple-element.17), channel_id=1, source_target_pairs={{0,384},{128,256},{256,128},{384,0},{1,385},{129,257},{257,129},{3... | collective-permute-start | bytes 49160 | tf_op jit(solution)/shard_map/ppermute | solution.py:15
  120.9 4.0 %collective-permute-done.6 = bf16[16,512]{1,0:T(8,128)(2,1)S(1)} collective-permute-done((bf16[16,512]{1,0:T(8,128)(2,1)S(1)}, bf16[16,512]{1,0:T(8,128)(2,1)S(1)}, u32[]{:S(2)}, u32[]{:S(2)}) %collective-permute-start.6) | collective-permute-done | bytes 16416 | tf_op jit(solution)/shard_map/ppermute | solution.py:15
  125.0 7.0 %collective-permute-start.7 = (f32[16,512]{1,0:T(8,128)S(1)}, f32[16,512]{1,0:T(8,128)S(1)}, u32[]{:S(2)}, u32[]{:S(2)}) collective-permute-start(f32[16,512]{1,0:T(8,128)S(1)} %convert_add_fusion.2), channel_id=1, source_target_pairs={{0,32},{32,0},{64,96},{96,64},{1,33},{33,1},{65,97},{97,65},{2,34}... | collective-permute-start | bytes 98312 | tf_op jit(solution)/shard_map/ppermute | solution.py:15
  132.0 7.2 %collective-permute-start.8 = (f32[16,512]{1,0:T(8,128)S(1)}, f32[16,512]{1,0:T(8,128)S(1)}, u32[]{:S(2)}, u32[]{:S(2)}) collective-permute-start(f32[16,512]{1,0:T(8,128)S(1)} %convert_add_fusion.2), channel_id=1, source_target_pairs={{0,64},{32,96},{64,0},{96,32},{1,65},{33,97},{65,1},{97,33},{2,66}... | collective-permute-start | bytes 98312 | tf_op jit(solution)/shard_map/ppermute | solution.py:15
  139.2 2.0 %collective-permute-start.9 = (f32[16,512]{1,0:T(8,128)S(1)}, f32[16,512]{1,0:T(8,128)S(1)}, u32[]{:S(2)}, u32[]{:S(2)}) collective-permute-start(f32[16,512]{1,0:T(8,128)S(1)} %convert_add_fusion.2), channel_id=1, source_target_pairs={{0,96},{32,64},{64,32},{96,0},{1,97},{33,65},{65,33},{97,1},{2,98}... | collective-permute-start | bytes 98312 | tf_op jit(solution)/shard_map/ppermute | solution.py:15
  141.4 6.6 %collective-permute-done.8 = f32[16,512]{1,0:T(8,128)S(1)} collective-permute-done((f32[16,512]{1,0:T(8,128)S(1)}, f32[16,512]{1,0:T(8,128)S(1)}, u32[]{:S(2)}, u32[]{:S(2)}) %collective-permute-start.8) | collective-permute-done | bytes 32800 | tf_op jit(solution)/shard_map/ppermute | solution.py:15
  148.9 8.1 %all_to_all.20 = f32[4,16,512]{2,1,0:T(8,128)S(1)} all-to-all(f32[4,16,512]{2,1,0:T(8,128)S(1)} %broadcast_in_dim.28), channel_id=1, replica_groups=mesh['y'=4,'z_hi'=4,'z_lo'=4,'core'=2,'slab'=4] {'z_lo'}, dimensions={0} | all-to-all | bytes 262144 | tf_op jit(solution)/shard_map/all_to_all | solution.py:36
  157.9 11.9 %all-to-all-start.3 = ((bf16[32,16,512]{2,1,0:T(8,128)(2,1)}), bf16[32,16,512]{2,1,0:T(8,128)(2,1)S(1)}, u32[]{:S(2)}, u32[]{:S(2)}) async-start(bf16[32,16,512]{2,1,0:T(8,128)(2,1)} %broadcast_in_dim.29), calls=%async_computation.3 | async-start | bytes 1048576 | tf_op jit(solution)/shard_map/all_to_all | solution.py:36
  170.1 1.2 fusion.3
  171.2 9.8 %all-to-all-done.3 = bf16[32,16,512]{2,1,0:T(8,128)(2,1)S(1)} async-done(((bf16[32,16,512]{2,1,0:T(8,128)(2,1)}), bf16[32,16,512]{2,1,0:T(8,128)(2,1)S(1)}, u32[]{:S(2)}, u32[]{:S(2)}) %all-to-all-start.3) | async-done | bytes 524320 | tf_op jit(solution)/shard_map/all_to_all | solution.py:36
  (51 shorter events, 8.6 us)
Async XLA Ops:
  0.6 78.9 %copy-start = (bf16[512,512]{1,0:T(8,128)(2,1)S(1)}, bf16[512,512]{1,0:T(8,128)(2,1)}, u32[]{:S(2)}) copy-start(bf16[512,512]{1,0:T(8,128)(2,1)} %param.11) | copy-start | bytes 1572868
  4.0 20.7 %copy-start.4 = (s32[256,2,128]{2,1,0:T(2,128)S(1)}, s32[256,2,128]{2,1,0:T(2,128)}, u32[]{:S(2)}) copy-start(s32[256,2,128]{2,1,0:T(2,128)} %param.14) | copy-start | bytes 786436
  4.0 20.9 %copy-start.5 = (s32[1024,2]{0,1:T(2,128)S(1)}, s32[1024,2]{0,1:T(2,128)}, u32[]{:S(2)}) copy-start(s32[1024,2]{0,1:T(2,128)} %param.19) | copy-start | bytes 24580
  4.0 20.9 %copy-start.6 = (s32[1024,2]{0,1:T(2,128)S(1)}, s32[1024,2]{0,1:T(2,128)}, u32[]{:S(2)}) copy-start(s32[1024,2]{0,1:T(2,128)} %param.18) | copy-start | bytes 24580
  4.0 75.1 %all-to-all-start = ((bf16[128,8,512]{2,1,0:T(8,128)(2,1)}), bf16[128,8,512]{2,1,0:T(8,128)(2,1)S(1)}, u32[]{:S(2)}, u32[]{:S(2)}) async-start(bf16[128,8,512]{2,1,0:T(8,128)(2,1)} %fusion), calls=%async_computation | async-start | bytes 2097152 | tf_op jit(solution)/shard_map/all_to_all | solution.py:95
  24.8 0.7 copy-start.7
  24.8 0.7 copy-start.9
  24.8 1.0 copy-start.1
  79.1 1.0 copy-start.8
  80.0 1.2 copy-start.2
  83.0 8.6 %copy-start.3 = (bf16[256,512]{1,0:T(8,128)(2,1)S(1)}, bf16[256,512]{1,0:T(8,128)(2,1)}, u32[]{:S(2)}) copy-start(bf16[256,512]{1,0:T(8,128)(2,1)} %copy-done.2) | copy-start | bytes 786436
  83.0 65.9 %all-to-all-start.1 = ((bf16[128,8,512]{2,1,0:T(8,128)(2,1)}), bf16[128,8,512]{2,1,0:T(8,128)(2,1)S(1)}, u32[]{:S(2)}, u32[]{:S(2)}) async-start(bf16[128,8,512]{2,1,0:T(8,128)(2,1)} %fusion.1), calls=%async_computation.1 | async-start | bytes 2097152 | tf_op jit(solution)/shard_map/all_to_all | solution.py:124
  92.0 4.1 %collective-permute-start = (bf16[256,512]{1,0:T(8,128)(2,1)S(1)}, bf16[256,512]{1,0:T(8,128)(2,1)}, u32[]{:S(2)}, u32[]{:S(2)}) collective-permute-start(bf16[256,512]{1,0:T(8,128)(2,1)S(1)} %dynamic-slice_convert_fusion), channel_id=1, source_target_pairs={{0,4},{4,0},{1,5},{5,1},{2,6},{6,2},{3,7},{7,3},{8,12},{12,8},{9,1... | collective-permute-start | bytes 786440 | tf_op jit(solution)/shard_map/ppermute | solution.py:15
  97.2 9.6 %collective-permute-start.1 = (bf16[64,512]{1,0:T(8,128)(2,1)S(1)}, bf16[64,512]{1,0:T(8,128)(2,1)S(1)}, u32[]{:S(2)}, u32[]{:S(2)}) collective-permute-start(bf16[64,512]{1,0:T(8,128)(2,1)S(1)} %get-tuple-element.11), channel_id=1, source_target_pairs={{0,1},{1,0},{2,3},{3,2},{4,5},{5,4},{6,7},{7,6},{8,9},{9,8},{10,11... | collective-permute-start | bytes 196616 | tf_op jit(solution)/shard_map/ppermute | solution.py:15
  100.3 6.8 %collective-permute-start.2 = (bf16[64,512]{1,0:T(8,128)(2,1)S(1)}, bf16[64,512]{1,0:T(8,128)(2,1)S(1)}, u32[]{:S(2)}, u32[]{:S(2)}) collective-permute-start(bf16[64,512]{1,0:T(8,128)(2,1)S(1)} %get-tuple-element.13), channel_id=1, source_target_pairs={{0,2},{1,3},{2,0},{3,1},{4,6},{5,7},{6,4},{7,5},{8,10},{9,11},{10,... | collective-permute-start | bytes 196616 | tf_op jit(solution)/shard_map/ppermute | solution.py:15
  104.7 6.5 %collective-permute-start.3 = (bf16[64,512]{1,0:T(8,128)(2,1)S(1)}, bf16[64,512]{1,0:T(8,128)(2,1)S(1)}, u32[]{:S(2)}, u32[]{:S(2)}) collective-permute-start(bf16[64,512]{1,0:T(8,128)(2,1)S(1)} %get-tuple-element.12), channel_id=1, source_target_pairs={{0,3},{1,2},{2,1},{3,0},{4,7},{5,6},{6,5},{7,4},{8,11},{9,10},{10,... | collective-permute-start | bytes 196616 | tf_op jit(solution)/shard_map/ppermute | solution.py:15
  111.3 9.6 %collective-permute-start.4 = (bf16[16,512]{1,0:T(8,128)(2,1)S(1)}, bf16[16,512]{1,0:T(8,128)(2,1)S(1)}, u32[]{:S(2)}, u32[]{:S(2)}) collective-permute-start(bf16[16,512]{1,0:T(8,128)(2,1)S(1)} %get-tuple-element.16), channel_id=1, source_target_pairs={{0,128},{128,0},{256,384},{384,256},{1,129},{129,1},{257,385},{385... | collective-permute-start | bytes 49160 | tf_op jit(solution)/shard_map/ppermute | solution.py:15
  114.2 6.7 %collective-permute-start.5 = (bf16[16,512]{1,0:T(8,128)(2,1)S(1)}, bf16[16,512]{1,0:T(8,128)(2,1)S(1)}, u32[]{:S(2)}, u32[]{:S(2)}) collective-permute-start(bf16[16,512]{1,0:T(8,128)(2,1)S(1)} %get-tuple-element.18), channel_id=1, source_target_pairs={{0,256},{128,384},{256,0},{384,128},{1,257},{129,385},{257,1},{385... | collective-permute-start | bytes 49160 | tf_op jit(solution)/shard_map/ppermute | solution.py:15
  118.9 6.1 %collective-permute-start.6 = (bf16[16,512]{1,0:T(8,128)(2,1)S(1)}, bf16[16,512]{1,0:T(8,128)(2,1)S(1)}, u32[]{:S(2)}, u32[]{:S(2)}) collective-permute-start(bf16[16,512]{1,0:T(8,128)(2,1)S(1)} %get-tuple-element.17), channel_id=1, source_target_pairs={{0,384},{128,256},{256,128},{384,0},{1,385},{129,257},{257,129},{3... | collective-permute-start | bytes 49160 | tf_op jit(solution)/shard_map/ppermute | solution.py:15
  125.0 16.5 %collective-permute-start.7 = (f32[16,512]{1,0:T(8,128)S(1)}, f32[16,512]{1,0:T(8,128)S(1)}, u32[]{:S(2)}, u32[]{:S(2)}) collective-permute-start(f32[16,512]{1,0:T(8,128)S(1)} %convert_add_fusion.2), channel_id=1, source_target_pairs={{0,32},{32,0},{64,96},{96,64},{1,33},{33,1},{65,97},{97,65},{2,34}... | collective-permute-start | bytes 98312 | tf_op jit(solution)/shard_map/ppermute | solution.py:15
  132.0 16.0 %collective-permute-start.8 = (f32[16,512]{1,0:T(8,128)S(1)}, f32[16,512]{1,0:T(8,128)S(1)}, u32[]{:S(2)}, u32[]{:S(2)}) collective-permute-start(f32[16,512]{1,0:T(8,128)S(1)} %convert_add_fusion.2), channel_id=1, source_target_pairs={{0,64},{32,96},{64,0},{96,32},{1,65},{33,97},{65,1},{97,33},{2,66}... | collective-permute-start | bytes 98312 | tf_op jit(solution)/shard_map/ppermute | solution.py:15
  139.2 9.7 %collective-permute-start.9 = (f32[16,512]{1,0:T(8,128)S(1)}, f32[16,512]{1,0:T(8,128)S(1)}, u32[]{:S(2)}, u32[]{:S(2)}) collective-permute-start(f32[16,512]{1,0:T(8,128)S(1)} %convert_add_fusion.2), channel_id=1, source_target_pairs={{0,96},{32,64},{64,32},{96,0},{1,97},{33,65},{65,33},{97,1},{2,98}... | collective-permute-start | bytes 98312 | tf_op jit(solution)/shard_map/ppermute | solution.py:15
  157.9 23.1 %all-to-all-start.3 = ((bf16[32,16,512]{2,1,0:T(8,128)(2,1)}), bf16[32,16,512]{2,1,0:T(8,128)(2,1)S(1)}, u32[]{:S(2)}, u32[]{:S(2)}) async-start(bf16[32,16,512]{2,1,0:T(8,128)(2,1)} %broadcast_in_dim.29), calls=%async_computation.3 | async-start | bytes 1048576 | tf_op jit(solution)/shard_map/all_to_all | solution.py:36

commit v4 on v3

--- a/solution.py
+++ b/solution.py
@@ -3,6 +3,8 @@
 import jax
 import jax.numpy as jnp
 from jax import lax
+from jax.experimental import pallas as pl
+from jax.experimental.pallas import tpu as pltpu
 from jax.sharding import Mesh
 from jax.sharding import PartitionSpec as P
 
@@ -47,6 +49,152 @@
 def finish_sum(mine, scale):
     mine = (jnp.sum(to_all(mine, "z_lo"), axis=0) * scale).astype(jnp.bfloat16)
     return to_all(mine, PLANE).reshape(-1, mine.shape[-1]).astype(jnp.float32)
+
+
+VMEM = pl.BlockSpec(memory_space=pltpu.VMEM)
+HBM = pl.BlockSpec(memory_space=pltpu.HBM)
+PARTS = 4
+
+
+def layer_kernel(
+    incoming, mixing, mixing_rows, local_sum, inv_degree, weight, cotangent,
+    output, aggregated, grad_pre, grad_sum, slot_grad,
+    output_rows, aggregated_rows, grad_rows, summed_rows, slots, done,
+):
+    copies = []
+
+    def leave(source, target):
+        copy = pltpu.make_async_copy(source, target, done.at[len(copies)])
+        copy.start()
+        copies.append(copy)
+
+    inverse = inv_degree[...]
+    remote = jnp.dot(mixing[...], incoming[...], preferred_element_type=jnp.float32)
+    gathered = ((local_sum[...] + remote) * inverse).astype(jnp.bfloat16)
+    aggregated_rows[...] = gathered
+    leave(aggregated_rows, aggregated)
+    pre_act = jnp.dot(gathered, weight[...], preferred_element_type=jnp.float32)
+    gating_value = jax.nn.sigmoid(pre_act)
+    output_rows[...] = (pre_act * gating_value).astype(jnp.bfloat16)
+    leave(output_rows, output)
+    scaled = cotangent[...].astype(jnp.float32) * gating_value
+    grad = (scaled * (1.0 + pre_act * (1.0 - gating_value))).astype(jnp.bfloat16)
+    grad_rows[...] = grad
+    leave(grad_rows, grad_pre)
+    summed = lax.dot_general(
+        grad, weight[...], (((1,), (1,)), ((), ())), preferred_element_type=jnp.float32
+    )
+    summed = (summed * inverse).astype(jnp.bfloat16)
+    summed_rows[...] = summed
+    leave(summed_rows, grad_sum)
+    rows = slots.shape[0] // PARTS
+    for part in range(PARTS):
+        span = pl.ds(part * rows, rows)
+        slots[span, :] = jnp.dot(
+            mixing_rows[span, :], summed, preferred_element_type=jnp.float32
+        ).astype(jnp.bfloat16)
+        leave(slots.at[span, :], slot_grad.at[span, :])
+    for copy in copies:
+        copy.wait()
+
+
+def layer(incoming, mixing, local_sum, inv_degree, weight, cotangent):
+    nodes, slot_count = mixing.shape
+    width = weight.shape[0]
+    rows = pltpu.HBM((nodes, width), jnp.bfloat16)
+    return pl.pallas_call(
+        layer_kernel,
+        out_shape=(rows, rows, rows, rows, pltpu.HBM((slot_count, width), jnp.bfloat16)),
+        in_specs=[VMEM] * 7,
+        out_specs=(HBM,) * 5,
+        scratch_shapes=[pltpu.VMEM((nodes, width), jnp.bfloat16)] * 4
+        + [
+            pltpu.VMEM((slot_count, width), jnp.bfloat16),
+            pltpu.SemaphoreType.DMA((4 + PARTS,)),
+        ],
+        compiler_params=pltpu.CompilerParams(vmem_limit_bytes=24 << 20),
+        cost_estimate=pl.CostEstimate(
+            flops=2 * nodes * width * (2 * slot_count + 2 * width),
+            bytes_accessed=6 << 20,
+            transcendentals=nodes * width,
+        ),
+        name="layer",
+    )(incoming, mixing, mixing.T, local_sum, inv_degree[:, None], weight, cotangent)
+
+
+def take_kernel(
+    send_rows, send_count, node_feats, outgoing, row_table, counts, feats, taken, ready, done
+):
+    arrivals = []
+    for at, (source, target) in enumerate(
+        ((send_rows, row_table), (send_count, counts), (node_feats, feats))
+    ):
+        copy = pltpu.make_async_copy(source, target, ready.at[at])
+        copy.start()
+        arrivals.append(copy)
+    slot_cap, peer_count = row_table.shape
+    nodes, slot_count = feats.shape[0], taken.shape[0]
+    slot = lax.broadcasted_iota(jnp.int32, (slot_count, peer_count), 0)
+    first = slot_cap * lax.broadcasted_iota(jnp.int32, (slot_count, peer_count), 1)
+    place = jnp.where((slot >= first) & (slot < first + slot_cap), 1.0, 0.0)
+    slot = lax.broadcasted_iota(jnp.int32, (slot_count, slot_cap), 0)
+    column = lax.rem(slot, slot_cap) == lax.broadcasted_iota(jnp.int32, slot.shape, 1)
+    arrivals[0].wait()
+    arrivals[1].wait()
+    rank = lax.broadcasted_iota(jnp.int32, (slot_cap, peer_count), 0)
+    live = jnp.where(rank < counts[...], row_table[...], nodes).astype(jnp.float32)
+    spread = lax.dot_general(
+        place.astype(jnp.bfloat16),
+        live.astype(jnp.bfloat16),
+        (((1,), (1,)), ((), ())),
+        preferred_element_type=jnp.float32,
+    )
+    spread = jnp.where(column, spread, 0.0).astype(jnp.bfloat16)
+    row = jnp.dot(
+        spread, jnp.ones((slot_cap, nodes), jnp.bfloat16), preferred_element_type=jnp.float32
+    )
+    node = lax.broadcasted_iota(jnp.int32, row.shape, 1).astype(jnp.float32)
+    chosen = jnp.where(row == node, 1.0, 0.0).astype(jnp.bfloat16)
+    arrivals[2].wait()
+    rows = slot_count // PARTS
+    copies = []
+    for part in range(PARTS):
+        span = pl.ds(part * rows, rows)
+        taken[span, :] = jnp.dot(
+            chosen[part * rows : (part + 1) * rows], feats[...], preferred_element_type=jnp.float32
+        ).astype(jnp.bfloat16)
+        copy = pltpu.make_async_copy(taken.at[span, :], outgoing.at[span, :], done.at[part])
+        copy.start()
+        copies.append(copy)
+    for copy in copies:
+        copy.wait()
+
+
+def take_rows(send_rows, send_count, node_feats):
+    peer_count, slot_cap = send_rows.shape
+    nodes, width = node_feats.shape
+    slots = jax.ShapeDtypeStruct((peer_count * slot_cap, width), jnp.bfloat16)
+    return pl.pallas_call(
+        take_kernel,
+        out_shape=slots,
+        in_specs=[HBM] * 3,
+        out_specs=HBM,
+        scratch_shapes=[
+            pltpu.VMEM((slot_cap, peer_count), jnp.int32),
+            pltpu.VMEM((1, peer_count), jnp.int32),
+            pltpu.VMEM((nodes, width), jnp.bfloat16),
+            pltpu.VMEM(slots.shape, slots.dtype),
+            pltpu.SemaphoreType.DMA((3,)),
+            pltpu.SemaphoreType.DMA((PARTS,)),
+        ],
+        compiler_params=pltpu.CompilerParams(vmem_limit_bytes=63_400_000),
+        cost_estimate=pl.CostEstimate(
+            flops=2 * nodes * width * peer_count * slot_cap,
+            bytes_accessed=2 << 20,
+            transcendentals=0,
+        ),
+        name="take_rows",
+    )(send_rows.T, send_count[None, :], node_feats)
 
 
 def shards(
@@ -88,10 +236,8 @@
     own_column = jnp.arange(slot_cap, dtype=jnp.int32)[:, None] == slot_ids[None, :] % slot_cap
     flat_rows = jnp.sum(jnp.where(own_column, spread, 0.0), axis=0)
     owner = (row_ids[:, None] == flat_rows.astype(jnp.int32)[None, :]).astype(jnp.bfloat16)
-    outgoing = lax.dot_general(
-        owner, node_feats, (((0,), (0,)), ((), ())), preferred_element_type=jnp.float32
-    )
-    outgoing = outgoing.astype(jnp.bfloat16).reshape(peer_count, slot_cap, feat_width)
+    outgoing = take_rows(send_rows, send_count, node_feats)
+    outgoing = outgoing.reshape(peer_count, slot_cap, feat_width)
     incoming = lax.all_to_all(outgoing, DOM, split_axis=0, concat_axis=0, tiled=True).reshape(
         slot_count, feat_width
     )
@@ -103,23 +249,11 @@
         axis=2,
     )
     mixing = mixing.astype(jnp.bfloat16)
-    remote = jnp.dot(mixing, incoming, preferred_element_type=jnp.float32)
     inv_degree = 1.0 / degrees.astype(jnp.float32)
-    aggregated = ((local_sum + remote) * inv_degree[:, None]).astype(jnp.bfloat16)
-    pre_act = jnp.dot(aggregated, weight, preferred_element_type=jnp.float32)
-    gating_value = jax.nn.sigmoid(pre_act)
-    output = (pre_act * gating_value).astype(jnp.bfloat16)
-    grad_pre = (
-        cotangent.astype(jnp.float32) * gating_value * (1.0 + pre_act * (1.0 - gating_value))
-    ).astype(jnp.bfloat16)
-    grad_sum = lax.dot_general(
-        grad_pre, weight, (((1,), (1,)), ((), ())), preferred_element_type=jnp.float32
-    )
-    grad_sum = (grad_sum * inv_degree[:, None]).astype(jnp.bfloat16)
-    slot_grad = lax.dot_general(
-        mixing, grad_sum, (((0,), (0,)), ((), ())), preferred_element_type=jnp.float32
-    )
-    slot_grad = slot_grad.astype(jnp.bfloat16).reshape(peer_count, slot_cap, feat_width)
+    output, aggregated, grad_pre, grad_sum, slot_grad = layer(
+        incoming, mixing, local_sum, inv_degree, weight, cotangent
+    )
+    slot_grad = slot_grad.reshape(peer_count, slot_cap, feat_width)
     slot_grad, aggregated = lax.optimization_barrier((slot_grad, aggregated))
     returned = lax.all_to_all(slot_grad, DOM, split_axis=0, concat_axis=0, tiled=True)
     returned = returned.reshape(slot_count, feat_width)

time: 183 us -> 182 us (level)
  blocking collectives: 8.09 us -> 0 us
  matrix products: 9.01 us -> 2.44 us
  Pallas kernels: 0 us -> 4.68 us
  starting transfers between devices: 79.3 us -> 83.5 us
  local copies, waits for them, and re-layouts: 1.6 us -> 4.89 us
    all_to_all x1 -> x0, blocking collectives: 8.09 us -> none  [to_all(): return lax.all_to_all(value, axes, split_axis=0, concat_axis=0, tiled=True)]
    dot_general x5 -> x0, matrix products: 5.82 us -> none  [the longest x1 2.41 us: shards(): lax.dot_general(owner, node_feats, (((0,), (0,)), ((), ())), preferred_el...]
    all_to_all x1, waiting for transfers between devices: 53.1 us -> 47.8 us  [shards(): lax.all_to_all(outgoing, DOM, split_axis=0, concat_axis=0, tiled=True)]
    pallas_call x0 -> x2, Pallas kernels: none -> 4.68 us  [the longest x1 2.52 us: take_rows(): pl.pallas_call(take_kernel, out_shape=slots, in_specs=[HBM] * 3, out_spec...]
    all_to_all x1 -> x2, waiting for transfers between devices: 9.78 us -> 14.2 us  [to_all(): return lax.all_to_all(value, axes, split_axis=0, concat_axis=0, tiled=True)]
    all_to_all x1 -> x2, starting transfers between devices: 11.9 us -> 16.2 us  [to_all(): return lax.all_to_all(value, axes, split_axis=0, concat_axis=0, tiled=True)]
  transfers between devices with their start and end apart: 13 -> 14, of which waited for: 9 -> 9; matrix products, arithmetic and copies ran while one was open for 2% -> 4% of each run, Pallas kernels for 0% -> 0%
where the time goes in v4:
time: 182 us; the launch traced here: 181 us
  starting transfers between devices  83.5 us (46%)
  waiting for transfers between devices  80.3 us (44%)
  local copies, waits for them, and re-layouts  4.89 us (3%)
  Pallas kernels  4.68 us (3%)
  other arithmetic  3.92 us (2%)
  matrix products  2.44 us (1%)
    all_to_all x1, waiting for transfers between devices, shards(): lax.all_to_all(outgoing, DOM, split_axis=0, concat_axis=0, tiled=True)  47.8 us
    ppermute x10, starting transfers between devices, from_peer(): lax.ppermute(value, axis, [(place, place ^ mask) for place in range(count)])  38.2 us
    all_to_all x1, starting transfers between devices, shards(): lax.all_to_all(outgoing, DOM, split_axis=0, concat_axis=0, tiled=True)  20.6 us
    ppermute x10, waiting for transfers between devices, from_peer(): lax.ppermute(value, axis, [(place, place ^ mask) for place in range(count)])  18.3 us
    all_to_all x2, starting transfers between devices, to_all(): return lax.all_to_all(value, axes, split_axis=0, concat_axis=0, tiled=True)  16.2 us
    all_to_all x2, waiting for transfers between devices, to_all(): return lax.all_to_all(value, axes, split_axis=0, concat_axis=0, tiled=True)  14.2 us
    all_to_all x1, starting transfers between devices, shards(): lax.all_to_all(slot_grad, DOM, split_axis=0, concat_axis=0, tiled=True)  8.63 us
  transfers between devices with their start and end apart: 14, of which 9 were waited for; matrix products, arithmetic and copies ran while one was open for 4% of the time, Pallas kernels for 0%

profile of v4, /device:TPU:1, one launch (start us, length us, event | category | flops | bytes accessed | tf_op | source)
XLA Modules:
  0.0 181.0 jit_solution(6460182810132562237)
XLA Ops:
  0.6 2.5 %take_rows.1 = bf16[1024,512]{1,0:T(8,128)(2,1)} custom-call(s32[8,128]{1,0:T(8,128)} %bitcast.39, s32[1,128]{1,0:T(1,128)} %bitcast.41, bf16[256,512]{1,0:T(8,128)(2,1)} %node_feats.1), custom_call_target="tpu_custom_call" | custom-call | flops 268435456 | bytes 2097152 | tf_op jit(solution)/shard_map/take_rows/pallas_call | solution.py:177
  3.2 20.6 %all-to-all-start = ((bf16[128,8,512]{2,1,0:T(8,128)(2,1)}), bf16[128,8,512]{2,1,0:T(8,128)(2,1)S(1)}, u32[]{:S(2)}, u32[]{:S(2)}) async-start(bf16[128,8,512]{2,1,0:T(8,128)(2,1)} %bitcast.33), calls=%async_computation | async-start | bytes 2097152 | tf_op jit(solution)/shard_map/all_to_all | solution.py:241
  23.8 1.4 select_reduce_fusion
  25.2 1.6 copy.20
  30.3 47.8 %all-to-all-done = bf16[128,8,512]{2,1,0:T(8,128)(2,1)S(1)} async-done(((bf16[128,8,512]{2,1,0:T(8,128)(2,1)}), bf16[128,8,512]{2,1,0:T(8,128)(2,1)S(1)}, u32[]{:S(2)}, u32[]{:S(2)}) %all-to-all-start) | async-done | bytes 1048608 | tf_op jit(solution)/shard_map/all_to_all | solution.py:241
  78.1 2.2 %layer.1 = (bf16[256,512]{1,0:T(8,128)(2,1)}, bf16[256,512]{1,0:T(8,128)(2,1)}, bf16[256,512]{1,0:T(8,128)(2,1)}, bf16[256,512]{1,0:T(8,128)(2,1)}, bf16[1024,512]{1,0:T(8,128)(2,1)}) custom-call(bf16[1024,512]{1,0:T(8,128)(2,1)S(1)} %bitcast.32, bf16[256,1024]{1,0:T(8,128)(2,1)S(1)} %copy.21.mixing, bf16[1024,256]{1,0:T(8,128)(2,1)S(1)} %convert_bitcast_fusion.mixing_rows, ...), custom_call_target="tpu_custom_call" | custom-call | flops 805306368 | bytes 6291456 | tf_op jit(solution)/shard_map/layer/pallas_call | solution.py:105
  80.3 8.6 %all-to-all-start.1 = ((bf16[128,8,512]{2,1,0:T(8,128)(2,1)}), bf16[128,8,512]{2,1,0:T(8,128)(2,1)S(1)}, u32[]{:S(2)}, u32[]{:S(2)}) async-start(bf16[128,8,512]{2,1,0:T(8,128)(2,1)} %bitcast.35), calls=%async_computation.1 | async-start | bytes 2097152 | tf_op jit(solution)/shard_map/all_to_all | solution.py:258
  89.4 2.8 %collective-permute-start = (bf16[256,512]{1,0:T(8,128)(2,1)S(1)}, bf16[256,512]{1,0:T(8,128)(2,1)S(1)}, u32[]{:S(2)}, u32[]{:S(2)}) collective-permute-start(bf16[256,512]{1,0:T(8,128)(2,1)S(1)} %dynamic-slice_convert_fusion), channel_id=1, source_target_pairs={{0,4},{4,0},{1,5},{5,1},{2,6},{6,2},{3,7},{7,3},{8,12},{12,8},{9,1... | collective-permute-start | bytes 786440 | tf_op jit(solution)/shard_map/ppermute | solution.py:17
  93.5 3.1 %collective-permute-start.1 = (bf16[64,512]{1,0:T(8,128)(2,1)S(1)}, bf16[64,512]{1,0:T(8,128)(2,1)S(1)}, u32[]{:S(2)}, u32[]{:S(2)}) collective-permute-start(bf16[64,512]{1,0:T(8,128)(2,1)S(1)} %get-tuple-element.21), channel_id=1, source_target_pairs={{0,1},{1,0},{2,3},{3,2},{4,5},{5,4},{6,7},{7,6},{8,9},{9,8},{10,11... | collective-permute-start | bytes 196616 | tf_op jit(solution)/shard_map/ppermute | solution.py:17
  96.6 4.4 %collective-permute-start.2 = (bf16[64,512]{1,0:T(8,128)(2,1)S(1)}, bf16[64,512]{1,0:T(8,128)(2,1)S(1)}, u32[]{:S(2)}, u32[]{:S(2)}) collective-permute-start(bf16[64,512]{1,0:T(8,128)(2,1)S(1)} %get-tuple-element.23), channel_id=1, source_target_pairs={{0,2},{1,3},{2,0},{3,1},{4,6},{5,7},{6,4},{7,5},{8,10},{9,11},{10,... | collective-permute-start | bytes 196616 | tf_op jit(solution)/shard_map/ppermute | solution.py:17
  100.9 2.1 %collective-permute-start.3 = (bf16[64,512]{1,0:T(8,128)(2,1)S(1)}, bf16[64,512]{1,0:T(8,128)(2,1)S(1)}, u32[]{:S(2)}, u32[]{:S(2)}) collective-permute-start(bf16[64,512]{1,0:T(8,128)(2,1)S(1)} %get-tuple-element.22), channel_id=1, source_target_pairs={{0,3},{1,2},{2,1},{3,0},{4,7},{5,6},{6,5},{7,4},{8,11},{9,10},{10,... | collective-permute-start | bytes 196616 | tf_op jit(solution)/shard_map/ppermute | solution.py:17
  103.4 4.1 %collective-permute-done.3 = bf16[64,512]{1,0:T(8,128)(2,1)S(1)} collective-permute-done((bf16[64,512]{1,0:T(8,128)(2,1)S(1)}, bf16[64,512]{1,0:T(8,128)(2,1)S(1)}, u32[]{:S(2)}, u32[]{:S(2)}) %collective-permute-start.3) | collective-permute-done | bytes 65568 | tf_op jit(solution)/shard_map/ppermute | solution.py:17
  107.5 2.9 %collective-permute-start.4 = (bf16[16,512]{1,0:T(8,128)(2,1)S(1)}, bf16[16,512]{1,0:T(8,128)(2,1)S(1)}, u32[]{:S(2)}, u32[]{:S(2)}) collective-permute-start(bf16[16,512]{1,0:T(8,128)(2,1)S(1)} %get-tuple-element.24), channel_id=1, source_target_pairs={{0,128},{128,0},{256,384},{384,256},{1,129},{129,1},{257,385},{385... | collective-permute-start | bytes 49160 | tf_op jit(solution)/shard_map/ppermute | solution.py:17
  110.4 4.7 %collective-permute-start.5 = (bf16[16,512]{1,0:T(8,128)(2,1)S(1)}, bf16[16,512]{1,0:T(8,128)(2,1)S(1)}, u32[]{:S(2)}, u32[]{:S(2)}) collective-permute-start(bf16[16,512]{1,0:T(8,128)(2,1)S(1)} %get-tuple-element.26), channel_id=1, source_target_pairs={{0,256},{128,384},{256,0},{384,128},{1,257},{129,385},{257,1},{385... | collective-permute-start | bytes 49160 | tf_op jit(solution)/shard_map/ppermute | solution.py:17
  115.1 2.0 %collective-permute-start.6 = (bf16[16,512]{1,0:T(8,128)(2,1)S(1)}, bf16[16,512]{1,0:T(8,128)(2,1)S(1)}, u32[]{:S(2)}, u32[]{:S(2)}) collective-permute-start(bf16[16,512]{1,0:T(8,128)(2,1)S(1)} %get-tuple-element.25), channel_id=1, source_target_pairs={{0,384},{128,256},{256,128},{384,0},{1,385},{129,257},{257,129},{3... | collective-permute-start | bytes 49160 | tf_op jit(solution)/shard_map/ppermute | solution.py:17
  117.2 4.1 %collective-permute-done.6 = bf16[16,512]{1,0:T(8,128)(2,1)S(1)} collective-permute-done((bf16[16,512]{1,0:T(8,128)(2,1)S(1)}, bf16[16,512]{1,0:T(8,128)(2,1)S(1)}, u32[]{:S(2)}, u32[]{:S(2)}) %collective-permute-start.6) | collective-permute-done | bytes 16416 | tf_op jit(solution)/shard_map/ppermute | solution.py:17
  121.3 6.9 %collective-permute-start.7 = (f32[16,512]{1,0:T(8,128)S(1)}, f32[16,512]{1,0:T(8,128)S(1)}, u32[]{:S(2)}, u32[]{:S(2)}) collective-permute-start(f32[16,512]{1,0:T(8,128)S(1)} %convert_add_fusion.2), channel_id=1, source_target_pairs={{0,32},{32,0},{64,96},{96,64},{1,33},{33,1},{65,97},{97,65},{2,34}... | collective-permute-start | bytes 98312 | tf_op jit(solution)/shard_map/ppermute | solution.py:17
  128.2 7.2 %collective-permute-start.8 = (f32[16,512]{1,0:T(8,128)S(1)}, f32[16,512]{1,0:T(8,128)S(1)}, u32[]{:S(2)}, u32[]{:S(2)}) collective-permute-start(f32[16,512]{1,0:T(8,128)S(1)} %convert_add_fusion.2), channel_id=1, source_target_pairs={{0,64},{32,96},{64,0},{96,32},{1,65},{33,97},{65,1},{97,33},{2,66}... | collective-permute-start | bytes 98312 | tf_op jit(solution)/shard_map/ppermute | solution.py:17
  135.4 2.1 %collective-permute-start.9 = (f32[16,512]{1,0:T(8,128)S(1)}, f32[16,512]{1,0:T(8,128)S(1)}, u32[]{:S(2)}, u32[]{:S(2)}) collective-permute-start(f32[16,512]{1,0:T(8,128)S(1)} %convert_add_fusion.2), channel_id=1, source_target_pairs={{0,96},{32,64},{64,32},{96,0},{1,97},{33,65},{65,33},{97,1},{2,98}... | collective-permute-start | bytes 98312 | tf_op jit(solution)/shard_map/ppermute | solution.py:17
  138.7 7.4 %collective-permute-done.8 = f32[16,512]{1,0:T(8,128)S(1)} collective-permute-done((f32[16,512]{1,0:T(8,128)S(1)}, f32[16,512]{1,0:T(8,128)S(1)}, u32[]{:S(2)}, u32[]{:S(2)}) %collective-permute-start.8) | collective-permute-done | bytes 32800 | tf_op jit(solution)/shard_map/ppermute | solution.py:17
  146.9 3.3 %all-to-all-start.2 = ((f32[4,16,512]{2,1,0:T(8,128)}), f32[4,16,512]{2,1,0:T(8,128)S(1)}, u32[]{:S(2)}, u32[]{:S(2)}) async-start(f32[4,16,512]{2,1,0:T(8,128)} %broadcast_in_dim.34), calls=%async_computation.2 | async-start | bytes 262144 | tf_op jit(solution)/shard_map/all_to_all | solution.py:38
  150.5 4.5 %all-to-all-done.2 = f32[4,16,512]{2,1,0:T(8,128)S(1)} async-done(((f32[4,16,512]{2,1,0:T(8,128)}), f32[4,16,512]{2,1,0:T(8,128)S(1)}, u32[]{:S(2)}, u32[]{:S(2)}) %all-to-all-start.2) | async-done | bytes 131104 | tf_op jit(solution)/shard_map/all_to_all | solution.py:38
  155.8 12.8 %all-to-all-start.3 = ((bf16[32,16,512]{2,1,0:T(8,128)(2,1)}), bf16[32,16,512]{2,1,0:T(8,128)(2,1)S(1)}, u32[]{:S(2)}, u32[]{:S(2)}) async-start(bf16[32,16,512]{2,1,0:T(8,128)(2,1)} %broadcast_in_dim.58), calls=%async_computation.3 | async-start | bytes 1048576 | tf_op jit(solution)/shard_map/all_to_all | solution.py:38
  170.1 9.8 %all-to-all-done.3 = bf16[32,16,512]{2,1,0:T(8,128)(2,1)S(1)} async-done(((bf16[32,16,512]{2,1,0:T(8,128)(2,1)}), bf16[32,16,512]{2,1,0:T(8,128)(2,1)S(1)}, u32[]{:S(2)}, u32[]{:S(2)}) %all-to-all-start.3) | async-done | bytes 524320 | tf_op jit(solution)/shard_map/all_to_all | solution.py:38
  (66 shorter events, 10.9 us)
Async XLA Ops:
  3.2 20.6 %copy-start.10 = (s32[1024,2]{0,1:T(2,128)S(1)}, s32[1024,2]{0,1:T(2,128)}, u32[]{:S(2)}) copy-start(s32[1024,2]{0,1:T(2,128)} %param.19) | copy-start | bytes 24580
  3.2 20.6 %copy-start.11 = (s32[1024,2]{0,1:T(2,128)S(1)}, s32[1024,2]{0,1:T(2,128)}, u32[]{:S(2)}) copy-start(s32[1024,2]{0,1:T(2,128)} %param.18) | copy-start | bytes 24580
  3.2 74.9 %all-to-all-start = ((bf16[128,8,512]{2,1,0:T(8,128)(2,1)}), bf16[128,8,512]{2,1,0:T(8,128)(2,1)S(1)}, u32[]{:S(2)}, u32[]{:S(2)}) async-start(bf16[128,8,512]{2,1,0:T(8,128)(2,1)} %bitcast.33), calls=%async_computation | async-start | bytes 2097152 | tf_op jit(solution)/shard_map/all_to_all | solution.py:241
  29.9 48.2 %copy-start = (bf16[512,512]{1,0:T(8,128)(2,1)S(1)}, bf16[512,512]{1,0:T(8,128)(2,1)}, u32[]{:S(2)}) copy-start(bf16[512,512]{1,0:T(8,128)(2,1)} %weight.1) | copy-start | bytes 1572868
  29.9 48.2 %copy-start.1 = (bf16[256,512]{1,0:T(8,128)(2,1)S(1)}, bf16[256,512]{1,0:T(8,128)(2,1)}, u32[]{:S(2)}) copy-start(bf16[256,512]{1,0:T(8,128)(2,1)} %cotangent.1) | copy-start | bytes 786436
  80.3 8.7 %copy-start.8 = (bf16[256,512]{1,0:T(8,128)(2,1)S(1)}, bf16[256,512]{1,0:T(8,128)(2,1)}, u32[]{:S(2)}) copy-start(bf16[256,512]{1,0:T(8,128)(2,1)} %get-tuple-element.17) | copy-start | bytes 786436
  80.3 8.7 %copy-start.9 = (bf16[256,512]{1,0:T(8,128)(2,1)S(1)}, bf16[256,512]{1,0:T(8,128)(2,1)}, u32[]{:S(2)}) copy-start(bf16[256,512]{1,0:T(8,128)(2,1)} %get-tuple-element.18) | copy-start | bytes 786436
  80.3 65.9 %all-to-all-start.1 = ((bf16[128,8,512]{2,1,0:T(8,128)(2,1)}), bf16[128,8,512]{2,1,0:T(8,128)(2,1)S(1)}, u32[]{:S(2)}, u32[]{:S(2)}) async-start(bf16[128,8,512]{2,1,0:T(8,128)(2,1)} %bitcast.35), calls=%async_computation.1 | async-start | bytes 2097152 | tf_op jit(solution)/shard_map/all_to_all | solution.py:258
  89.4 3.9 %collective-permute-start = (bf16[256,512]{1,0:T(8,128)(2,1)S(1)}, bf16[256,512]{1,0:T(8,128)(2,1)S(1)}, u32[]{:S(2)}, u32[]{:S(2)}) collective-permute-start(bf16[256,512]{1,0:T(8,128)(2,1)S(1)} %dynamic-slice_convert_fusion), channel_id=1, source_target_pairs={{0,4},{4,0},{1,5},{5,1},{2,6},{6,2},{3,7},{7,3},{8,12},{12,8},{9,1... | collective-permute-start | bytes 786440 | tf_op jit(solution)/shard_map/ppermute | solution.py:17
  93.4 56.8 %copy-start.12 = (s32[128,8]{0,1:T(8,128)S(1)}, s32[128,8]{0,1:T(8,128)}, u32[]{:S(2)}) copy-start(s32[128,8]{0,1:T(8,128)} %param.16) | copy-start | bytes 12292
  93.4 56.8 %copy-start.14 = (s32[128]{0:T(128)S(1)}, s32[128]{0:T(128)}, u32[]{:S(2)}) copy-start(s32[128]{0:T(128)} %param.17) | copy-start | bytes 1540
  93.5 9.6 %collective-permute-start.1 = (bf16[64,512]{1,0:T(8,128)(2,1)S(1)}, bf16[64,512]{1,0:T(8,128)(2,1)S(1)}, u32[]{:S(2)}, u32[]{:S(2)}) collective-permute-start(bf16[64,512]{1,0:T(8,128)(2,1)S(1)} %get-tuple-element.21), channel_id=1, source_target_pairs={{0,1},{1,0},{2,3},{3,2},{4,5},{5,4},{6,7},{7,6},{8,9},{9,8},{10,11... | collective-permute-start | bytes 196616 | tf_op jit(solution)/shard_map/ppermute | solution.py:17
  96.6 6.8 %collective-permute-start.2 = (bf16[64,512]{1,0:T(8,128)(2,1)S(1)}, bf16[64,512]{1,0:T(8,128)(2,1)S(1)}, u32[]{:S(2)}, u32[]{:S(2)}) collective-permute-start(bf16[64,512]{1,0:T(8,128)(2,1)S(1)} %get-tuple-element.23), channel_id=1, source_target_pairs={{0,2},{1,3},{2,0},{3,1},{4,6},{5,7},{6,4},{7,5},{8,10},{9,11},{10,... | collective-permute-start | bytes 196616 | tf_op jit(solution)/shard_map/ppermute | solution.py:17
  100.9 6.5 %collective-permute-start.3 = (bf16[64,512]{1,0:T(8,128)(2,1)S(1)}, bf16[64,512]{1,0:T(8,128)(2,1)S(1)}, u32[]{:S(2)}, u32[]{:S(2)}) collective-permute-start(bf16[64,512]{1,0:T(8,128)(2,1)S(1)} %get-tuple-element.22), channel_id=1, source_target_pairs={{0,3},{1,2},{2,1},{3,0},{4,7},{5,6},{6,5},{7,4},{8,11},{9,10},{10,... | collective-permute-start | bytes 196616 | tf_op jit(solution)/shard_map/ppermute | solution.py:17
  107.5 9.6 %collective-permute-start.4 = (bf16[16,512]{1,0:T(8,128)(2,1)S(1)}, bf16[16,512]{1,0:T(8,128)(2,1)S(1)}, u32[]{:S(2)}, u32[]{:S(2)}) collective-permute-start(bf16[16,512]{1,0:T(8,128)(2,1)S(1)} %get-tuple-element.24), channel_id=1, source_target_pairs={{0,128},{128,0},{256,384},{384,256},{1,129},{129,1},{257,385},{385... | collective-permute-start | bytes 49160 | tf_op jit(solution)/shard_map/ppermute | solution.py:17
  110.4 6.7 %collective-permute-start.5 = (bf16[16,512]{1,0:T(8,128)(2,1)S(1)}, bf16[16,512]{1,0:T(8,128)(2,1)S(1)}, u32[]{:S(2)}, u32[]{:S(2)}) collective-permute-start(bf16[16,512]{1,0:T(8,128)(2,1)S(1)} %get-tuple-element.26), channel_id=1, source_target_pairs={{0,256},{128,384},{256,0},{384,128},{1,257},{129,385},{257,1},{385... | collective-permute-start | bytes 49160 | tf_op jit(solution)/shard_map/ppermute | solution.py:17
  115.1 6.1 %collective-permute-start.6 = (bf16[16,512]{1,0:T(8,128)(2,1)S(1)}, bf16[16,512]{1,0:T(8,128)(2,1)S(1)}, u32[]{:S(2)}, u32[]{:S(2)}) collective-permute-start(bf16[16,512]{1,0:T(8,128)(2,1)S(1)} %get-tuple-element.25), channel_id=1, source_target_pairs={{0,384},{128,256},{256,128},{384,0},{1,385},{129,257},{257,129},{3... | collective-permute-start | bytes 49160 | tf_op jit(solution)/shard_map/ppermute | solution.py:17
  121.3 17.4 %collective-permute-start.7 = (f32[16,512]{1,0:T(8,128)S(1)}, f32[16,512]{1,0:T(8,128)S(1)}, u32[]{:S(2)}, u32[]{:S(2)}) collective-permute-start(f32[16,512]{1,0:T(8,128)S(1)} %convert_add_fusion.2), channel_id=1, source_target_pairs={{0,32},{32,0},{64,96},{96,64},{1,33},{33,1},{65,97},{97,65},{2,34}... | collective-permute-start | bytes 98312 | tf_op jit(solution)/shard_map/ppermute | solution.py:17
  128.2 17.9 %collective-permute-start.8 = (f32[16,512]{1,0:T(8,128)S(1)}, f32[16,512]{1,0:T(8,128)S(1)}, u32[]{:S(2)}, u32[]{:S(2)}) collective-permute-start(f32[16,512]{1,0:T(8,128)S(1)} %convert_add_fusion.2), channel_id=1, source_target_pairs={{0,64},{32,96},{64,0},{96,32},{1,65},{33,97},{65,1},{97,33},{2,66}... | collective-permute-start | bytes 98312 | tf_op jit(solution)/shard_map/ppermute | solution.py:17
  135.4 10.8 %collective-permute-start.9 = (f32[16,512]{1,0:T(8,128)S(1)}, f32[16,512]{1,0:T(8,128)S(1)}, u32[]{:S(2)}, u32[]{:S(2)}) collective-permute-start(f32[16,512]{1,0:T(8,128)S(1)} %convert_add_fusion.2), channel_id=1, source_target_pairs={{0,96},{32,64},{64,32},{96,0},{1,97},{33,65},{65,33},{97,1},{2,98}... | collective-permute-start | bytes 98312 | tf_op jit(solution)/shard_map/ppermute | solution.py:17
  146.9 8.1 %all-to-all-start.2 = ((f32[4,16,512]{2,1,0:T(8,128)}), f32[4,16,512]{2,1,0:T(8,128)S(1)}, u32[]{:S(2)}, u32[]{:S(2)}) async-start(f32[4,16,512]{2,1,0:T(8,128)} %broadcast_in_dim.34), calls=%async_computation.2 | async-start | bytes 262144 | tf_op jit(solution)/shard_map/all_to_all | solution.py:38
  150.2 18.5 %copy-start.6 = (bf16[2,2,128,128]{3,1,2,0:T(2,128)(2,1)S(1)}, bf16[2,2,128,128]{3,1,2,0:T(2,128)(2,1)}, u32[]{:S(2)}) copy-start(bf16[2,2,128,128]{3,1,2,0:T(2,128)(2,1)} %copy-done.5) | copy-start | bytes 393220
  150.2 18.5 %copy-start.7 = (bf16[256,512]{1,0:T(8,128)(2,1)S(1)}, bf16[256,512]{1,0:T(8,128)(2,1)}, u32[]{:S(2)}) copy-start(bf16[256,512]{1,0:T(8,128)(2,1)} %get-tuple-element.13) | copy-start | bytes 786436
  155.8 24.0 %all-to-all-start.3 = ((bf16[32,16,512]{2,1,0:T(8,128)(2,1)}), bf16[32,16,512]{2,1,0:T(8,128)(2,1)S(1)}, u32[]{:S(2)}, u32[]{:S(2)}) async-start(bf16[32,16,512]{2,1,0:T(8,128)(2,1)} %broadcast_in_dim.58), calls=%async_computation.3 | async-start | bytes 1048576 | tf_op jit(solution)/shard_map/all_to_all | solution.py:38
  (6 other events, 9.9 us)

commit v5 on v4

--- a/solution.py
+++ b/solution.py
@@ -17,19 +17,20 @@
     return lax.ppermute(value, axis, [(place, place ^ mask) for place in range(count)])
 
 
-def scatter_sum(part, axis):
+def scatter_sum(part, axis, crossing=jnp.bfloat16):
     count, here = lax.axis_size(axis), lax.axis_index(axis)
     rows = part.shape[0] // count
     total = lax.dynamic_slice_in_dim(part, here * rows, rows)
     for mask in range(1, count):
         block = lax.dynamic_slice_in_dim(part, (here ^ mask) * rows, rows)
-        total = total + from_peer(block.astype(jnp.bfloat16), axis, mask).astype(jnp.float32)
+        total = total + from_peer(block.astype(crossing), axis, mask).astype(jnp.float32)
     return total
 
 
 def quad_sum(value, axis):
-    near = value + from_peer(value, axis, 1)
-    return near + (from_peer(value, axis, 2) + from_peer(value, axis, 3))
+    value = value.astype(jnp.bfloat16)
+    near, middle, far = (from_peer(value, axis, mask).astype(jnp.float32) for mask in (1, 2, 3))
+    return (value.astype(jnp.float32) + near) + (middle + far)
 
 
 def to_all(value, axes):
@@ -42,7 +43,7 @@
 
 
 def sum_blocks(part):
-    mine = scatter_sum(scatter_sum(scatter_sum(part, "core"), "slab"), "y")
+    mine = scatter_sum(scatter_sum(scatter_sum(part, "core", jnp.float32), "slab"), "y")
     return quad_sum(mine, "z_hi")
 
 

time: 182 us -> 179 us (0.984)
  transfers between devices with their start and end apart: 14 -> 14, of which waited for: 9 -> 8; matrix products, arithmetic and copies ran while one was open for 4% -> 4% of each run, Pallas kernels for 0% -> 0%
where the time goes in v5:
time: 179 us; the launch traced here: 178 us
  starting transfers between devices  81.9 us (46%)
  waiting for transfers between devices  79.1 us (44%)
  local copies, waits for them, and re-layouts  4.89 us (3%)
  Pallas kernels  4.68 us (3%)
  other arithmetic  3.93 us (2%)
  matrix products  2.44 us (1%)
    all_to_all x1, waiting for transfers between devices, shards(): lax.all_to_all(outgoing, DOM, split_axis=0, concat_axis=0, tiled=True)  47.8 us
    ppermute x10, starting transfers between devices, from_peer(): lax.ppermute(value, axis, [(place, place ^ mask) for place in range(count)])  38.2 us
    all_to_all x1, starting transfers between devices, shards(): lax.all_to_all(outgoing, DOM, split_axis=0, concat_axis=0, tiled=True)  20.6 us
    ppermute x10, waiting for transfers between devices, from_peer(): lax.ppermute(value, axis, [(place, place ^ mask) for place in range(count)])  17.1 us
    all_to_all x2, starting transfers between devices, to_all(): return lax.all_to_all(value, axes, split_axis=0, concat_axis=0, tiled=True)  14.5 us
    all_to_all x2, waiting for transfers between devices, to_all(): return lax.all_to_all(value, axes, split_axis=0, concat_axis=0, tiled=True)  14.2 us
    all_to_all x1, starting transfers between devices, shards(): lax.all_to_all(slot_grad, DOM, split_axis=0, concat_axis=0, tiled=True)  8.63 us
  transfers between devices with their start and end apart: 14, of which 8 were waited for; matrix products, arithmetic and copies ran while one was open for 4% of the time, Pallas kernels for 0%

profile of v5, /device:TPU:1, one launch (start us, length us, event | category | flops | bytes accessed | tf_op | source)
XLA Modules:
  0.0 178.2 jit_solution(17338508153920910540)
XLA Ops:
  0.6 2.5 %take_rows.1 = bf16[1024,512]{1,0:T(8,128)(2,1)} custom-call(s32[8,128]{1,0:T(8,128)} %bitcast.39, s32[1,128]{1,0:T(1,128)} %bitcast.41, bf16[256,512]{1,0:T(8,128)(2,1)} %node_feats.1), custom_call_target="tpu_custom_call" | custom-call | flops 268435456 | bytes 2097152 | tf_op jit(solution)/shard_map/take_rows/pallas_call | solution.py:178
  3.2 20.6 %all-to-all-start = ((bf16[128,8,512]{2,1,0:T(8,128)(2,1)}), bf16[128,8,512]{2,1,0:T(8,128)(2,1)S(1)}, u32[]{:S(2)}, u32[]{:S(2)}) async-start(bf16[128,8,512]{2,1,0:T(8,128)(2,1)} %bitcast.33), calls=%async_computation | async-start | bytes 2097152 | tf_op jit(solution)/shard_map/all_to_all | solution.py:242
  25.2 1.6 copy.20
  30.3 47.8 %all-to-all-done = bf16[128,8,512]{2,1,0:T(8,128)(2,1)S(1)} async-done(((bf16[128,8,512]{2,1,0:T(8,128)(2,1)}), bf16[128,8,512]{2,1,0:T(8,128)(2,1)S(1)}, u32[]{:S(2)}, u32[]{:S(2)}) %all-to-all-start) | async-done | bytes 1048608 | tf_op jit(solution)/shard_map/all_to_all | solution.py:242
  78.1 2.2 %layer.1 = (bf16[256,512]{1,0:T(8,128)(2,1)}, bf16[256,512]{1,0:T(8,128)(2,1)}, bf16[256,512]{1,0:T(8,128)(2,1)}, bf16[256,512]{1,0:T(8,128)(2,1)}, bf16[1024,512]{1,0:T(8,128)(2,1)}) custom-call(bf16[1024,512]{1,0:T(8,128)(2,1)S(1)} %bitcast.32, bf16[256,1024]{1,0:T(8,128)(2,1)S(1)} %copy.21.mixing, bf16[1024,256]{1,0:T(8,128)(2,1)S(1)} %convert_bitcast_fusion.mixing_rows, ...), custom_call_target="tpu_custom_call" | custom-call | flops 805306368 | bytes 6291456 | tf_op jit(solution)/shard_map/layer/pallas_call | solution.py:106
  80.3 8.6 %all-to-all-start.1 = ((bf16[128,8,512]{2,1,0:T(8,128)(2,1)}), bf16[128,8,512]{2,1,0:T(8,128)(2,1)S(1)}, u32[]{:S(2)}, u32[]{:S(2)}) async-start(bf16[128,8,512]{2,1,0:T(8,128)(2,1)} %bitcast.35), calls=%async_computation.1 | async-start | bytes 2097152 | tf_op jit(solution)/shard_map/all_to_all | solution.py:259
  89.4 2.8 %collective-permute-start = (f32[256,512]{1,0:T(8,128)S(1)}, f32[256,512]{1,0:T(8,128)S(1)}, u32[]{:S(2)}, u32[]{:S(2)}) collective-permute-start(f32[256,512]{1,0:T(8,128)S(1)} %constant_dynamic-slice_fusion), channel_id=1, source_target_pairs={{0,4},{4,0},{1,5},{5,1},{2,6},{6,2},{3,7},{7,3},{8,12},{12,8},{9,1... | collective-permute-start | bytes 1572872 | tf_op jit(solution)/shard_map/ppermute | solution.py:17
  92.2 1.5 collective-permute-done
  93.8 3.1 %collective-permute-start.1 = (bf16[64,512]{1,0:T(8,128)(2,1)S(1)}, bf16[64,512]{1,0:T(8,128)(2,1)S(1)}, u32[]{:S(2)}, u32[]{:S(2)}) collective-permute-start(bf16[64,512]{1,0:T(8,128)(2,1)S(1)} %get-tuple-element.21), channel_id=1, source_target_pairs={{0,1},{1,0},{2,3},{3,2},{4,5},{5,4},{6,7},{7,6},{8,9},{9,8},{10,11... | collective-permute-start | bytes 196616 | tf_op jit(solution)/shard_map/ppermute | solution.py:17
  97.0 4.4 %collective-permute-start.2 = (bf16[64,512]{1,0:T(8,128)(2,1)S(1)}, bf16[64,512]{1,0:T(8,128)(2,1)S(1)}, u32[]{:S(2)}, u32[]{:S(2)}) collective-permute-start(bf16[64,512]{1,0:T(8,128)(2,1)S(1)} %get-tuple-element.23), channel_id=1, source_target_pairs={{0,2},{1,3},{2,0},{3,1},{4,6},{5,7},{6,4},{7,5},{8,10},{9,11},{10,... | collective-permute-start | bytes 196616 | tf_op jit(solution)/shard_map/ppermute | solution.py:17
  101.3 2.1 %collective-permute-start.3 = (bf16[64,512]{1,0:T(8,128)(2,1)S(1)}, bf16[64,512]{1,0:T(8,128)(2,1)S(1)}, u32[]{:S(2)}, u32[]{:S(2)}) collective-permute-start(bf16[64,512]{1,0:T(8,128)(2,1)S(1)} %get-tuple-element.22), channel_id=1, source_target_pairs={{0,3},{1,2},{2,1},{3,0},{4,7},{5,6},{6,5},{7,4},{8,11},{9,10},{10,... | collective-permute-start | bytes 196616 | tf_op jit(solution)/shard_map/ppermute | solution.py:17
  103.8 4.1 %collective-permute-done.3 = bf16[64,512]{1,0:T(8,128)(2,1)S(1)} collective-permute-done((bf16[64,512]{1,0:T(8,128)(2,1)S(1)}, bf16[64,512]{1,0:T(8,128)(2,1)S(1)}, u32[]{:S(2)}, u32[]{:S(2)}) %collective-permute-start.3) | collective-permute-done | bytes 65568 | tf_op jit(solution)/shard_map/ppermute | solution.py:17
  107.9 2.9 %collective-permute-start.4 = (bf16[16,512]{1,0:T(8,128)(2,1)S(1)}, bf16[16,512]{1,0:T(8,128)(2,1)S(1)}, u32[]{:S(2)}, u32[]{:S(2)}) collective-permute-start(bf16[16,512]{1,0:T(8,128)(2,1)S(1)} %get-tuple-element.24), channel_id=1, source_target_pairs={{0,128},{128,0},{256,384},{384,256},{1,129},{129,1},{257,385},{385... | collective-permute-start | bytes 49160 | tf_op jit(solution)/shard_map/ppermute | solution.py:17
  110.8 4.7 %collective-permute-start.5 = (bf16[16,512]{1,0:T(8,128)(2,1)S(1)}, bf16[16,512]{1,0:T(8,128)(2,1)S(1)}, u32[]{:S(2)}, u32[]{:S(2)}) collective-permute-start(bf16[16,512]{1,0:T(8,128)(2,1)S(1)} %get-tuple-element.26), channel_id=1, source_target_pairs={{0,256},{128,384},{256,0},{384,128},{1,257},{129,385},{257,1},{385... | collective-permute-start | bytes 49160 | tf_op jit(solution)/shard_map/ppermute | solution.py:17
  115.5 2.0 %collective-permute-start.6 = (bf16[16,512]{1,0:T(8,128)(2,1)S(1)}, bf16[16,512]{1,0:T(8,128)(2,1)S(1)}, u32[]{:S(2)}, u32[]{:S(2)}) collective-permute-start(bf16[16,512]{1,0:T(8,128)(2,1)S(1)} %get-tuple-element.25), channel_id=1, source_target_pairs={{0,384},{128,256},{256,128},{384,0},{1,385},{129,257},{257,129},{3... | collective-permute-start | bytes 49160 | tf_op jit(solution)/shard_map/ppermute | solution.py:17
  117.5 4.0 %collective-permute-done.6 = bf16[16,512]{1,0:T(8,128)(2,1)S(1)} collective-permute-done((bf16[16,512]{1,0:T(8,128)(2,1)S(1)}, bf16[16,512]{1,0:T(8,128)(2,1)S(1)}, u32[]{:S(2)}, u32[]{:S(2)}) %collective-permute-start.6) | collective-permute-done | bytes 16416 | tf_op jit(solution)/shard_map/ppermute | solution.py:17
  121.6 7.1 %collective-permute-start.7 = (bf16[16,512]{1,0:T(8,128)(2,1)S(1)}, bf16[16,512]{1,0:T(8,128)(2,1)S(1)}, u32[]{:S(2)}, u32[]{:S(2)}) collective-permute-start(bf16[16,512]{1,0:T(8,128)(2,1)S(1)} %add_convert_fusion), channel_id=1, source_target_pairs={{0,32},{32,0},{64,96},{96,64},{1,33},{33,1},{65,97},{97,65},{2,34}... | collective-permute-start | bytes 49160 | tf_op jit(solution)/shard_map/ppermute | solution.py:17
  128.7 7.1 %collective-permute-start.8 = (bf16[16,512]{1,0:T(8,128)(2,1)S(1)}, bf16[16,512]{1,0:T(8,128)(2,1)S(1)}, u32[]{:S(2)}, u32[]{:S(2)}) collective-permute-start(bf16[16,512]{1,0:T(8,128)(2,1)S(1)} %add_convert_fusion), channel_id=1, source_target_pairs={{0,64},{32,96},{64,0},{96,32},{1,65},{33,97},{65,1},{97,33},{2,66}... | collective-permute-start | bytes 49160 | tf_op jit(solution)/shard_map/ppermute | solution.py:17
  135.8 2.0 %collective-permute-start.9 = (bf16[16,512]{1,0:T(8,128)(2,1)S(1)}, bf16[16,512]{1,0:T(8,128)(2,1)S(1)}, u32[]{:S(2)}, u32[]{:S(2)}) collective-permute-start(bf16[16,512]{1,0:T(8,128)(2,1)S(1)} %add_convert_fusion), channel_id=1, source_target_pairs={{0,96},{32,64},{64,32},{96,0},{1,97},{33,65},{65,33},{97,1},{2,98}... | collective-permute-start | bytes 49160 | tf_op jit(solution)/shard_map/ppermute | solution.py:17
  137.8 7.2 %collective-permute-done.8 = bf16[16,512]{1,0:T(8,128)(2,1)S(1)} collective-permute-done((bf16[16,512]{1,0:T(8,128)(2,1)S(1)}, bf16[16,512]{1,0:T(8,128)(2,1)S(1)}, u32[]{:S(2)}, u32[]{:S(2)}) %collective-permute-start.8) | collective-permute-done | bytes 16416 | tf_op jit(solution)/shard_map/ppermute | solution.py:17
  145.7 3.3 %all-to-all-start.2 = ((f32[4,16,512]{2,1,0:T(8,128)}), f32[4,16,512]{2,1,0:T(8,128)S(1)}, u32[]{:S(2)}, u32[]{:S(2)}) async-start(f32[4,16,512]{2,1,0:T(8,128)} %broadcast_in_dim.34), calls=%async_computation.2 | async-start | bytes 262144 | tf_op jit(solution)/shard_map/all_to_all | solution.py:39
  149.3 4.5 %all-to-all-done.2 = f32[4,16,512]{2,1,0:T(8,128)S(1)} async-done(((f32[4,16,512]{2,1,0:T(8,128)}), f32[4,16,512]{2,1,0:T(8,128)S(1)}, u32[]{:S(2)}, u32[]{:S(2)}) %all-to-all-start.2) | async-done | bytes 131104 | tf_op jit(solution)/shard_map/all_to_all | solution.py:39
  154.6 11.2 %all-to-all-start.3 = ((bf16[32,16,512]{2,1,0:T(8,128)(2,1)}), bf16[32,16,512]{2,1,0:T(8,128)(2,1)S(1)}, u32[]{:S(2)}, u32[]{:S(2)}) async-start(bf16[32,16,512]{2,1,0:T(8,128)(2,1)} %broadcast_in_dim.58), calls=%async_computation.3 | async-start | bytes 1048576 | tf_op jit(solution)/shard_map/all_to_all | solution.py:39
  167.3 9.8 %all-to-all-done.3 = bf16[32,16,512]{2,1,0:T(8,128)(2,1)S(1)} async-done(((bf16[32,16,512]{2,1,0:T(8,128)(2,1)}), bf16[32,16,512]{2,1,0:T(8,128)(2,1)S(1)}, u32[]{:S(2)}, u32[]{:S(2)}) %all-to-all-start.3) | async-done | bytes 524320 | tf_op jit(solution)/shard_map/all_to_all | solution.py:39
  (66 shorter events, 10.0 us)
Async XLA Ops:
  3.2 20.6 %copy-start.10 = (s32[1024,2]{0,1:T(2,128)S(1)}, s32[1024,2]{0,1:T(2,128)}, u32[]{:S(2)}) copy-start(s32[1024,2]{0,1:T(2,128)} %param.19) | copy-start | bytes 24580
  3.2 20.6 %copy-start.11 = (s32[1024,2]{0,1:T(2,128)S(1)}, s32[1024,2]{0,1:T(2,128)}, u32[]{:S(2)}) copy-start(s32[1024,2]{0,1:T(2,128)} %param.18) | copy-start | bytes 24580
  3.2 74.9 %all-to-all-start = ((bf16[128,8,512]{2,1,0:T(8,128)(2,1)}), bf16[128,8,512]{2,1,0:T(8,128)(2,1)S(1)}, u32[]{:S(2)}, u32[]{:S(2)}) async-start(bf16[128,8,512]{2,1,0:T(8,128)(2,1)} %bitcast.33), calls=%async_computation | async-start | bytes 2097152 | tf_op jit(solution)/shard_map/all_to_all | solution.py:242
  29.9 48.2 %copy-start = (bf16[512,512]{1,0:T(8,128)(2,1)S(1)}, bf16[512,512]{1,0:T(8,128)(2,1)}, u32[]{:S(2)}) copy-start(bf16[512,512]{1,0:T(8,128)(2,1)} %weight.1) | copy-start | bytes 1572868
  29.9 48.2 %copy-start.1 = (bf16[256,512]{1,0:T(8,128)(2,1)S(1)}, bf16[256,512]{1,0:T(8,128)(2,1)}, u32[]{:S(2)}) copy-start(bf16[256,512]{1,0:T(8,128)(2,1)} %cotangent.1) | copy-start | bytes 786436
  80.3 8.7 %copy-start.8 = (bf16[256,512]{1,0:T(8,128)(2,1)S(1)}, bf16[256,512]{1,0:T(8,128)(2,1)}, u32[]{:S(2)}) copy-start(bf16[256,512]{1,0:T(8,128)(2,1)} %get-tuple-element.17) | copy-start | bytes 786436
  80.3 8.7 %copy-start.9 = (bf16[256,512]{1,0:T(8,128)(2,1)S(1)}, bf16[256,512]{1,0:T(8,128)(2,1)}, u32[]{:S(2)}) copy-start(bf16[256,512]{1,0:T(8,128)(2,1)} %get-tuple-element.18) | copy-start | bytes 786436
  80.3 64.7 %all-to-all-start.1 = ((bf16[128,8,512]{2,1,0:T(8,128)(2,1)}), bf16[128,8,512]{2,1,0:T(8,128)(2,1)S(1)}, u32[]{:S(2)}, u32[]{:S(2)}) async-start(bf16[128,8,512]{2,1,0:T(8,128)(2,1)} %bitcast.35), calls=%async_computation.1 | async-start | bytes 2097152 | tf_op jit(solution)/shard_map/all_to_all | solution.py:259
  89.4 4.3 %collective-permute-start = (f32[256,512]{1,0:T(8,128)S(1)}, f32[256,512]{1,0:T(8,128)S(1)}, u32[]{:S(2)}, u32[]{:S(2)}) collective-permute-start(f32[256,512]{1,0:T(8,128)S(1)} %constant_dynamic-slice_fusion), channel_id=1, source_target_pairs={{0,4},{4,0},{1,5},{5,1},{2,6},{6,2},{3,7},{7,3},{8,12},{12,8},{9,1... | collective-permute-start | bytes 1572872 | tf_op jit(solution)/shard_map/ppermute | solution.py:17
  93.8 55.3 %copy-start.12 = (s32[128,8]{0,1:T(8,128)S(1)}, s32[128,8]{0,1:T(8,128)}, u32[]{:S(2)}) copy-start(s32[128,8]{0,1:T(8,128)} %param.16) | copy-start | bytes 12292
  93.8 55.3 %copy-start.14 = (s32[128]{0:T(128)S(1)}, s32[128]{0:T(128)}, u32[]{:S(2)}) copy-start(s32[128]{0:T(128)} %param.17) | copy-start | bytes 1540
  93.8 9.6 %collective-permute-start.1 = (bf16[64,512]{1,0:T(8,128)(2,1)S(1)}, bf16[64,512]{1,0:T(8,128)(2,1)S(1)}, u32[]{:S(2)}, u32[]{:S(2)}) collective-permute-start(bf16[64,512]{1,0:T(8,128)(2,1)S(1)} %get-tuple-element.21), channel_id=1, source_target_pairs={{0,1},{1,0},{2,3},{3,2},{4,5},{5,4},{6,7},{7,6},{8,9},{9,8},{10,11... | collective-permute-start | bytes 196616 | tf_op jit(solution)/shard_map/ppermute | solution.py:17
  97.0 6.8 %collective-permute-start.2 = (bf16[64,512]{1,0:T(8,128)(2,1)S(1)}, bf16[64,512]{1,0:T(8,128)(2,1)S(1)}, u32[]{:S(2)}, u32[]{:S(2)}) collective-permute-start(bf16[64,512]{1,0:T(8,128)(2,1)S(1)} %get-tuple-element.23), channel_id=1, source_target_pairs={{0,2},{1,3},{2,0},{3,1},{4,6},{5,7},{6,4},{7,5},{8,10},{9,11},{10,... | collective-permute-start | bytes 196616 | tf_op jit(solution)/shard_map/ppermute | solution.py:17
  101.3 6.5 %collective-permute-start.3 = (bf16[64,512]{1,0:T(8,128)(2,1)S(1)}, bf16[64,512]{1,0:T(8,128)(2,1)S(1)}, u32[]{:S(2)}, u32[]{:S(2)}) collective-permute-start(bf16[64,512]{1,0:T(8,128)(2,1)S(1)} %get-tuple-element.22), channel_id=1, source_target_pairs={{0,3},{1,2},{2,1},{3,0},{4,7},{5,6},{6,5},{7,4},{8,11},{9,10},{10,... | collective-permute-start | bytes 196616 | tf_op jit(solution)/shard_map/ppermute | solution.py:17
  107.9 9.6 %collective-permute-start.4 = (bf16[16,512]{1,0:T(8,128)(2,1)S(1)}, bf16[16,512]{1,0:T(8,128)(2,1)S(1)}, u32[]{:S(2)}, u32[]{:S(2)}) collective-permute-start(bf16[16,512]{1,0:T(8,128)(2,1)S(1)} %get-tuple-element.24), channel_id=1, source_target_pairs={{0,128},{128,0},{256,384},{384,256},{1,129},{129,1},{257,385},{385... | collective-permute-start | bytes 49160 | tf_op jit(solution)/shard_map/ppermute | solution.py:17
  110.8 6.7 %collective-permute-start.5 = (bf16[16,512]{1,0:T(8,128)(2,1)S(1)}, bf16[16,512]{1,0:T(8,128)(2,1)S(1)}, u32[]{:S(2)}, u32[]{:S(2)}) collective-permute-start(bf16[16,512]{1,0:T(8,128)(2,1)S(1)} %get-tuple-element.26), channel_id=1, source_target_pairs={{0,256},{128,384},{256,0},{384,128},{1,257},{129,385},{257,1},{385... | collective-permute-start | bytes 49160 | tf_op jit(solution)/shard_map/ppermute | solution.py:17
  115.5 6.0 %collective-permute-start.6 = (bf16[16,512]{1,0:T(8,128)(2,1)S(1)}, bf16[16,512]{1,0:T(8,128)(2,1)S(1)}, u32[]{:S(2)}, u32[]{:S(2)}) collective-permute-start(bf16[16,512]{1,0:T(8,128)(2,1)S(1)} %get-tuple-element.25), channel_id=1, source_target_pairs={{0,384},{128,256},{256,128},{384,0},{1,385},{129,257},{257,129},{3... | collective-permute-start | bytes 49160 | tf_op jit(solution)/shard_map/ppermute | solution.py:17
  121.6 16.2 %collective-permute-start.7 = (bf16[16,512]{1,0:T(8,128)(2,1)S(1)}, bf16[16,512]{1,0:T(8,128)(2,1)S(1)}, u32[]{:S(2)}, u32[]{:S(2)}) collective-permute-start(bf16[16,512]{1,0:T(8,128)(2,1)S(1)} %add_convert_fusion), channel_id=1, source_target_pairs={{0,32},{32,0},{64,96},{96,64},{1,33},{33,1},{65,97},{97,65},{2,34}... | collective-permute-start | bytes 49160 | tf_op jit(solution)/shard_map/ppermute | solution.py:17
  128.7 16.3 %collective-permute-start.8 = (bf16[16,512]{1,0:T(8,128)(2,1)S(1)}, bf16[16,512]{1,0:T(8,128)(2,1)S(1)}, u32[]{:S(2)}, u32[]{:S(2)}) collective-permute-start(bf16[16,512]{1,0:T(8,128)(2,1)S(1)} %add_convert_fusion), channel_id=1, source_target_pairs={{0,64},{32,96},{64,0},{96,32},{1,65},{33,97},{65,1},{97,33},{2,66}... | collective-permute-start | bytes 49160 | tf_op jit(solution)/shard_map/ppermute | solution.py:17
  135.8 9.2 %collective-permute-start.9 = (bf16[16,512]{1,0:T(8,128)(2,1)S(1)}, bf16[16,512]{1,0:T(8,128)(2,1)S(1)}, u32[]{:S(2)}, u32[]{:S(2)}) collective-permute-start(bf16[16,512]{1,0:T(8,128)(2,1)S(1)} %add_convert_fusion), channel_id=1, source_target_pairs={{0,96},{32,64},{64,32},{96,0},{1,97},{33,65},{65,33},{97,1},{2,98}... | collective-permute-start | bytes 49160 | tf_op jit(solution)/shard_map/ppermute | solution.py:17
  145.7 8.1 %all-to-all-start.2 = ((f32[4,16,512]{2,1,0:T(8,128)}), f32[4,16,512]{2,1,0:T(8,128)S(1)}, u32[]{:S(2)}, u32[]{:S(2)}) async-start(f32[4,16,512]{2,1,0:T(8,128)} %broadcast_in_dim.34), calls=%async_computation.2 | async-start | bytes 262144 | tf_op jit(solution)/shard_map/all_to_all | solution.py:39
  149.0 16.8 %copy-start.6 = (bf16[2,2,128,128]{3,1,2,0:T(2,128)(2,1)S(1)}, bf16[2,2,128,128]{3,1,2,0:T(2,128)(2,1)}, u32[]{:S(2)}) copy-start(bf16[2,2,128,128]{3,1,2,0:T(2,128)(2,1)} %copy-done.5) | copy-start | bytes 393220
  149.0 16.8 %copy-start.7 = (bf16[256,512]{1,0:T(8,128)(2,1)S(1)}, bf16[256,512]{1,0:T(8,128)(2,1)}, u32[]{:S(2)}) copy-start(bf16[256,512]{1,0:T(8,128)(2,1)} %get-tuple-element.13) | copy-start | bytes 786436
  154.6 22.4 %all-to-all-start.3 = ((bf16[32,16,512]{2,1,0:T(8,128)(2,1)}), bf16[32,16,512]{2,1,0:T(8,128)(2,1)S(1)}, u32[]{:S(2)}, u32[]{:S(2)}) async-start(bf16[32,16,512]{2,1,0:T(8,128)(2,1)} %broadcast_in_dim.58), calls=%async_computation.3 | async-start | bytes 1048576 | tf_op jit(solution)/shard_map/all_to_all | solution.py:39
  (6 other events, 9.9 us)

commit v6 on v5

--- a/solution.py
+++ b/solution.py
@@ -43,12 +43,12 @@
 
 
 def sum_blocks(part):
-    mine = scatter_sum(scatter_sum(scatter_sum(part, "core", jnp.float32), "slab"), "y")
+    mine = scatter_sum(scatter_sum(scatter_sum(part, "core", jnp.float32), "slab"), "y", jnp.float32)
     return quad_sum(mine, "z_hi")
 
 
 def finish_sum(mine, scale):
-    mine = (jnp.sum(to_all(mine, "z_lo"), axis=0) * scale).astype(jnp.bfloat16)
+    mine = (jnp.sum(to_all(mine.astype(jnp.bfloat16), "z_lo").astype(jnp.float32), axis=0) * scale).astype(jnp.bfloat16)
     return to_all(mine, PLANE).reshape(-1, mine.shape[-1]).astype(jnp.float32)
 
 

time: 179 us -> 179 us (level)
  transfers between devices with their start and end apart: 14 -> 14, of which waited for: 8 -> 9; matrix products, arithmetic and copies ran while one was open for 4% -> 4% of each run, Pallas kernels for 0% -> 0%
where the time goes in v6:
time: 179 us; the launch traced here: 178 us
  starting transfers between devices  81.8 us (46%)
  waiting for transfers between devices  79 us (44%)
  local copies, waits for them, and re-layouts  4.86 us (3%)
  Pallas kernels  4.68 us (3%)
  other arithmetic  3.94 us (2%)
  matrix products  2.44 us (1%)
    all_to_all x1, waiting for transfers between devices, shards(): lax.all_to_all(outgoing, DOM, split_axis=0, concat_axis=0, tiled=True)  47.8 us
    ppermute x10, starting transfers between devices, from_peer(): lax.ppermute(value, axis, [(place, place ^ mask) for place in range(count)])  38.2 us
    all_to_all x1, starting transfers between devices, shards(): lax.all_to_all(outgoing, DOM, split_axis=0, concat_axis=0, tiled=True)  20.6 us
    ppermute x10, waiting for transfers between devices, from_peer(): lax.ppermute(value, axis, [(place, place ^ mask) for place in range(count)])  17.1 us
    all_to_all x2, starting transfers between devices, to_all(): return lax.all_to_all(value, axes, split_axis=0, concat_axis=0, tiled=True)  14.5 us
    all_to_all x2, waiting for transfers between devices, to_all(): return lax.all_to_all(value, axes, split_axis=0, concat_axis=0, tiled=True)  14.1 us
    all_to_all x1, starting transfers between devices, shards(): lax.all_to_all(slot_grad, DOM, split_axis=0, concat_axis=0, tiled=True)  8.63 us
  transfers between devices with their start and end apart: 14, of which 9 were waited for; matrix products, arithmetic and copies ran while one was open for 4% of the time, Pallas kernels for 0%

profile of v6, /device:TPU:1, one launch (start us, length us, event | category | flops | bytes accessed | tf_op | source)
XLA Modules:
  0.0 178.0 jit_solution(8579326475464967003)
XLA Ops:
  0.6 2.5 %take_rows.1 = bf16[1024,512]{1,0:T(8,128)(2,1)} custom-call(s32[8,128]{1,0:T(8,128)} %bitcast.39, s32[1,128]{1,0:T(1,128)} %bitcast.41, bf16[256,512]{1,0:T(8,128)(2,1)} %node_feats.1), custom_call_target="tpu_custom_call" | custom-call | flops 268435456 | bytes 2097152 | tf_op jit(solution)/shard_map/take_rows/pallas_call | solution.py:178
  3.2 20.6 %all-to-all-start = ((bf16[128,8,512]{2,1,0:T(8,128)(2,1)}), bf16[128,8,512]{2,1,0:T(8,128)(2,1)S(1)}, u32[]{:S(2)}, u32[]{:S(2)}) async-start(bf16[128,8,512]{2,1,0:T(8,128)(2,1)} %bitcast.33), calls=%async_computation | async-start | bytes 2097152 | tf_op jit(solution)/shard_map/all_to_all | solution.py:242
  25.2 1.6 copy.20
  30.3 47.8 %all-to-all-done = bf16[128,8,512]{2,1,0:T(8,128)(2,1)S(1)} async-done(((bf16[128,8,512]{2,1,0:T(8,128)(2,1)}), bf16[128,8,512]{2,1,0:T(8,128)(2,1)S(1)}, u32[]{:S(2)}, u32[]{:S(2)}) %all-to-all-start) | async-done | bytes 1048608 | tf_op jit(solution)/shard_map/all_to_all | solution.py:242
  78.1 2.2 %layer.1 = (bf16[256,512]{1,0:T(8,128)(2,1)}, bf16[256,512]{1,0:T(8,128)(2,1)}, bf16[256,512]{1,0:T(8,128)(2,1)}, bf16[256,512]{1,0:T(8,128)(2,1)}, bf16[1024,512]{1,0:T(8,128)(2,1)}) custom-call(bf16[1024,512]{1,0:T(8,128)(2,1)S(1)} %bitcast.32, bf16[256,1024]{1,0:T(8,128)(2,1)S(1)} %copy.21.mixing, bf16[1024,256]{1,0:T(8,128)(2,1)S(1)} %convert_bitcast_fusion.mixing_rows, ...), custom_call_target="tpu_custom_call" | custom-call | flops 805306368 | bytes 6291456 | tf_op jit(solution)/shard_map/layer/pallas_call | solution.py:106
  80.3 8.6 %all-to-all-start.1 = ((bf16[128,8,512]{2,1,0:T(8,128)(2,1)}), bf16[128,8,512]{2,1,0:T(8,128)(2,1)S(1)}, u32[]{:S(2)}, u32[]{:S(2)}) async-start(bf16[128,8,512]{2,1,0:T(8,128)(2,1)} %bitcast.35), calls=%async_computation.1 | async-start | bytes 2097152 | tf_op jit(solution)/shard_map/all_to_all | solution.py:259
  89.4 2.8 %collective-permute-start = (f32[256,512]{1,0:T(8,128)S(1)}, f32[256,512]{1,0:T(8,128)S(1)}, u32[]{:S(2)}, u32[]{:S(2)}) collective-permute-start(f32[256,512]{1,0:T(8,128)S(1)} %constant_dynamic-slice_fusion.2), channel_id=1, source_target_pairs={{0,4},{4,0},{1,5},{5,1},{2,6},{6,2},{3,7},{7,3},{8,12},{12,8},{9,1... | collective-permute-start | bytes 1572872 | tf_op jit(solution)/shard_map/ppermute | solution.py:17
  92.2 1.5 collective-permute-done
  93.8 3.1 %collective-permute-start.1 = (bf16[64,512]{1,0:T(8,128)(2,1)S(1)}, bf16[64,512]{1,0:T(8,128)(2,1)S(1)}, u32[]{:S(2)}, u32[]{:S(2)}) collective-permute-start(bf16[64,512]{1,0:T(8,128)(2,1)S(1)} %get-tuple-element.21), channel_id=1, source_target_pairs={{0,1},{1,0},{2,3},{3,2},{4,5},{5,4},{6,7},{7,6},{8,9},{9,8},{10,11... | collective-permute-start | bytes 196616 | tf_op jit(solution)/shard_map/ppermute | solution.py:17
  97.0 4.4 %collective-permute-start.2 = (bf16[64,512]{1,0:T(8,128)(2,1)S(1)}, bf16[64,512]{1,0:T(8,128)(2,1)S(1)}, u32[]{:S(2)}, u32[]{:S(2)}) collective-permute-start(bf16[64,512]{1,0:T(8,128)(2,1)S(1)} %get-tuple-element.23), channel_id=1, source_target_pairs={{0,2},{1,3},{2,0},{3,1},{4,6},{5,7},{6,4},{7,5},{8,10},{9,11},{10,... | collective-permute-start | bytes 196616 | tf_op jit(solution)/shard_map/ppermute | solution.py:17
  101.3 2.1 %collective-permute-start.3 = (bf16[64,512]{1,0:T(8,128)(2,1)S(1)}, bf16[64,512]{1,0:T(8,128)(2,1)S(1)}, u32[]{:S(2)}, u32[]{:S(2)}) collective-permute-start(bf16[64,512]{1,0:T(8,128)(2,1)S(1)} %get-tuple-element.22), channel_id=1, source_target_pairs={{0,3},{1,2},{2,1},{3,0},{4,7},{5,6},{6,5},{7,4},{8,11},{9,10},{10,... | collective-permute-start | bytes 196616 | tf_op jit(solution)/shard_map/ppermute | solution.py:17
  103.8 4.1 %collective-permute-done.3 = bf16[64,512]{1,0:T(8,128)(2,1)S(1)} collective-permute-done((bf16[64,512]{1,0:T(8,128)(2,1)S(1)}, bf16[64,512]{1,0:T(8,128)(2,1)S(1)}, u32[]{:S(2)}, u32[]{:S(2)}) %collective-permute-start.3) | collective-permute-done | bytes 65568 | tf_op jit(solution)/shard_map/ppermute | solution.py:17
  107.9 2.9 %collective-permute-start.4 = (f32[16,512]{1,0:T(8,128)S(1)}, f32[16,512]{1,0:T(8,128)S(1)}, u32[]{:S(2)}, u32[]{:S(2)}) collective-permute-start(f32[16,512]{1,0:T(8,128)S(1)} %get-tuple-element.24), channel_id=1, source_target_pairs={{0,128},{128,0},{256,384},{384,256},{1,129},{129,1},{257,385},{385... | collective-permute-start | bytes 98312 | tf_op jit(solution)/shard_map/ppermute | solution.py:17
  110.8 4.7 %collective-permute-start.5 = (f32[16,512]{1,0:T(8,128)S(1)}, f32[16,512]{1,0:T(8,128)S(1)}, u32[]{:S(2)}, u32[]{:S(2)}) collective-permute-start(f32[16,512]{1,0:T(8,128)S(1)} %get-tuple-element.26), channel_id=1, source_target_pairs={{0,256},{128,384},{256,0},{384,128},{1,257},{129,385},{257,1},{385... | collective-permute-start | bytes 98312 | tf_op jit(solution)/shard_map/ppermute | solution.py:17
  115.5 2.0 %collective-permute-start.6 = (f32[16,512]{1,0:T(8,128)S(1)}, f32[16,512]{1,0:T(8,128)S(1)}, u32[]{:S(2)}, u32[]{:S(2)}) collective-permute-start(f32[16,512]{1,0:T(8,128)S(1)} %get-tuple-element.25), channel_id=1, source_target_pairs={{0,384},{128,256},{256,128},{384,0},{1,385},{129,257},{257,129},{3... | collective-permute-start | bytes 98312 | tf_op jit(solution)/shard_map/ppermute | solution.py:17
  117.6 4.1 %collective-permute-done.6 = f32[16,512]{1,0:T(8,128)S(1)} collective-permute-done((f32[16,512]{1,0:T(8,128)S(1)}, f32[16,512]{1,0:T(8,128)S(1)}, u32[]{:S(2)}, u32[]{:S(2)}) %collective-permute-start.6) | collective-permute-done | bytes 32800 | tf_op jit(solution)/shard_map/ppermute | solution.py:17
  121.8 7.1 %collective-permute-start.7 = (bf16[16,512]{1,0:T(8,128)(2,1)S(1)}, bf16[16,512]{1,0:T(8,128)(2,1)S(1)}, u32[]{:S(2)}, u32[]{:S(2)}) collective-permute-start(bf16[16,512]{1,0:T(8,128)(2,1)S(1)} %add_convert_fusion), channel_id=1, source_target_pairs={{0,32},{32,0},{64,96},{96,64},{1,33},{33,1},{65,97},{97,65},{2,34}... | collective-permute-start | bytes 49160 | tf_op jit(solution)/shard_map/ppermute | solution.py:17
  128.9 7.1 %collective-permute-start.8 = (bf16[16,512]{1,0:T(8,128)(2,1)S(1)}, bf16[16,512]{1,0:T(8,128)(2,1)S(1)}, u32[]{:S(2)}, u32[]{:S(2)}) collective-permute-start(bf16[16,512]{1,0:T(8,128)(2,1)S(1)} %add_convert_fusion), channel_id=1, source_target_pairs={{0,64},{32,96},{64,0},{96,32},{1,65},{33,97},{65,1},{97,33},{2,66}... | collective-permute-start | bytes 49160 | tf_op jit(solution)/shard_map/ppermute | solution.py:17
  136.0 2.0 %collective-permute-start.9 = (bf16[16,512]{1,0:T(8,128)(2,1)S(1)}, bf16[16,512]{1,0:T(8,128)(2,1)S(1)}, u32[]{:S(2)}, u32[]{:S(2)}) collective-permute-start(bf16[16,512]{1,0:T(8,128)(2,1)S(1)} %add_convert_fusion), channel_id=1, source_target_pairs={{0,96},{32,64},{64,32},{96,0},{1,97},{33,65},{65,33},{97,1},{2,98}... | collective-permute-start | bytes 49160 | tf_op jit(solution)/shard_map/ppermute | solution.py:17
  138.0 7.0 %collective-permute-done.8 = bf16[16,512]{1,0:T(8,128)(2,1)S(1)} collective-permute-done((bf16[16,512]{1,0:T(8,128)(2,1)S(1)}, bf16[16,512]{1,0:T(8,128)(2,1)S(1)}, u32[]{:S(2)}, u32[]{:S(2)}) %collective-permute-start.8) | collective-permute-done | bytes 16416 | tf_op jit(solution)/shard_map/ppermute | solution.py:17
  145.7 3.3 %all-to-all-start.2 = ((bf16[4,16,512]{2,1,0:T(8,128)(2,1)}), bf16[4,16,512]{2,1,0:T(8,128)(2,1)S(1)}, u32[]{:S(2)}, u32[]{:S(2)}) async-start(bf16[4,16,512]{2,1,0:T(8,128)(2,1)} %broadcast_in_dim.34), calls=%async_computation.2 | async-start | bytes 131072 | tf_op jit(solution)/shard_map/all_to_all | solution.py:39
  149.2 4.3 %all-to-all-done.2 = bf16[4,16,512]{2,1,0:T(8,128)(2,1)S(1)} async-done(((bf16[4,16,512]{2,1,0:T(8,128)(2,1)}), bf16[4,16,512]{2,1,0:T(8,128)(2,1)S(1)}, u32[]{:S(2)}, u32[]{:S(2)}) %all-to-all-start.2) | async-done | bytes 65568 | tf_op jit(solution)/shard_map/all_to_all | solution.py:39
  154.4 11.2 %all-to-all-start.3 = ((bf16[32,16,512]{2,1,0:T(8,128)(2,1)}), bf16[32,16,512]{2,1,0:T(8,128)(2,1)S(1)}, u32[]{:S(2)}, u32[]{:S(2)}) async-start(bf16[32,16,512]{2,1,0:T(8,128)(2,1)} %broadcast_in_dim.58), calls=%async_computation.3 | async-start | bytes 1048576 | tf_op jit(solution)/shard_map/all_to_all | solution.py:39
  167.1 9.8 %all-to-all-done.3 = bf16[32,16,512]{2,1,0:T(8,128)(2,1)S(1)} async-done(((bf16[32,16,512]{2,1,0:T(8,128)(2,1)}), bf16[32,16,512]{2,1,0:T(8,128)(2,1)S(1)}, u32[]{:S(2)}, u32[]{:S(2)}) %all-to-all-start.3) | async-done | bytes 524320 | tf_op jit(solution)/shard_map/all_to_all | solution.py:39
  (66 shorter events, 10.1 us)
Async XLA Ops:
  3.2 20.6 %copy-start.10 = (s32[1024,2]{0,1:T(2,128)S(1)}, s32[1024,2]{0,1:T(2,128)}, u32[]{:S(2)}) copy-start(s32[1024,2]{0,1:T(2,128)} %param.19) | copy-start | bytes 24580
  3.2 20.6 %copy-start.11 = (s32[1024,2]{0,1:T(2,128)S(1)}, s32[1024,2]{0,1:T(2,128)}, u32[]{:S(2)}) copy-start(s32[1024,2]{0,1:T(2,128)} %param.18) | copy-start | bytes 24580
  3.2 74.9 %all-to-all-start = ((bf16[128,8,512]{2,1,0:T(8,128)(2,1)}), bf16[128,8,512]{2,1,0:T(8,128)(2,1)S(1)}, u32[]{:S(2)}, u32[]{:S(2)}) async-start(bf16[128,8,512]{2,1,0:T(8,128)(2,1)} %bitcast.33), calls=%async_computation | async-start | bytes 2097152 | tf_op jit(solution)/shard_map/all_to_all | solution.py:242
  29.9 48.2 %copy-start = (bf16[512,512]{1,0:T(8,128)(2,1)S(1)}, bf16[512,512]{1,0:T(8,128)(2,1)}, u32[]{:S(2)}) copy-start(bf16[512,512]{1,0:T(8,128)(2,1)} %weight.1) | copy-start | bytes 1572868
  29.9 48.2 %copy-start.1 = (bf16[256,512]{1,0:T(8,128)(2,1)S(1)}, bf16[256,512]{1,0:T(8,128)(2,1)}, u32[]{:S(2)}) copy-start(bf16[256,512]{1,0:T(8,128)(2,1)} %cotangent.1) | copy-start | bytes 786436
  80.3 8.7 %copy-start.8 = (bf16[256,512]{1,0:T(8,128)(2,1)S(1)}, bf16[256,512]{1,0:T(8,128)(2,1)}, u32[]{:S(2)}) copy-start(bf16[256,512]{1,0:T(8,128)(2,1)} %get-tuple-element.17) | copy-start | bytes 786436
  80.3 8.7 %copy-start.9 = (bf16[256,512]{1,0:T(8,128)(2,1)S(1)}, bf16[256,512]{1,0:T(8,128)(2,1)}, u32[]{:S(2)}) copy-start(bf16[256,512]{1,0:T(8,128)(2,1)} %get-tuple-element.18) | copy-start | bytes 786436
  80.3 64.7 %all-to-all-start.1 = ((bf16[128,8,512]{2,1,0:T(8,128)(2,1)}), bf16[128,8,512]{2,1,0:T(8,128)(2,1)S(1)}, u32[]{:S(2)}, u32[]{:S(2)}) async-start(bf16[128,8,512]{2,1,0:T(8,128)(2,1)} %bitcast.35), calls=%async_computation.1 | async-start | bytes 2097152 | tf_op jit(solution)/shard_map/all_to_all | solution.py:259
  89.4 4.3 %collective-permute-start = (f32[256,512]{1,0:T(8,128)S(1)}, f32[256,512]{1,0:T(8,128)S(1)}, u32[]{:S(2)}, u32[]{:S(2)}) collective-permute-start(f32[256,512]{1,0:T(8,128)S(1)} %constant_dynamic-slice_fusion.2), channel_id=1, source_target_pairs={{0,4},{4,0},{1,5},{5,1},{2,6},{6,2},{3,7},{7,3},{8,12},{12,8},{9,1... | collective-permute-start | bytes 1572872 | tf_op jit(solution)/shard_map/ppermute | solution.py:17
  93.8 55.2 %copy-start.12 = (s32[128,8]{0,1:T(8,128)S(1)}, s32[128,8]{0,1:T(8,128)}, u32[]{:S(2)}) copy-start(s32[128,8]{0,1:T(8,128)} %param.16) | copy-start | bytes 12292
  93.8 55.2 %copy-start.14 = (s32[128]{0:T(128)S(1)}, s32[128]{0:T(128)}, u32[]{:S(2)}) copy-start(s32[128]{0:T(128)} %param.17) | copy-start | bytes 1540
  93.8 9.6 %collective-permute-start.1 = (bf16[64,512]{1,0:T(8,128)(2,1)S(1)}, bf16[64,512]{1,0:T(8,128)(2,1)S(1)}, u32[]{:S(2)}, u32[]{:S(2)}) collective-permute-start(bf16[64,512]{1,0:T(8,128)(2,1)S(1)} %get-tuple-element.21), channel_id=1, source_target_pairs={{0,1},{1,0},{2,3},{3,2},{4,5},{5,4},{6,7},{7,6},{8,9},{9,8},{10,11... | collective-permute-start | bytes 196616 | tf_op jit(solution)/shard_map/ppermute | solution.py:17
  97.0 6.8 %collective-permute-start.2 = (bf16[64,512]{1,0:T(8,128)(2,1)S(1)}, bf16[64,512]{1,0:T(8,128)(2,1)S(1)}, u32[]{:S(2)}, u32[]{:S(2)}) collective-permute-start(bf16[64,512]{1,0:T(8,128)(2,1)S(1)} %get-tuple-element.23), channel_id=1, source_target_pairs={{0,2},{1,3},{2,0},{3,1},{4,6},{5,7},{6,4},{7,5},{8,10},{9,11},{10,... | collective-permute-start | bytes 196616 | tf_op jit(solution)/shard_map/ppermute | solution.py:17
  101.3 6.5 %collective-permute-start.3 = (bf16[64,512]{1,0:T(8,128)(2,1)S(1)}, bf16[64,512]{1,0:T(8,128)(2,1)S(1)}, u32[]{:S(2)}, u32[]{:S(2)}) collective-permute-start(bf16[64,512]{1,0:T(8,128)(2,1)S(1)} %get-tuple-element.22), channel_id=1, source_target_pairs={{0,3},{1,2},{2,1},{3,0},{4,7},{5,6},{6,5},{7,4},{8,11},{9,10},{10,... | collective-permute-start | bytes 196616 | tf_op jit(solution)/shard_map/ppermute | solution.py:17
  107.9 9.6 %collective-permute-start.4 = (f32[16,512]{1,0:T(8,128)S(1)}, f32[16,512]{1,0:T(8,128)S(1)}, u32[]{:S(2)}, u32[]{:S(2)}) collective-permute-start(f32[16,512]{1,0:T(8,128)S(1)} %get-tuple-element.24), channel_id=1, source_target_pairs={{0,128},{128,0},{256,384},{384,256},{1,129},{129,1},{257,385},{385... | collective-permute-start | bytes 98312 | tf_op jit(solution)/shard_map/ppermute | solution.py:17
  110.8 6.8 %collective-permute-start.5 = (f32[16,512]{1,0:T(8,128)S(1)}, f32[16,512]{1,0:T(8,128)S(1)}, u32[]{:S(2)}, u32[]{:S(2)}) collective-permute-start(f32[16,512]{1,0:T(8,128)S(1)} %get-tuple-element.26), channel_id=1, source_target_pairs={{0,256},{128,384},{256,0},{384,128},{1,257},{129,385},{257,1},{385... | collective-permute-start | bytes 98312 | tf_op jit(solution)/shard_map/ppermute | solution.py:17
  115.5 6.2 %collective-permute-start.6 = (f32[16,512]{1,0:T(8,128)S(1)}, f32[16,512]{1,0:T(8,128)S(1)}, u32[]{:S(2)}, u32[]{:S(2)}) collective-permute-start(f32[16,512]{1,0:T(8,128)S(1)} %get-tuple-element.25), channel_id=1, source_target_pairs={{0,384},{128,256},{256,128},{384,0},{1,385},{129,257},{257,129},{3... | collective-permute-start | bytes 98312 | tf_op jit(solution)/shard_map/ppermute | solution.py:17
  121.8 16.2 %collective-permute-start.7 = (bf16[16,512]{1,0:T(8,128)(2,1)S(1)}, bf16[16,512]{1,0:T(8,128)(2,1)S(1)}, u32[]{:S(2)}, u32[]{:S(2)}) collective-permute-start(bf16[16,512]{1,0:T(8,128)(2,1)S(1)} %add_convert_fusion), channel_id=1, source_target_pairs={{0,32},{32,0},{64,96},{96,64},{1,33},{33,1},{65,97},{97,65},{2,34}... | collective-permute-start | bytes 49160 | tf_op jit(solution)/shard_map/ppermute | solution.py:17
  128.9 16.1 %collective-permute-start.8 = (bf16[16,512]{1,0:T(8,128)(2,1)S(1)}, bf16[16,512]{1,0:T(8,128)(2,1)S(1)}, u32[]{:S(2)}, u32[]{:S(2)}) collective-permute-start(bf16[16,512]{1,0:T(8,128)(2,1)S(1)} %add_convert_fusion), channel_id=1, source_target_pairs={{0,64},{32,96},{64,0},{96,32},{1,65},{33,97},{65,1},{97,33},{2,66}... | collective-permute-start | bytes 49160 | tf_op jit(solution)/shard_map/ppermute | solution.py:17
  136.0 9.0 %collective-permute-start.9 = (bf16[16,512]{1,0:T(8,128)(2,1)S(1)}, bf16[16,512]{1,0:T(8,128)(2,1)S(1)}, u32[]{:S(2)}, u32[]{:S(2)}) collective-permute-start(bf16[16,512]{1,0:T(8,128)(2,1)S(1)} %add_convert_fusion), channel_id=1, source_target_pairs={{0,96},{32,64},{64,32},{96,0},{1,97},{33,65},{65,33},{97,1},{2,98}... | collective-permute-start | bytes 49160 | tf_op jit(solution)/shard_map/ppermute | solution.py:17
  145.0 20.6 %copy-start.6 = (bf16[2,2,128,128]{3,1,2,0:T(2,128)(2,1)S(1)}, bf16[2,2,128,128]{3,1,2,0:T(2,128)(2,1)}, u32[]{:S(2)}) copy-start(bf16[2,2,128,128]{3,1,2,0:T(2,128)(2,1)} %copy-done.5) | copy-start | bytes 393220
  145.0 20.6 %copy-start.7 = (bf16[256,512]{1,0:T(8,128)(2,1)S(1)}, bf16[256,512]{1,0:T(8,128)(2,1)}, u32[]{:S(2)}) copy-start(bf16[256,512]{1,0:T(8,128)(2,1)} %get-tuple-element.13) | copy-start | bytes 786436
  145.7 7.9 %all-to-all-start.2 = ((bf16[4,16,512]{2,1,0:T(8,128)(2,1)}), bf16[4,16,512]{2,1,0:T(8,128)(2,1)S(1)}, u32[]{:S(2)}, u32[]{:S(2)}) async-start(bf16[4,16,512]{2,1,0:T(8,128)(2,1)} %broadcast_in_dim.34), calls=%async_computation.2 | async-start | bytes 131072 | tf_op jit(solution)/shard_map/all_to_all | solution.py:39
  154.4 22.4 %all-to-all-start.3 = ((bf16[32,16,512]{2,1,0:T(8,128)(2,1)}), bf16[32,16,512]{2,1,0:T(8,128)(2,1)S(1)}, u32[]{:S(2)}, u32[]{:S(2)}) async-start(bf16[32,16,512]{2,1,0:T(8,128)(2,1)} %broadcast_in_dim.58), calls=%async_computation.3 | async-start | bytes 1048576 | tf_op jit(solution)/shard_map/all_to_all | solution.py:39
  (6 other events, 9.9 us)

commit v7 on v6

--- a/solution.py
+++ b/solution.py
@@ -39,17 +39,20 @@
     return lax.all_to_all(value, axes, split_axis=0, concat_axis=0, tiled=True)
 
 
-PLANE = ("core", "slab", "y")
-
-
 def sum_blocks(part):
-    mine = scatter_sum(scatter_sum(scatter_sum(part, "core", jnp.float32), "slab"), "y", jnp.float32)
-    return quad_sum(mine, "z_hi")
+    rows, width = part.shape
+    plane, cores = lax.axis_size(("slab", "y")), lax.axis_size("core")
+    part = part.reshape(plane, cores, rows // plane // cores, width).swapaxes(0, 1)
+    mine = scatter_sum(part.reshape(rows, width), "core", jnp.float32)
+    return quad_sum(scatter_sum(scatter_sum(mine, "slab"), "y", jnp.float32), "z_hi")
 
 
 def finish_sum(mine, scale):
-    mine = (jnp.sum(to_all(mine.astype(jnp.bfloat16), "z_lo").astype(jnp.float32), axis=0) * scale).astype(jnp.bfloat16)
-    return to_all(mine, PLANE).reshape(-1, mine.shape[-1]).astype(jnp.float32)
+    quads = to_all(mine.astype(jnp.bfloat16), ("core", "z_lo"))
+    quads = quads.reshape((lax.axis_size("core"), lax.axis_size("z_lo")) + mine.shape)
+    mine = (jnp.sum(quads.astype(jnp.float32), axis=1) * scale).astype(jnp.bfloat16)
+    mine = mine.reshape(-1, mine.shape[-1])
+    return to_all(mine, ("slab", "y")).reshape(-1, mine.shape[-1]).astype(jnp.float32)
 
 
 VMEM = pl.BlockSpec(memory_space=pltpu.VMEM)

time: 179 us -> 179 us (level)
  no operation moved by 1% of the time
where the time goes in v7:
time: 179 us; the launch traced here: 178 us
  starting transfers between devices  80.4 us (45%)
  waiting for transfers between devices  80.1 us (45%)
  local copies, waits for them, and re-layouts  4.96 us (3%)
  Pallas kernels  4.68 us (3%)
  other arithmetic  3.94 us (2%)
  matrix products  2.45 us (1%)
    all_to_all x1, waiting for transfers between devices, shards(): lax.all_to_all(outgoing, DOM, split_axis=0, concat_axis=0, tiled=True)  47.8 us
    ppermute x10, starting transfers between devices, from_peer(): lax.ppermute(value, axis, [(place, place ^ mask) for place in range(count)])  38.2 us
    all_to_all x1, starting transfers between devices, shards(): lax.all_to_all(outgoing, DOM, split_axis=0, concat_axis=0, tiled=True)  20.6 us
    ppermute x10, waiting for transfers between devices, from_peer(): lax.ppermute(value, axis, [(place, place ^ mask) for place in range(count)])  17 us
    all_to_all x2, waiting for transfers between devices, to_all(): return lax.all_to_all(value, axes, split_axis=0, concat_axis=0, tiled=True)  15.2 us
    all_to_all x2, starting transfers between devices, to_all(): return lax.all_to_all(value, axes, split_axis=0, concat_axis=0, tiled=True)  13 us
    all_to_all x1, starting transfers between devices, shards(): lax.all_to_all(slot_grad, DOM, split_axis=0, concat_axis=0, tiled=True)  8.63 us
  transfers between devices with their start and end apart: 14, of which 9 were waited for; matrix products, arithmetic and copies ran while one was open for 4% of the time, Pallas kernels for 0%

profile of v7, /device:TPU:1, one launch (start us, length us, event | category | flops | bytes accessed | tf_op | source)
XLA Modules:
  0.0 177.6 jit_solution(17904323460018079251)
XLA Ops:
  0.6 2.5 %take_rows.1 = bf16[1024,512]{1,0:T(8,128)(2,1)} custom-call(s32[8,128]{1,0:T(8,128)} %bitcast.51, s32[1,128]{1,0:T(1,128)} %bitcast.53, bf16[256,512]{1,0:T(8,128)(2,1)} %node_feats.1), custom_call_target="tpu_custom_call" | custom-call | flops 268435456 | bytes 2097152 | tf_op jit(solution)/shard_map/take_rows/pallas_call | solution.py:181
  3.2 20.6 %all-to-all-start = ((bf16[128,8,512]{2,1,0:T(8,128)(2,1)}), bf16[128,8,512]{2,1,0:T(8,128)(2,1)S(1)}, u32[]{:S(2)}, u32[]{:S(2)}) async-start(bf16[128,8,512]{2,1,0:T(8,128)(2,1)} %bitcast.43), calls=%async_computation | async-start | bytes 2097152 | tf_op jit(solution)/shard_map/all_to_all | solution.py:245
  25.2 1.6 copy.21
  30.3 47.8 %all-to-all-done = bf16[128,8,512]{2,1,0:T(8,128)(2,1)S(1)} async-done(((bf16[128,8,512]{2,1,0:T(8,128)(2,1)}), bf16[128,8,512]{2,1,0:T(8,128)(2,1)S(1)}, u32[]{:S(2)}, u32[]{:S(2)}) %all-to-all-start) | async-done | bytes 1048608 | tf_op jit(solution)/shard_map/all_to_all | solution.py:245
  78.1 2.2 %layer.1 = (bf16[256,512]{1,0:T(8,128)(2,1)}, bf16[256,512]{1,0:T(8,128)(2,1)}, bf16[256,512]{1,0:T(8,128)(2,1)}, bf16[256,512]{1,0:T(8,128)(2,1)}, bf16[1024,512]{1,0:T(8,128)(2,1)}) custom-call(bf16[1024,512]{1,0:T(8,128)(2,1)S(1)} %bitcast.40, bf16[256,1024]{1,0:T(8,128)(2,1)S(1)} %copy.22.mixing, bf16[1024,256]{1,0:T(8,128)(2,1)S(1)} %convert_bitcast_fusion.mixing_rows, ...), custom_call_target="tpu_custom_call" | custom-call | flops 805306368 | bytes 6291456 | tf_op jit(solution)/shard_map/layer/pallas_call | solution.py:109
  80.3 8.6 %all-to-all-start.1 = ((bf16[128,8,512]{2,1,0:T(8,128)(2,1)}), bf16[128,8,512]{2,1,0:T(8,128)(2,1)S(1)}, u32[]{:S(2)}, u32[]{:S(2)}) async-start(bf16[128,8,512]{2,1,0:T(8,128)(2,1)} %bitcast.46), calls=%async_computation.1 | async-start | bytes 2097152 | tf_op jit(solution)/shard_map/all_to_all | solution.py:262
  89.5 2.8 %collective-permute-start = (f32[256,512]{1,0:T(8,128)S(1)}, f32[256,512]{1,0:T(8,128)S(1)}, u32[]{:S(2)}, u32[]{:S(2)}) collective-permute-start(f32[256,512]{1,0:T(8,128)S(1)} %constant_dynamic-slice_fusion.2), channel_id=1, source_target_pairs={{0,4},{4,0},{1,5},{5,1},{2,6},{6,2},{3,7},{7,3},{8,12},{12,8},{9,1... | collective-permute-start | bytes 1572872 | tf_op jit(solution)/shard_map/ppermute | solution.py:17
  92.3 1.5 collective-permute-done
  93.9 3.1 %collective-permute-start.1 = (bf16[64,512]{1,0:T(8,128)(2,1)S(1)}, bf16[64,512]{1,0:T(8,128)(2,1)S(1)}, u32[]{:S(2)}, u32[]{:S(2)}) collective-permute-start(bf16[64,512]{1,0:T(8,128)(2,1)S(1)} %get-tuple-element.21), channel_id=1, source_target_pairs={{0,1},{1,0},{2,3},{3,2},{4,5},{5,4},{6,7},{7,6},{8,9},{9,8},{10,11... | collective-permute-start | bytes 196616 | tf_op jit(solution)/shard_map/ppermute | solution.py:17
  97.1 4.4 %collective-permute-start.2 = (bf16[64,512]{1,0:T(8,128)(2,1)S(1)}, bf16[64,512]{1,0:T(8,128)(2,1)S(1)}, u32[]{:S(2)}, u32[]{:S(2)}) collective-permute-start(bf16[64,512]{1,0:T(8,128)(2,1)S(1)} %get-tuple-element.23), channel_id=1, source_target_pairs={{0,2},{1,3},{2,0},{3,1},{4,6},{5,7},{6,4},{7,5},{8,10},{9,11},{10,... | collective-permute-start | bytes 196616 | tf_op jit(solution)/shard_map/ppermute | solution.py:17
  101.4 2.1 %collective-permute-start.3 = (bf16[64,512]{1,0:T(8,128)(2,1)S(1)}, bf16[64,512]{1,0:T(8,128)(2,1)S(1)}, u32[]{:S(2)}, u32[]{:S(2)}) collective-permute-start(bf16[64,512]{1,0:T(8,128)(2,1)S(1)} %get-tuple-element.22), channel_id=1, source_target_pairs={{0,3},{1,2},{2,1},{3,0},{4,7},{5,6},{6,5},{7,4},{8,11},{9,10},{10,... | collective-permute-start | bytes 196616 | tf_op jit(solution)/shard_map/ppermute | solution.py:17
  103.9 4.1 %collective-permute-done.3 = bf16[64,512]{1,0:T(8,128)(2,1)S(1)} collective-permute-done((bf16[64,512]{1,0:T(8,128)(2,1)S(1)}, bf16[64,512]{1,0:T(8,128)(2,1)S(1)}, u32[]{:S(2)}, u32[]{:S(2)}) %collective-permute-start.3) | collective-permute-done | bytes 65568 | tf_op jit(solution)/shard_map/ppermute | solution.py:17
  108.0 2.9 %collective-permute-start.4 = (f32[16,512]{1,0:T(8,128)S(1)}, f32[16,512]{1,0:T(8,128)S(1)}, u32[]{:S(2)}, u32[]{:S(2)}) collective-permute-start(f32[16,512]{1,0:T(8,128)S(1)} %get-tuple-element.24), channel_id=1, source_target_pairs={{0,128},{128,0},{256,384},{384,256},{1,129},{129,1},{257,385},{385... | collective-permute-start | bytes 98312 | tf_op jit(solution)/shard_map/ppermute | solution.py:17
  110.9 4.7 %collective-permute-start.5 = (f32[16,512]{1,0:T(8,128)S(1)}, f32[16,512]{1,0:T(8,128)S(1)}, u32[]{:S(2)}, u32[]{:S(2)}) collective-permute-start(f32[16,512]{1,0:T(8,128)S(1)} %get-tuple-element.26), channel_id=1, source_target_pairs={{0,256},{128,384},{256,0},{384,128},{1,257},{129,385},{257,1},{385... | collective-permute-start | bytes 98312 | tf_op jit(solution)/shard_map/ppermute | solution.py:17
  115.6 2.0 %collective-permute-start.6 = (f32[16,512]{1,0:T(8,128)S(1)}, f32[16,512]{1,0:T(8,128)S(1)}, u32[]{:S(2)}, u32[]{:S(2)}) collective-permute-start(f32[16,512]{1,0:T(8,128)S(1)} %get-tuple-element.25), channel_id=1, source_target_pairs={{0,384},{128,256},{256,128},{384,0},{1,385},{129,257},{257,129},{3... | collective-permute-start | bytes 98312 | tf_op jit(solution)/shard_map/ppermute | solution.py:17
  117.7 4.2 %collective-permute-done.6 = f32[16,512]{1,0:T(8,128)S(1)} collective-permute-done((f32[16,512]{1,0:T(8,128)S(1)}, f32[16,512]{1,0:T(8,128)S(1)}, u32[]{:S(2)}, u32[]{:S(2)}) %collective-permute-start.6) | collective-permute-done | bytes 32800 | tf_op jit(solution)/shard_map/ppermute | solution.py:17
  121.9 7.0 %collective-permute-start.7 = (bf16[16,512]{1,0:T(8,128)(2,1)S(1)}, bf16[16,512]{1,0:T(8,128)(2,1)S(1)}, u32[]{:S(2)}, u32[]{:S(2)}) collective-permute-start(bf16[16,512]{1,0:T(8,128)(2,1)S(1)} %add_convert_fusion), channel_id=1, source_target_pairs={{0,32},{32,0},{64,96},{96,64},{1,33},{33,1},{65,97},{97,65},{2,34}... | collective-permute-start | bytes 49160 | tf_op jit(solution)/shard_map/ppermute | solution.py:17
  128.9 7.1 %collective-permute-start.8 = (bf16[16,512]{1,0:T(8,128)(2,1)S(1)}, bf16[16,512]{1,0:T(8,128)(2,1)S(1)}, u32[]{:S(2)}, u32[]{:S(2)}) collective-permute-start(bf16[16,512]{1,0:T(8,128)(2,1)S(1)} %add_convert_fusion), channel_id=1, source_target_pairs={{0,64},{32,96},{64,0},{96,32},{1,65},{33,97},{65,1},{97,33},{2,66}... | collective-permute-start | bytes 49160 | tf_op jit(solution)/shard_map/ppermute | solution.py:17
  136.1 2.1 %collective-permute-start.9 = (bf16[16,512]{1,0:T(8,128)(2,1)S(1)}, bf16[16,512]{1,0:T(8,128)(2,1)S(1)}, u32[]{:S(2)}, u32[]{:S(2)}) collective-permute-start(bf16[16,512]{1,0:T(8,128)(2,1)S(1)} %add_convert_fusion), channel_id=1, source_target_pairs={{0,96},{32,64},{64,32},{96,0},{1,97},{33,65},{65,33},{97,1},{2,98}... | collective-permute-start | bytes 49160 | tf_op jit(solution)/shard_map/ppermute | solution.py:17
  138.2 6.8 %collective-permute-done.8 = bf16[16,512]{1,0:T(8,128)(2,1)S(1)} collective-permute-done((bf16[16,512]{1,0:T(8,128)(2,1)S(1)}, bf16[16,512]{1,0:T(8,128)(2,1)S(1)}, u32[]{:S(2)}, u32[]{:S(2)}) %collective-permute-start.8) | collective-permute-done | bytes 16416 | tf_op jit(solution)/shard_map/ppermute | solution.py:17
  145.7 7.6 %all-to-all-start.2 = ((bf16[8,16,512]{2,1,0:T(8,128)(2,1)}), bf16[8,16,512]{2,1,0:T(8,128)(2,1)S(1)}, u32[]{:S(2)}, u32[]{:S(2)}) async-start(bf16[8,16,512]{2,1,0:T(8,128)(2,1)} %broadcast_in_dim.56), calls=%async_computation.2 | async-start | bytes 262144 | tf_op jit(solution)/shard_map/all_to_all | solution.py:39
  153.6 6.3 %all-to-all-done.2 = bf16[8,16,512]{2,1,0:T(8,128)(2,1)S(1)} async-done(((bf16[8,16,512]{2,1,0:T(8,128)(2,1)}), bf16[8,16,512]{2,1,0:T(8,128)(2,1)S(1)}, u32[]{:S(2)}, u32[]{:S(2)}) %all-to-all-start.2) | async-done | bytes 131104 | tf_op jit(solution)/shard_map/all_to_all | solution.py:39
  160.8 5.4 %all-to-all-start.3 = ((bf16[16,32,512]{2,1,0:T(8,128)(2,1)}), bf16[16,32,512]{2,1,0:T(8,128)(2,1)S(1)}, u32[]{:S(2)}, u32[]{:S(2)}) async-start(bf16[16,32,512]{2,1,0:T(8,128)(2,1)} %broadcast_in_dim.57), calls=%async_computation.3 | async-start | bytes 1048576 | tf_op jit(solution)/shard_map/all_to_all | solution.py:39
  167.6 8.9 %all-to-all-done.3 = bf16[16,32,512]{2,1,0:T(8,128)(2,1)S(1)} async-done(((bf16[16,32,512]{2,1,0:T(8,128)(2,1)}), bf16[16,32,512]{2,1,0:T(8,128)(2,1)S(1)}, u32[]{:S(2)}, u32[]{:S(2)}) %all-to-all-start.3) | async-done | bytes 524320 | tf_op jit(solution)/shard_map/all_to_all | solution.py:39
  (67 shorter events, 10.2 us)
Async XLA Ops:
  3.2 20.6 %copy-start.10 = (s32[1024,2]{0,1:T(2,128)S(1)}, s32[1024,2]{0,1:T(2,128)}, u32[]{:S(2)}) copy-start(s32[1024,2]{0,1:T(2,128)} %param.19) | copy-start | bytes 24580
  3.2 20.6 %copy-start.11 = (s32[1024,2]{0,1:T(2,128)S(1)}, s32[1024,2]{0,1:T(2,128)}, u32[]{:S(2)}) copy-start(s32[1024,2]{0,1:T(2,128)} %param.18) | copy-start | bytes 24580
  3.2 74.9 %all-to-all-start = ((bf16[128,8,512]{2,1,0:T(8,128)(2,1)}), bf16[128,8,512]{2,1,0:T(8,128)(2,1)S(1)}, u32[]{:S(2)}, u32[]{:S(2)}) async-start(bf16[128,8,512]{2,1,0:T(8,128)(2,1)} %bitcast.43), calls=%async_computation | async-start | bytes 2097152 | tf_op jit(solution)/shard_map/all_to_all | solution.py:245
  29.9 48.2 %copy-start = (bf16[512,512]{1,0:T(8,128)(2,1)S(1)}, bf16[512,512]{1,0:T(8,128)(2,1)}, u32[]{:S(2)}) copy-start(bf16[512,512]{1,0:T(8,128)(2,1)} %weight.1) | copy-start | bytes 1572868
  29.9 48.2 %copy-start.1 = (bf16[256,512]{1,0:T(8,128)(2,1)S(1)}, bf16[256,512]{1,0:T(8,128)(2,1)}, u32[]{:S(2)}) copy-start(bf16[256,512]{1,0:T(8,128)(2,1)} %cotangent.1) | copy-start | bytes 786436
  80.3 8.7 %copy-start.8 = (bf16[256,512]{1,0:T(8,128)(2,1)S(1)}, bf16[256,512]{1,0:T(8,128)(2,1)}, u32[]{:S(2)}) copy-start(bf16[256,512]{1,0:T(8,128)(2,1)} %get-tuple-element.17) | copy-start | bytes 786436
  80.3 8.7 %copy-start.9 = (bf16[256,512]{1,0:T(8,128)(2,1)S(1)}, bf16[256,512]{1,0:T(8,128)(2,1)}, u32[]{:S(2)}) copy-start(bf16[256,512]{1,0:T(8,128)(2,1)} %get-tuple-element.18) | copy-start | bytes 786436
  80.3 64.7 %all-to-all-start.1 = ((bf16[128,8,512]{2,1,0:T(8,128)(2,1)}), bf16[128,8,512]{2,1,0:T(8,128)(2,1)S(1)}, u32[]{:S(2)}, u32[]{:S(2)}) async-start(bf16[128,8,512]{2,1,0:T(8,128)(2,1)} %bitcast.46), calls=%async_computation.1 | async-start | bytes 2097152 | tf_op jit(solution)/shard_map/all_to_all | solution.py:262
  89.5 4.3 %collective-permute-start = (f32[256,512]{1,0:T(8,128)S(1)}, f32[256,512]{1,0:T(8,128)S(1)}, u32[]{:S(2)}, u32[]{:S(2)}) collective-permute-start(f32[256,512]{1,0:T(8,128)S(1)} %constant_dynamic-slice_fusion.2), channel_id=1, source_target_pairs={{0,4},{4,0},{1,5},{5,1},{2,6},{6,2},{3,7},{7,3},{8,12},{12,8},{9,1... | collective-permute-start | bytes 1572872 | tf_op jit(solution)/shard_map/ppermute | solution.py:17
  93.9 59.5 %copy-start.12 = (s32[128,8]{0,1:T(8,128)S(1)}, s32[128,8]{0,1:T(8,128)}, u32[]{:S(2)}) copy-start(s32[128,8]{0,1:T(8,128)} %param.16) | copy-start | bytes 12292
  93.9 59.5 %copy-start.14 = (s32[128]{0:T(128)S(1)}, s32[128]{0:T(128)}, u32[]{:S(2)}) copy-start(s32[128]{0:T(128)} %param.17) | copy-start | bytes 1540
  93.9 9.6 %collective-permute-start.1 = (bf16[64,512]{1,0:T(8,128)(2,1)S(1)}, bf16[64,512]{1,0:T(8,128)(2,1)S(1)}, u32[]{:S(2)}, u32[]{:S(2)}) collective-permute-start(bf16[64,512]{1,0:T(8,128)(2,1)S(1)} %get-tuple-element.21), channel_id=1, source_target_pairs={{0,1},{1,0},{2,3},{3,2},{4,5},{5,4},{6,7},{7,6},{8,9},{9,8},{10,11... | collective-permute-start | bytes 196616 | tf_op jit(solution)/shard_map/ppermute | solution.py:17
  97.1 6.8 %collective-permute-start.2 = (bf16[64,512]{1,0:T(8,128)(2,1)S(1)}, bf16[64,512]{1,0:T(8,128)(2,1)S(1)}, u32[]{:S(2)}, u32[]{:S(2)}) collective-permute-start(bf16[64,512]{1,0:T(8,128)(2,1)S(1)} %get-tuple-element.23), channel_id=1, source_target_pairs={{0,2},{1,3},{2,0},{3,1},{4,6},{5,7},{6,4},{7,5},{8,10},{9,11},{10,... | collective-permute-start | bytes 196616 | tf_op jit(solution)/shard_map/ppermute | solution.py:17
  101.4 6.5 %collective-permute-start.3 = (bf16[64,512]{1,0:T(8,128)(2,1)S(1)}, bf16[64,512]{1,0:T(8,128)(2,1)S(1)}, u32[]{:S(2)}, u32[]{:S(2)}) collective-permute-start(bf16[64,512]{1,0:T(8,128)(2,1)S(1)} %get-tuple-element.22), channel_id=1, source_target_pairs={{0,3},{1,2},{2,1},{3,0},{4,7},{5,6},{6,5},{7,4},{8,11},{9,10},{10,... | collective-permute-start | bytes 196616 | tf_op jit(solution)/shard_map/ppermute | solution.py:17
  108.0 9.6 %collective-permute-start.4 = (f32[16,512]{1,0:T(8,128)S(1)}, f32[16,512]{1,0:T(8,128)S(1)}, u32[]{:S(2)}, u32[]{:S(2)}) collective-permute-start(f32[16,512]{1,0:T(8,128)S(1)} %get-tuple-element.24), channel_id=1, source_target_pairs={{0,128},{128,0},{256,384},{384,256},{1,129},{129,1},{257,385},{385... | collective-permute-start | bytes 98312 | tf_op jit(solution)/shard_map/ppermute | solution.py:17
  110.9 6.8 %collective-permute-start.5 = (f32[16,512]{1,0:T(8,128)S(1)}, f32[16,512]{1,0:T(8,128)S(1)}, u32[]{:S(2)}, u32[]{:S(2)}) collective-permute-start(f32[16,512]{1,0:T(8,128)S(1)} %get-tuple-element.26), channel_id=1, source_target_pairs={{0,256},{128,384},{256,0},{384,128},{1,257},{129,385},{257,1},{385... | collective-permute-start | bytes 98312 | tf_op jit(solution)/shard_map/ppermute | solution.py:17
  115.6 6.3 %collective-permute-start.6 = (f32[16,512]{1,0:T(8,128)S(1)}, f32[16,512]{1,0:T(8,128)S(1)}, u32[]{:S(2)}, u32[]{:S(2)}) collective-permute-start(f32[16,512]{1,0:T(8,128)S(1)} %get-tuple-element.25), channel_id=1, source_target_pairs={{0,384},{128,256},{256,128},{384,0},{1,385},{129,257},{257,129},{3... | collective-permute-start | bytes 98312 | tf_op jit(solution)/shard_map/ppermute | solution.py:17
  121.9 16.2 %collective-permute-start.7 = (bf16[16,512]{1,0:T(8,128)(2,1)S(1)}, bf16[16,512]{1,0:T(8,128)(2,1)S(1)}, u32[]{:S(2)}, u32[]{:S(2)}) collective-permute-start(bf16[16,512]{1,0:T(8,128)(2,1)S(1)} %add_convert_fusion), channel_id=1, source_target_pairs={{0,32},{32,0},{64,96},{96,64},{1,33},{33,1},{65,97},{97,65},{2,34}... | collective-permute-start | bytes 49160 | tf_op jit(solution)/shard_map/ppermute | solution.py:17
  128.9 16.1 %collective-permute-start.8 = (bf16[16,512]{1,0:T(8,128)(2,1)S(1)}, bf16[16,512]{1,0:T(8,128)(2,1)S(1)}, u32[]{:S(2)}, u32[]{:S(2)}) collective-permute-start(bf16[16,512]{1,0:T(8,128)(2,1)S(1)} %add_convert_fusion), channel_id=1, source_target_pairs={{0,64},{32,96},{64,0},{96,32},{1,65},{33,97},{65,1},{97,33},{2,66}... | collective-permute-start | bytes 49160 | tf_op jit(solution)/shard_map/ppermute | solution.py:17
  136.1 8.9 %collective-permute-start.9 = (bf16[16,512]{1,0:T(8,128)(2,1)S(1)}, bf16[16,512]{1,0:T(8,128)(2,1)S(1)}, u32[]{:S(2)}, u32[]{:S(2)}) collective-permute-start(bf16[16,512]{1,0:T(8,128)(2,1)S(1)} %add_convert_fusion), channel_id=1, source_target_pairs={{0,96},{32,64},{64,32},{96,0},{1,97},{33,65},{65,33},{97,1},{2,98}... | collective-permute-start | bytes 49160 | tf_op jit(solution)/shard_map/ppermute | solution.py:17
  145.7 14.2 %all-to-all-start.2 = ((bf16[8,16,512]{2,1,0:T(8,128)(2,1)}), bf16[8,16,512]{2,1,0:T(8,128)(2,1)S(1)}, u32[]{:S(2)}, u32[]{:S(2)}) async-start(bf16[8,16,512]{2,1,0:T(8,128)(2,1)} %broadcast_in_dim.56), calls=%async_computation.2 | async-start | bytes 262144 | tf_op jit(solution)/shard_map/all_to_all | solution.py:39
  153.3 12.8 %copy-start.6 = (bf16[2,2,128,128]{3,1,2,0:T(2,128)(2,1)S(1)}, bf16[2,2,128,128]{3,1,2,0:T(2,128)(2,1)}, u32[]{:S(2)}) copy-start(bf16[2,2,128,128]{3,1,2,0:T(2,128)(2,1)} %copy-done.5) | copy-start | bytes 393220
  153.3 12.8 %copy-start.7 = (bf16[256,512]{1,0:T(8,128)(2,1)S(1)}, bf16[256,512]{1,0:T(8,128)(2,1)}, u32[]{:S(2)}) copy-start(bf16[256,512]{1,0:T(8,128)(2,1)} %get-tuple-element.13) | copy-start | bytes 786436
  160.8 15.7 %all-to-all-start.3 = ((bf16[16,32,512]{2,1,0:T(8,128)(2,1)}), bf16[16,32,512]{2,1,0:T(8,128)(2,1)S(1)}, u32[]{:S(2)}, u32[]{:S(2)}) async-start(bf16[16,32,512]{2,1,0:T(8,128)(2,1)} %broadcast_in_dim.57), calls=%async_computation.3 | async-start | bytes 1048576 | tf_op jit(solution)/shard_map/all_to_all | solution.py:39
  (6 other events, 9.9 us)

commit v8 on v6

--- a/solution.py
+++ b/solution.py
@@ -76,8 +76,6 @@
     leave(aggregated_rows, aggregated)
     pre_act = jnp.dot(gathered, weight[...], preferred_element_type=jnp.float32)
     gating_value = jax.nn.sigmoid(pre_act)
-    output_rows[...] = (pre_act * gating_value).astype(jnp.bfloat16)
-    leave(output_rows, output)
     scaled = cotangent[...].astype(jnp.float32) * gating_value
     grad = (scaled * (1.0 + pre_act * (1.0 - gating_value))).astype(jnp.bfloat16)
     grad_rows[...] = grad
@@ -95,6 +93,8 @@
             mixing_rows[span, :], summed, preferred_element_type=jnp.float32
         ).astype(jnp.bfloat16)
         leave(slots.at[span, :], slot_grad.at[span, :])
+    output_rows[...] = (pre_act * gating_value).astype(jnp.bfloat16)
+    leave(output_rows, output)
     for copy in copies:
         copy.wait()
 

time: 179 us -> 179 us (level)
  no operation moved by 1% of the time
where the time goes in v8:
time: 179 us; the launch traced here: 178 us
  starting transfers between devices  81.8 us (46%)
  waiting for transfers between devices  79 us (44%)
  local copies, waits for them, and re-layouts  4.86 us (3%)
  Pallas kernels  4.77 us (3%)
  other arithmetic  3.94 us (2%)
  matrix products  2.45 us (1%)
    all_to_all x1, waiting for transfers between devices, shards(): lax.all_to_all(outgoing, DOM, split_axis=0, concat_axis=0, tiled=True)  47.8 us
    ppermute x10, starting transfers between devices, from_peer(): lax.ppermute(value, axis, [(place, place ^ mask) for place in range(count)])  38.2 us
    all_to_all x1, starting transfers between devices, shards(): lax.all_to_all(outgoing, DOM, split_axis=0, concat_axis=0, tiled=True)  20.6 us
    ppermute x10, waiting for transfers between devices, from_peer(): lax.ppermute(value, axis, [(place, place ^ mask) for place in range(count)])  17.1 us
    all_to_all x2, starting transfers between devices, to_all(): return lax.all_to_all(value, axes, split_axis=0, concat_axis=0, tiled=True)  14.5 us
    all_to_all x2, waiting for transfers between devices, to_all(): return lax.all_to_all(value, axes, split_axis=0, concat_axis=0, tiled=True)  14.1 us
    all_to_all x1, starting transfers between devices, shards(): lax.all_to_all(slot_grad, DOM, split_axis=0, concat_axis=0, tiled=True)  8.63 us
  transfers between devices with their start and end apart: 14, of which 9 were waited for; matrix products, arithmetic and copies ran while one was open for 4% of the time, Pallas kernels for 0%

profile of v8, /device:TPU:1, one launch (start us, length us, event | category | flops | bytes accessed | tf_op | source)
XLA Modules:
  0.0 178.0 jit_solution(14653519408930483739)
XLA Ops:
  0.6 2.5 %take_rows.1 = bf16[1024,512]{1,0:T(8,128)(2,1)} custom-call(s32[8,128]{1,0:T(8,128)} %bitcast.39, s32[1,128]{1,0:T(1,128)} %bitcast.41, bf16[256,512]{1,0:T(8,128)(2,1)} %node_feats.1), custom_call_target="tpu_custom_call" | custom-call | flops 268435456 | bytes 2097152 | tf_op jit(solution)/shard_map/take_rows/pallas_call | solution.py:178
  3.2 20.6 %all-to-all-start = ((bf16[128,8,512]{2,1,0:T(8,128)(2,1)}), bf16[128,8,512]{2,1,0:T(8,128)(2,1)S(1)}, u32[]{:S(2)}, u32[]{:S(2)}) async-start(bf16[128,8,512]{2,1,0:T(8,128)(2,1)} %bitcast.33), calls=%async_computation | async-start | bytes 2097152 | tf_op jit(solution)/shard_map/all_to_all | solution.py:242
  25.2 1.6 copy.20
  30.3 47.8 %all-to-all-done = bf16[128,8,512]{2,1,0:T(8,128)(2,1)S(1)} async-done(((bf16[128,8,512]{2,1,0:T(8,128)(2,1)}), bf16[128,8,512]{2,1,0:T(8,128)(2,1)S(1)}, u32[]{:S(2)}, u32[]{:S(2)}) %all-to-all-start) | async-done | bytes 1048608 | tf_op jit(solution)/shard_map/all_to_all | solution.py:242
  78.1 2.3 %layer.1 = (bf16[256,512]{1,0:T(8,128)(2,1)}, bf16[256,512]{1,0:T(8,128)(2,1)}, bf16[256,512]{1,0:T(8,128)(2,1)}, bf16[256,512]{1,0:T(8,128)(2,1)}, bf16[1024,512]{1,0:T(8,128)(2,1)}) custom-call(bf16[1024,512]{1,0:T(8,128)(2,1)S(1)} %bitcast.32, bf16[256,1024]{1,0:T(8,128)(2,1)S(1)} %copy.21.mixing, bf16[1024,256]{1,0:T(8,128)(2,1)S(1)} %convert_bitcast_fusion.mixing_rows, ...), custom_call_target="tpu_custom_call" | custom-call | flops 805306368 | bytes 6291456 | tf_op jit(solution)/shard_map/layer/pallas_call | solution.py:106
  80.4 8.6 %all-to-all-start.1 = ((bf16[128,8,512]{2,1,0:T(8,128)(2,1)}), bf16[128,8,512]{2,1,0:T(8,128)(2,1)S(1)}, u32[]{:S(2)}, u32[]{:S(2)}) async-start(bf16[128,8,512]{2,1,0:T(8,128)(2,1)} %bitcast.35), calls=%async_computation.1 | async-start | bytes 2097152 | tf_op jit(solution)/shard_map/all_to_all | solution.py:259
  89.4 2.8 %collective-permute-start = (f32[256,512]{1,0:T(8,128)S(1)}, f32[256,512]{1,0:T(8,128)S(1)}, u32[]{:S(2)}, u32[]{:S(2)}) collective-permute-start(f32[256,512]{1,0:T(8,128)S(1)} %constant_dynamic-slice_fusion.2), channel_id=1, source_target_pairs={{0,4},{4,0},{1,5},{5,1},{2,6},{6,2},{3,7},{7,3},{8,12},{12,8},{9,1... | collective-permute-start | bytes 1572872 | tf_op jit(solution)/shard_map/ppermute | solution.py:17
  92.3 1.5 collective-permute-done
  93.9 3.1 %collective-permute-start.1 = (bf16[64,512]{1,0:T(8,128)(2,1)S(1)}, bf16[64,512]{1,0:T(8,128)(2,1)S(1)}, u32[]{:S(2)}, u32[]{:S(2)}) collective-permute-start(bf16[64,512]{1,0:T(8,128)(2,1)S(1)} %get-tuple-element.21), channel_id=1, source_target_pairs={{0,1},{1,0},{2,3},{3,2},{4,5},{5,4},{6,7},{7,6},{8,9},{9,8},{10,11... | collective-permute-start | bytes 196616 | tf_op jit(solution)/shard_map/ppermute | solution.py:17
  97.1 4.4 %collective-permute-start.2 = (bf16[64,512]{1,0:T(8,128)(2,1)S(1)}, bf16[64,512]{1,0:T(8,128)(2,1)S(1)}, u32[]{:S(2)}, u32[]{:S(2)}) collective-permute-start(bf16[64,512]{1,0:T(8,128)(2,1)S(1)} %get-tuple-element.23), channel_id=1, source_target_pairs={{0,2},{1,3},{2,0},{3,1},{4,6},{5,7},{6,4},{7,5},{8,10},{9,11},{10,... | collective-permute-start | bytes 196616 | tf_op jit(solution)/shard_map/ppermute | solution.py:17
  101.4 2.1 %collective-permute-start.3 = (bf16[64,512]{1,0:T(8,128)(2,1)S(1)}, bf16[64,512]{1,0:T(8,128)(2,1)S(1)}, u32[]{:S(2)}, u32[]{:S(2)}) collective-permute-start(bf16[64,512]{1,0:T(8,128)(2,1)S(1)} %get-tuple-element.22), channel_id=1, source_target_pairs={{0,3},{1,2},{2,1},{3,0},{4,7},{5,6},{6,5},{7,4},{8,11},{9,10},{10,... | collective-permute-start | bytes 196616 | tf_op jit(solution)/shard_map/ppermute | solution.py:17
  103.9 4.1 %collective-permute-done.3 = bf16[64,512]{1,0:T(8,128)(2,1)S(1)} collective-permute-done((bf16[64,512]{1,0:T(8,128)(2,1)S(1)}, bf16[64,512]{1,0:T(8,128)(2,1)S(1)}, u32[]{:S(2)}, u32[]{:S(2)}) %collective-permute-start.3) | collective-permute-done | bytes 65568 | tf_op jit(solution)/shard_map/ppermute | solution.py:17
  108.0 2.9 %collective-permute-start.4 = (f32[16,512]{1,0:T(8,128)S(1)}, f32[16,512]{1,0:T(8,128)S(1)}, u32[]{:S(2)}, u32[]{:S(2)}) collective-permute-start(f32[16,512]{1,0:T(8,128)S(1)} %get-tuple-element.24), channel_id=1, source_target_pairs={{0,128},{128,0},{256,384},{384,256},{1,129},{129,1},{257,385},{385... | collective-permute-start | bytes 98312 | tf_op jit(solution)/shard_map/ppermute | solution.py:17
  110.9 4.7 %collective-permute-start.5 = (f32[16,512]{1,0:T(8,128)S(1)}, f32[16,512]{1,0:T(8,128)S(1)}, u32[]{:S(2)}, u32[]{:S(2)}) collective-permute-start(f32[16,512]{1,0:T(8,128)S(1)} %get-tuple-element.26), channel_id=1, source_target_pairs={{0,256},{128,384},{256,0},{384,128},{1,257},{129,385},{257,1},{385... | collective-permute-start | bytes 98312 | tf_op jit(solution)/shard_map/ppermute | solution.py:17
  115.6 2.0 %collective-permute-start.6 = (f32[16,512]{1,0:T(8,128)S(1)}, f32[16,512]{1,0:T(8,128)S(1)}, u32[]{:S(2)}, u32[]{:S(2)}) collective-permute-start(f32[16,512]{1,0:T(8,128)S(1)} %get-tuple-element.25), channel_id=1, source_target_pairs={{0,384},{128,256},{256,128},{384,0},{1,385},{129,257},{257,129},{3... | collective-permute-start | bytes 98312 | tf_op jit(solution)/shard_map/ppermute | solution.py:17
  117.7 4.1 %collective-permute-done.6 = f32[16,512]{1,0:T(8,128)S(1)} collective-permute-done((f32[16,512]{1,0:T(8,128)S(1)}, f32[16,512]{1,0:T(8,128)S(1)}, u32[]{:S(2)}, u32[]{:S(2)}) %collective-permute-start.6) | collective-permute-done | bytes 32800 | tf_op jit(solution)/shard_map/ppermute | solution.py:17
  121.9 7.1 %collective-permute-start.7 = (bf16[16,512]{1,0:T(8,128)(2,1)S(1)}, bf16[16,512]{1,0:T(8,128)(2,1)S(1)}, u32[]{:S(2)}, u32[]{:S(2)}) collective-permute-start(bf16[16,512]{1,0:T(8,128)(2,1)S(1)} %add_convert_fusion), channel_id=1, source_target_pairs={{0,32},{32,0},{64,96},{96,64},{1,33},{33,1},{65,97},{97,65},{2,34}... | collective-permute-start | bytes 49160 | tf_op jit(solution)/shard_map/ppermute | solution.py:17
  129.0 7.1 %collective-permute-start.8 = (bf16[16,512]{1,0:T(8,128)(2,1)S(1)}, bf16[16,512]{1,0:T(8,128)(2,1)S(1)}, u32[]{:S(2)}, u32[]{:S(2)}) collective-permute-start(bf16[16,512]{1,0:T(8,128)(2,1)S(1)} %add_convert_fusion), channel_id=1, source_target_pairs={{0,64},{32,96},{64,0},{96,32},{1,65},{33,97},{65,1},{97,33},{2,66}... | collective-permute-start | bytes 49160 | tf_op jit(solution)/shard_map/ppermute | solution.py:17
  136.1 2.0 %collective-permute-start.9 = (bf16[16,512]{1,0:T(8,128)(2,1)S(1)}, bf16[16,512]{1,0:T(8,128)(2,1)S(1)}, u32[]{:S(2)}, u32[]{:S(2)}) collective-permute-start(bf16[16,512]{1,0:T(8,128)(2,1)S(1)} %add_convert_fusion), channel_id=1, source_target_pairs={{0,96},{32,64},{64,32},{96,0},{1,97},{33,65},{65,33},{97,1},{2,98}... | collective-permute-start | bytes 49160 | tf_op jit(solution)/shard_map/ppermute | solution.py:17
  138.1 7.0 %collective-permute-done.8 = bf16[16,512]{1,0:T(8,128)(2,1)S(1)} collective-permute-done((bf16[16,512]{1,0:T(8,128)(2,1)S(1)}, bf16[16,512]{1,0:T(8,128)(2,1)S(1)}, u32[]{:S(2)}, u32[]{:S(2)}) %collective-permute-start.8) | collective-permute-done | bytes 16416 | tf_op jit(solution)/shard_map/ppermute | solution.py:17
  145.8 3.3 %all-to-all-start.2 = ((bf16[4,16,512]{2,1,0:T(8,128)(2,1)}), bf16[4,16,512]{2,1,0:T(8,128)(2,1)S(1)}, u32[]{:S(2)}, u32[]{:S(2)}) async-start(bf16[4,16,512]{2,1,0:T(8,128)(2,1)} %broadcast_in_dim.34), calls=%async_computation.2 | async-start | bytes 131072 | tf_op jit(solution)/shard_map/all_to_all | solution.py:39
  149.3 4.3 %all-to-all-done.2 = bf16[4,16,512]{2,1,0:T(8,128)(2,1)S(1)} async-done(((bf16[4,16,512]{2,1,0:T(8,128)(2,1)}), bf16[4,16,512]{2,1,0:T(8,128)(2,1)S(1)}, u32[]{:S(2)}, u32[]{:S(2)}) %all-to-all-start.2) | async-done | bytes 65568 | tf_op jit(solution)/shard_map/all_to_all | solution.py:39
  154.5 11.2 %all-to-all-start.3 = ((bf16[32,16,512]{2,1,0:T(8,128)(2,1)}), bf16[32,16,512]{2,1,0:T(8,128)(2,1)S(1)}, u32[]{:S(2)}, u32[]{:S(2)}) async-start(bf16[32,16,512]{2,1,0:T(8,128)(2,1)} %broadcast_in_dim.58), calls=%async_computation.3 | async-start | bytes 1048576 | tf_op jit(solution)/shard_map/all_to_all | solution.py:39
  167.1 9.7 %all-to-all-done.3 = bf16[32,16,512]{2,1,0:T(8,128)(2,1)S(1)} async-done(((bf16[32,16,512]{2,1,0:T(8,128)(2,1)}), bf16[32,16,512]{2,1,0:T(8,128)(2,1)S(1)}, u32[]{:S(2)}, u32[]{:S(2)}) %all-to-all-start.3) | async-done | bytes 524320 | tf_op jit(solution)/shard_map/all_to_all | solution.py:39
  (66 shorter events, 10.1 us)
Async XLA Ops:
  3.2 20.6 %copy-start.10 = (s32[1024,2]{0,1:T(2,128)S(1)}, s32[1024,2]{0,1:T(2,128)}, u32[]{:S(2)}) copy-start(s32[1024,2]{0,1:T(2,128)} %param.19) | copy-start | bytes 24580
  3.2 20.6 %copy-start.11 = (s32[1024,2]{0,1:T(2,128)S(1)}, s32[1024,2]{0,1:T(2,128)}, u32[]{:S(2)}) copy-start(s32[1024,2]{0,1:T(2,128)} %param.18) | copy-start | bytes 24580
  3.2 74.9 %all-to-all-start = ((bf16[128,8,512]{2,1,0:T(8,128)(2,1)}), bf16[128,8,512]{2,1,0:T(8,128)(2,1)S(1)}, u32[]{:S(2)}, u32[]{:S(2)}) async-start(bf16[128,8,512]{2,1,0:T(8,128)(2,1)} %bitcast.33), calls=%async_computation | async-start | bytes 2097152 | tf_op jit(solution)/shard_map/all_to_all | solution.py:242
  29.9 48.2 %copy-start = (bf16[512,512]{1,0:T(8,128)(2,1)S(1)}, bf16[512,512]{1,0:T(8,128)(2,1)}, u32[]{:S(2)}) copy-start(bf16[512,512]{1,0:T(8,128)(2,1)} %weight.1) | copy-start | bytes 1572868
  29.9 48.2 %copy-start.1 = (bf16[256,512]{1,0:T(8,128)(2,1)S(1)}, bf16[256,512]{1,0:T(8,128)(2,1)}, u32[]{:S(2)}) copy-start(bf16[256,512]{1,0:T(8,128)(2,1)} %cotangent.1) | copy-start | bytes 786436
  80.4 8.7 %copy-start.8 = (bf16[256,512]{1,0:T(8,128)(2,1)S(1)}, bf16[256,512]{1,0:T(8,128)(2,1)}, u32[]{:S(2)}) copy-start(bf16[256,512]{1,0:T(8,128)(2,1)} %get-tuple-element.17) | copy-start | bytes 786436
  80.4 8.7 %copy-start.9 = (bf16[256,512]{1,0:T(8,128)(2,1)S(1)}, bf16[256,512]{1,0:T(8,128)(2,1)}, u32[]{:S(2)}) copy-start(bf16[256,512]{1,0:T(8,128)(2,1)} %get-tuple-element.18) | copy-start | bytes 786436
  80.4 64.7 %all-to-all-start.1 = ((bf16[128,8,512]{2,1,0:T(8,128)(2,1)}), bf16[128,8,512]{2,1,0:T(8,128)(2,1)S(1)}, u32[]{:S(2)}, u32[]{:S(2)}) async-start(bf16[128,8,512]{2,1,0:T(8,128)(2,1)} %bitcast.35), calls=%async_computation.1 | async-start | bytes 2097152 | tf_op jit(solution)/shard_map/all_to_all | solution.py:259
  89.4 4.3 %collective-permute-start = (f32[256,512]{1,0:T(8,128)S(1)}, f32[256,512]{1,0:T(8,128)S(1)}, u32[]{:S(2)}, u32[]{:S(2)}) collective-permute-start(f32[256,512]{1,0:T(8,128)S(1)} %constant_dynamic-slice_fusion.2), channel_id=1, source_target_pairs={{0,4},{4,0},{1,5},{5,1},{2,6},{6,2},{3,7},{7,3},{8,12},{12,8},{9,1... | collective-permute-start | bytes 1572872 | tf_op jit(solution)/shard_map/ppermute | solution.py:17
  93.9 55.2 %copy-start.12 = (s32[128,8]{0,1:T(8,128)S(1)}, s32[128,8]{0,1:T(8,128)}, u32[]{:S(2)}) copy-start(s32[128,8]{0,1:T(8,128)} %param.16) | copy-start | bytes 12292
  93.9 55.2 %copy-start.14 = (s32[128]{0:T(128)S(1)}, s32[128]{0:T(128)}, u32[]{:S(2)}) copy-start(s32[128]{0:T(128)} %param.17) | copy-start | bytes 1540
  93.9 9.6 %collective-permute-start.1 = (bf16[64,512]{1,0:T(8,128)(2,1)S(1)}, bf16[64,512]{1,0:T(8,128)(2,1)S(1)}, u32[]{:S(2)}, u32[]{:S(2)}) collective-permute-start(bf16[64,512]{1,0:T(8,128)(2,1)S(1)} %get-tuple-element.21), channel_id=1, source_target_pairs={{0,1},{1,0},{2,3},{3,2},{4,5},{5,4},{6,7},{7,6},{8,9},{9,8},{10,11... | collective-permute-start | bytes 196616 | tf_op jit(solution)/shard_map/ppermute | solution.py:17
  97.1 6.8 %collective-permute-start.2 = (bf16[64,512]{1,0:T(8,128)(2,1)S(1)}, bf16[64,512]{1,0:T(8,128)(2,1)S(1)}, u32[]{:S(2)}, u32[]{:S(2)}) collective-permute-start(bf16[64,512]{1,0:T(8,128)(2,1)S(1)} %get-tuple-element.23), channel_id=1, source_target_pairs={{0,2},{1,3},{2,0},{3,1},{4,6},{5,7},{6,4},{7,5},{8,10},{9,11},{10,... | collective-permute-start | bytes 196616 | tf_op jit(solution)/shard_map/ppermute | solution.py:17
  101.4 6.5 %collective-permute-start.3 = (bf16[64,512]{1,0:T(8,128)(2,1)S(1)}, bf16[64,512]{1,0:T(8,128)(2,1)S(1)}, u32[]{:S(2)}, u32[]{:S(2)}) collective-permute-start(bf16[64,512]{1,0:T(8,128)(2,1)S(1)} %get-tuple-element.22), channel_id=1, source_target_pairs={{0,3},{1,2},{2,1},{3,0},{4,7},{5,6},{6,5},{7,4},{8,11},{9,10},{10,... | collective-permute-start | bytes 196616 | tf_op jit(solution)/shard_map/ppermute | solution.py:17
  108.0 9.6 %collective-permute-start.4 = (f32[16,512]{1,0:T(8,128)S(1)}, f32[16,512]{1,0:T(8,128)S(1)}, u32[]{:S(2)}, u32[]{:S(2)}) collective-permute-start(f32[16,512]{1,0:T(8,128)S(1)} %get-tuple-element.24), channel_id=1, source_target_pairs={{0,128},{128,0},{256,384},{384,256},{1,129},{129,1},{257,385},{385... | collective-permute-start | bytes 98312 | tf_op jit(solution)/shard_map/ppermute | solution.py:17
  110.9 6.8 %collective-permute-start.5 = (f32[16,512]{1,0:T(8,128)S(1)}, f32[16,512]{1,0:T(8,128)S(1)}, u32[]{:S(2)}, u32[]{:S(2)}) collective-permute-start(f32[16,512]{1,0:T(8,128)S(1)} %get-tuple-element.26), channel_id=1, source_target_pairs={{0,256},{128,384},{256,0},{384,128},{1,257},{129,385},{257,1},{385... | collective-permute-start | bytes 98312 | tf_op jit(solution)/shard_map/ppermute | solution.py:17
  115.6 6.2 %collective-permute-start.6 = (f32[16,512]{1,0:T(8,128)S(1)}, f32[16,512]{1,0:T(8,128)S(1)}, u32[]{:S(2)}, u32[]{:S(2)}) collective-permute-start(f32[16,512]{1,0:T(8,128)S(1)} %get-tuple-element.25), channel_id=1, source_target_pairs={{0,384},{128,256},{256,128},{384,0},{1,385},{129,257},{257,129},{3... | collective-permute-start | bytes 98312 | tf_op jit(solution)/shard_map/ppermute | solution.py:17
  121.9 16.2 %collective-permute-start.7 = (bf16[16,512]{1,0:T(8,128)(2,1)S(1)}, bf16[16,512]{1,0:T(8,128)(2,1)S(1)}, u32[]{:S(2)}, u32[]{:S(2)}) collective-permute-start(bf16[16,512]{1,0:T(8,128)(2,1)S(1)} %add_convert_fusion), channel_id=1, source_target_pairs={{0,32},{32,0},{64,96},{96,64},{1,33},{33,1},{65,97},{97,65},{2,34}... | collective-permute-start | bytes 49160 | tf_op jit(solution)/shard_map/ppermute | solution.py:17
  129.0 16.1 %collective-permute-start.8 = (bf16[16,512]{1,0:T(8,128)(2,1)S(1)}, bf16[16,512]{1,0:T(8,128)(2,1)S(1)}, u32[]{:S(2)}, u32[]{:S(2)}) collective-permute-start(bf16[16,512]{1,0:T(8,128)(2,1)S(1)} %add_convert_fusion), channel_id=1, source_target_pairs={{0,64},{32,96},{64,0},{96,32},{1,65},{33,97},{65,1},{97,33},{2,66}... | collective-permute-start | bytes 49160 | tf_op jit(solution)/shard_map/ppermute | solution.py:17
  136.1 9.0 %collective-permute-start.9 = (bf16[16,512]{1,0:T(8,128)(2,1)S(1)}, bf16[16,512]{1,0:T(8,128)(2,1)S(1)}, u32[]{:S(2)}, u32[]{:S(2)}) collective-permute-start(bf16[16,512]{1,0:T(8,128)(2,1)S(1)} %add_convert_fusion), channel_id=1, source_target_pairs={{0,96},{32,64},{64,32},{96,0},{1,97},{33,65},{65,33},{97,1},{2,98}... | collective-permute-start | bytes 49160 | tf_op jit(solution)/shard_map/ppermute | solution.py:17
  145.1 20.6 %copy-start.6 = (bf16[2,2,128,128]{3,1,2,0:T(2,128)(2,1)S(1)}, bf16[2,2,128,128]{3,1,2,0:T(2,128)(2,1)}, u32[]{:S(2)}) copy-start(bf16[2,2,128,128]{3,1,2,0:T(2,128)(2,1)} %copy-done.5) | copy-start | bytes 393220
  145.1 20.6 %copy-start.7 = (bf16[256,512]{1,0:T(8,128)(2,1)S(1)}, bf16[256,512]{1,0:T(8,128)(2,1)}, u32[]{:S(2)}) copy-start(bf16[256,512]{1,0:T(8,128)(2,1)} %get-tuple-element.13) | copy-start | bytes 786436
  145.8 7.9 %all-to-all-start.2 = ((bf16[4,16,512]{2,1,0:T(8,128)(2,1)}), bf16[4,16,512]{2,1,0:T(8,128)(2,1)S(1)}, u32[]{:S(2)}, u32[]{:S(2)}) async-start(bf16[4,16,512]{2,1,0:T(8,128)(2,1)} %broadcast_in_dim.34), calls=%async_computation.2 | async-start | bytes 131072 | tf_op jit(solution)/shard_map/all_to_all | solution.py:39
  154.5 22.4 %all-to-all-start.3 = ((bf16[32,16,512]{2,1,0:T(8,128)(2,1)}), bf16[32,16,512]{2,1,0:T(8,128)(2,1)S(1)}, u32[]{:S(2)}, u32[]{:S(2)}) async-start(bf16[32,16,512]{2,1,0:T(8,128)(2,1)} %broadcast_in_dim.58), calls=%async_computation.3 | async-start | bytes 1048576 | tf_op jit(solution)/shard_map/all_to_all | solution.py:39
  (6 other events, 9.9 us)
